TPU v7x, 32 devices: a whole 2x2x4 slice. The times are simulated.
32 devices in a mesh: dp: 8 (over z, x), seq: 4 (over y, core).
Axes of the slice: x: 2, y: 2, z: 4, core: 2. Of those that a mesh axis runs over, the one named last changes fastest.
Arguments:
- tokens: bfloat16 [16, 1024, 1536], P('dp', 'seq'), may hold values from -6 to 6
- cotangent: bfloat16 [16, 1024, 1536], P('dp', 'seq'), may hold values from -6 to 6
- attn_norm: bfloat16 [2, 1536], P(None, 'dp'), may hold values from 0.5 to 1.5
- w_query: bfloat16 [2, 1536, 1536], P(None, 'dp'), may hold values from -0.15625 to 0.15625
- w_key: bfloat16 [2, 1536, 768], P(None, 'dp'), may hold values from -0.15625 to 0.15625
- w_value: bfloat16 [2, 1536, 768], P(None, 'dp'), may hold values from -0.15625 to 0.15625
- w_out: bfloat16 [2, 1536, 1536], P(None, 'dp'), may hold values from -0.875 to 0.875
- mlp_norm: bfloat16 [2, 1536], P(None, 'dp'), may hold values from 0.5 to 1.5
- w_gate: bfloat16 [2, 1536, 4096], P(None, 'dp'), may hold values from -0.15625 to 0.15625
- w_up: bfloat16 [2, 1536, 4096], P(None, 'dp'), may hold values from -0.15625 to 0.15625
- w_down: bfloat16 [2, 4096, 1536], P(None, 'dp'), may hold values from -0.125 to 0.125
Outputs:
- out: bfloat16 [16, 1024, 1536], P('dp', 'seq')
- d_tokens: float32 [16, 1024, 1536], P('dp', 'seq')
- grad_attn_norm: float32 [2, 1536], P(None, 'dp')
- grad_w_query: float32 [2, 1536, 1536], P(None, 'dp')
- grad_w_key: float32 [2, 1536, 768], P(None, 'dp')
- grad_w_value: float32 [2, 1536, 768], P(None, 'dp')
- grad_w_out: float32 [2, 1536, 1536], P(None, 'dp')
- grad_mlp_norm: float32 [2, 1536], P(None, 'dp')
- grad_w_gate: float32 [2, 1536, 4096], P(None, 'dp')
- grad_w_up: float32 [2, 1536, 4096], P(None, 'dp')
- grad_w_down: float32 [2, 4096, 1536], P(None, 'dp')
All inputs are finite; a program needn't handle non-finite values.
Results may differ from a plain program's by a relative error of at most 0.029.
Values may be sent and summed in bfloat16 or wider, within the bound.
No kernel may reach another device: no remote copies, remote signals or barrier semaphores. Data moves between devices by JAX's collectives and lax.ppermute only.
A program may use at most 448 MiB of HBM per device.

v0:
```python
import jax
import jax.numpy as jnp
from jax import lax
from jax.sharding import PartitionSpec as P

QH = 16
KVH = 8
HD = 96


epsilon = 1e-05
rope_base = 100000.0


def rotate(values, cosine, sine):
    middle = values.shape[-1] // 2
    first = values[..., :middle]
    second = values[..., middle:]
    cos_b = cosine[:, None, :]
    sin_b = sine[:, None, :]
    return jnp.concatenate(
        [first * cos_b - second * sin_b, second * cos_b + first * sin_b], axis=-1
    )


def norm_rows(stream, gain):
    inverse = lax.rsqrt(jnp.mean(stream * stream, axis=-1, keepdims=True) + epsilon)
    normed = stream * inverse
    return (normed, inverse, (normed * gain.astype(jnp.float32)).astype(jnp.bfloat16))


def norm_back(grad_out, normed, inverse, gain):
    gain_grad = jnp.sum(grad_out * normed, axis=0)
    scaled = grad_out * gain.astype(jnp.float32)
    grad_in = inverse * (scaled - normed * jnp.mean(scaled * normed, axis=-1, keepdims=True))
    return (grad_in, gain_grad)


def inner_rows(left, right):
    return lax.dot_general(
        left, right, (((0,), (0,)), ((), ())), preferred_element_type=jnp.float32
    )


def against(left, right):
    return lax.dot_general(
        left, right, (((1,), (1,)), ((), ())), preferred_element_type=jnp.float32
    )


def scores_of(queries, keys):
    raw = jnp.einsum("qgah,kgh->gaqk", queries, keys, preferred_element_type=jnp.float32) * HD ** (
        -0.5
    )
    length = queries.shape[0]
    causal = jnp.arange(length)[:, None] >= jnp.arange(length)[None, :]
    return jnp.where(causal, raw, -1e30)


def attend_forward(pieces):
    queries, keys, values = pieces
    scores = scores_of(queries, keys)
    maxima = jnp.max(scores, axis=-1, keepdims=True)
    exponent_vals = jnp.exp(scores - maxima)
    totals = jnp.sum(exponent_vals, axis=-1, keepdims=True)
    softened = (exponent_vals / totals).astype(jnp.bfloat16)
    mixed = jnp.einsum("gaqk,kgh->qgah", softened, values, preferred_element_type=jnp.float32)
    return (
        mixed.astype(jnp.bfloat16).reshape(mixed.shape[0], -1),
        (maxima + jnp.log(totals))[..., 0],
    )


def attend_backward(pieces):
    queries, keys, values, log_total, grad_out = pieces
    scores = scores_of(queries, keys)
    softened = jnp.exp(scores - log_total[..., None])
    soft_low = softened.astype(jnp.bfloat16)
    grad_values = jnp.einsum(
        "gaqk,qgah->kgh", soft_low, grad_out, preferred_element_type=jnp.float32
    )
    grad_soft = jnp.einsum("qgah,kgh->gaqk", grad_out, values, preferred_element_type=jnp.float32)
    grad_scores = softened * (grad_soft - jnp.sum(softened * grad_soft, axis=-1, keepdims=True))
    scores_low = grad_scores.astype(jnp.bfloat16)
    grad_queries = jnp.einsum(
        "gaqk,kgh->qgah", scores_low, keys, preferred_element_type=jnp.float32
    ) * HD ** (-0.5)
    grad_keys = jnp.einsum(
        "gaqk,qgah->kgh", scores_low, queries, preferred_element_type=jnp.float32
    ) * HD ** (-0.5)
    length = queries.shape[0]
    pair = jnp.concatenate(
        [
            grad_keys.astype(jnp.bfloat16).reshape(length, -1),
            grad_values.astype(jnp.bfloat16).reshape(length, -1),
        ],
        axis=-1,
    )
    return (grad_queries.astype(jnp.bfloat16).reshape(length, -1), pair)


def layer_forward(stream, weights, cosine, sine, seq_dev, span_rows):
    (
        gain_one,
        query_weight,
        key_weight,
        value_weight,
        out_weight,
        gain_two,
        gate_weight,
        up_weight,
        down_weight,
    ) = weights
    groups = lax.axis_size("seq")
    kv_local = KVH // groups
    normed_one, inverse_one, input_one = norm_rows(stream, gain_one)
    query_raw = jnp.dot(input_one, query_weight, preferred_element_type=jnp.float32)
    key_raw = jnp.dot(input_one, key_weight, preferred_element_type=jnp.float32)
    value_raw = jnp.dot(input_one, value_weight, preferred_element_type=jnp.float32)
    query_rot = rotate(query_raw.reshape(seq_dev, span_rows, QH, HD), cosine, sine).astype(
        jnp.bfloat16
    )
    key_rot = rotate(key_raw.reshape(seq_dev, span_rows, KVH, HD), cosine, sine).astype(
        jnp.bfloat16
    )
    value_low = value_raw.astype(jnp.bfloat16)
    query_send = query_rot.reshape(seq_dev, span_rows, groups, -1)
    pair_send = jnp.concatenate(
        [
            key_rot.reshape(seq_dev, span_rows, groups, -1),
            value_low.reshape(seq_dev, span_rows, groups, -1),
        ],
        axis=-1,
    )
    query_heads, pair_heads = (
        lax.all_to_all(query_send, "seq", split_axis=2, concat_axis=1, tiled=True),
        lax.all_to_all(pair_send, "seq", split_axis=2, concat_axis=1, tiled=True),
    )
    length = query_heads.shape[1]
    queries = query_heads.reshape(seq_dev, length, kv_local, 2, HD)
    pairs = pair_heads.reshape(seq_dev, length, 2, kv_local, HD)
    keys = pairs[:, :, 0]
    values = pairs[:, :, 1]
    attended, log_total = lax.map(attend_forward, (queries, keys, values))
    returned = lax.all_to_all(
        attended.reshape(seq_dev, length, 1, -1), "seq", split_axis=1, concat_axis=2, tiled=True
    )
    mixed = returned.reshape(seq_dev * span_rows, -1)
    stream_two = stream + jnp.dot(mixed, out_weight, preferred_element_type=jnp.float32)
    normed_two, inverse_two, input_two = norm_rows(stream_two, gain_two)
    gate = jnp.dot(input_two, gate_weight, preferred_element_type=jnp.float32)
    up_part = jnp.dot(input_two, up_weight, preferred_element_type=jnp.float32)
    hidden = (jax.nn.silu(gate) * up_part).astype(jnp.bfloat16)
    result = stream_two + jnp.dot(hidden, down_weight, preferred_element_type=jnp.float32)
    saved = (
        normed_one,
        inverse_one,
        input_one,
        queries,
        keys,
        values,
        log_total,
        mixed,
        normed_two,
        inverse_two,
        input_two,
        gate,
        up_part,
        hidden,
    )
    return (result, saved)


def layer_backward(grad, saved, weights, cosine, sine, seq_dev, span_rows):
    (
        normed_one,
        inverse_one,
        input_one,
        queries,
        keys,
        values,
        log_total,
        mixed,
        normed_two,
        inverse_two,
        input_two,
        gate,
        up_part,
        hidden,
    ) = saved
    (
        gain_one,
        query_weight,
        key_weight,
        value_weight,
        out_weight,
        gain_two,
        gate_weight,
        up_weight,
        down_weight,
    ) = weights
    groups = lax.axis_size("seq")
    rows = seq_dev * span_rows
    length = queries.shape[1]
    kv_local = KVH // groups
    grad_low = grad.astype(jnp.bfloat16)
    grad_down = inner_rows(hidden, grad_low)
    grad_hidden = against(grad_low, down_weight)
    sigmoid_gate = jax.nn.sigmoid(gate)
    grad_gate = (grad_hidden * up_part * sigmoid_gate * (1.0 + gate * (1.0 - sigmoid_gate))).astype(
        jnp.bfloat16
    )
    grad_up = (grad_hidden * gate * sigmoid_gate).astype(jnp.bfloat16)
    grad_gate_w = inner_rows(input_two, grad_gate)
    grad_up_w = inner_rows(input_two, grad_up)
    grad_two = against(grad_gate, gate_weight) + against(grad_up, up_weight)
    norm_two_in, grad_gain_two = norm_back(grad_two, normed_two, inverse_two, gain_two)
    grad_mid = grad + norm_two_in
    mid_low = grad_mid.astype(jnp.bfloat16)
    grad_out_w = inner_rows(mixed, mid_low)
    grad_mixed = against(mid_low, out_weight).astype(jnp.bfloat16)
    grad_heads = lax.all_to_all(
        grad_mixed.reshape(seq_dev, span_rows, groups, -1),
        "seq",
        split_axis=2,
        concat_axis=1,
        tiled=True,
    )
    grad_heads = grad_heads.reshape(seq_dev, length, kv_local, 2, HD)
    grad_queries, grad_pairs = lax.map(
        attend_backward, (queries, keys, values, log_total, grad_heads)
    )
    back_query, back_pair = (
        lax.all_to_all(
            grad_queries.reshape(seq_dev, length, 1, -1),
            "seq",
            split_axis=1,
            concat_axis=2,
            tiled=True,
        ),
        lax.all_to_all(
            grad_pairs.reshape(seq_dev, length, 1, -1),
            "seq",
            split_axis=1,
            concat_axis=2,
            tiled=True,
        ),
    )
    back_pair = back_pair.reshape(seq_dev, span_rows, groups, 2, kv_local, HD)
    grad_key_rot = back_pair[:, :, :, 0].reshape(seq_dev, span_rows, KVH, HD)
    grad_value_raw = back_pair[:, :, :, 1].reshape(rows, KVH * HD)
    grad_query_raw = (
        rotate(back_query.reshape(seq_dev, span_rows, QH, HD).astype(jnp.float32), cosine, -sine)
        .astype(jnp.bfloat16)
        .reshape(rows, QH * HD)
    )
    grad_key_raw = (
        rotate(grad_key_rot.astype(jnp.float32), cosine, -sine)
        .astype(jnp.bfloat16)
        .reshape(rows, KVH * HD)
    )
    grad_query_w = inner_rows(input_one, grad_query_raw)
    grad_key_w = inner_rows(input_one, grad_key_raw)
    grad_value_w = inner_rows(input_one, grad_value_raw)
    grad_one = (
        against(grad_query_raw, query_weight)
        + against(grad_key_raw, key_weight)
        + against(grad_value_raw, value_weight)
    )
    norm_one_in, grad_gain_one = norm_back(grad_one, normed_one, inverse_one, gain_one)
    grads = (
        grad_gain_one,
        grad_query_w,
        grad_key_w,
        grad_value_w,
        grad_out_w,
        grad_gain_two,
        grad_gate_w,
        grad_up_w,
        grad_down,
    )
    return (grad_mid + norm_one_in, grads)


def body(
    tokens, cotangent, attn_norm, w_query, w_key, w_value, w_out, mlp_norm, w_gate, w_up, w_down
):
    seq_dev, span_rows, features = tokens.shape
    layer_total = w_query.shape[0]
    middle = HD // 2
    positions = (lax.axis_index("seq") * span_rows + jnp.arange(span_rows)).astype(jnp.float32)
    frequency = rope_base ** (-jnp.arange(middle, dtype=jnp.float32) / middle)
    angles = positions[:, None] * frequency[None, :]
    cosine = jnp.cos(angles)
    sine = jnp.sin(angles)
    stream = tokens.astype(jnp.float32).reshape(seq_dev * span_rows, features)
    kept = []
    saved_all = []
    for layer_idx in range(layer_total):
        weights = (
            lax.all_gather(attn_norm[layer_idx], "dp", axis=0, tiled=True),
            lax.all_gather(w_query[layer_idx], "dp", axis=0, tiled=True),
            lax.all_gather(w_key[layer_idx], "dp", axis=0, tiled=True),
            lax.all_gather(w_value[layer_idx], "dp", axis=0, tiled=True),
            lax.all_gather(w_out[layer_idx], "dp", axis=0, tiled=True),
            lax.all_gather(mlp_norm[layer_idx], "dp", axis=0, tiled=True),
            lax.all_gather(w_gate[layer_idx], "dp", axis=0, tiled=True),
            lax.all_gather(w_up[layer_idx], "dp", axis=0, tiled=True),
            lax.all_gather(w_down[layer_idx], "dp", axis=0, tiled=True),
        )
        stream, saved = layer_forward(stream, weights, cosine, sine, seq_dev, span_rows)
        kept.append(weights)
        saved_all.append(saved)
    output = stream.astype(jnp.bfloat16).reshape(seq_dev, span_rows, features)
    grad = cotangent.astype(jnp.float32).reshape(seq_dev * span_rows, features)
    layer_grads = [None] * layer_total
    for layer_idx in reversed(range(layer_total)):
        weights = (
            lax.all_gather(attn_norm[layer_idx], "dp", axis=0, tiled=True),
            lax.all_gather(w_query[layer_idx], "dp", axis=0, tiled=True),
            lax.all_gather(w_key[layer_idx], "dp", axis=0, tiled=True),
            lax.all_gather(w_value[layer_idx], "dp", axis=0, tiled=True),
            lax.all_gather(w_out[layer_idx], "dp", axis=0, tiled=True),
            lax.all_gather(mlp_norm[layer_idx], "dp", axis=0, tiled=True),
            lax.all_gather(w_gate[layer_idx], "dp", axis=0, tiled=True),
            lax.all_gather(w_up[layer_idx], "dp", axis=0, tiled=True),
            lax.all_gather(w_down[layer_idx], "dp", axis=0, tiled=True),
        )
        grad, grads = layer_backward(
            grad, saved_all[layer_idx], weights, cosine, sine, seq_dev, span_rows
        )
        gain_one_g, query_g, key_g, value_g, out_g, gain_two_g, gate_g, up_g, down_g = grads
        summed = (
            lax.psum_scatter(
                gain_one_g.astype(jnp.bfloat16), "dp", scatter_dimension=0, tiled=True
            ).astype(jnp.float32),
            lax.psum_scatter(
                query_g.astype(jnp.bfloat16), "dp", scatter_dimension=0, tiled=True
            ).astype(jnp.float32),
            lax.psum_scatter(
                key_g.astype(jnp.bfloat16), "dp", scatter_dimension=0, tiled=True
            ).astype(jnp.float32),
            lax.psum_scatter(
                value_g.astype(jnp.bfloat16), "dp", scatter_dimension=0, tiled=True
            ).astype(jnp.float32),
            lax.psum_scatter(
                out_g.astype(jnp.bfloat16), "dp", scatter_dimension=0, tiled=True
            ).astype(jnp.float32),
            lax.psum_scatter(
                gain_two_g.astype(jnp.bfloat16), "dp", scatter_dimension=0, tiled=True
            ).astype(jnp.float32),
            lax.psum_scatter(
                gate_g.astype(jnp.bfloat16), "dp", scatter_dimension=0, tiled=True
            ).astype(jnp.float32),
            lax.psum_scatter(
                up_g.astype(jnp.bfloat16), "dp", scatter_dimension=0, tiled=True
            ).astype(jnp.float32),
            lax.psum_scatter(
                down_g.astype(jnp.bfloat16), "dp", scatter_dimension=0, tiled=True
            ).astype(jnp.float32),
        )
        (
            part_one,
            part_two,
            part_three,
            part_four,
            part_five,
            part_six,
            part_seven,
            part_eight,
            part_nine,
        ) = summed
        summed = (
            lax.psum(part_one.astype(jnp.bfloat16), "seq").astype(jnp.float32),
            lax.psum(part_two.astype(jnp.bfloat16), "seq").astype(jnp.float32),
            lax.psum(part_three.astype(jnp.bfloat16), "seq").astype(jnp.float32),
            lax.psum(part_four.astype(jnp.bfloat16), "seq").astype(jnp.float32),
            lax.psum(part_five.astype(jnp.bfloat16), "seq").astype(jnp.float32),
            lax.psum(part_six.astype(jnp.bfloat16), "seq").astype(jnp.float32),
            lax.psum(part_seven.astype(jnp.bfloat16), "seq").astype(jnp.float32),
            lax.psum(part_eight.astype(jnp.bfloat16), "seq").astype(jnp.float32),
            lax.psum(part_nine.astype(jnp.bfloat16), "seq").astype(jnp.float32),
        )
        layer_grads[layer_idx] = summed
    stacked = [
        jnp.stack([layer_grads[layer_idx][member] for layer_idx in range(layer_total)])
        for member in range(9)
    ]
    d_tokens = grad.reshape(seq_dev, span_rows, features)
    return (
        output,
        d_tokens,
        stacked[0],
        stacked[1],
        stacked[2],
        stacked[3],
        stacked[4],
        stacked[5],
        stacked[6],
        stacked[7],
        stacked[8],
    )


def solution(mesh):
    in_specs = (
        P("dp", "seq", None),
        P("dp", "seq", None),
        P(None, "dp"),
        P(None, "dp", None),
        P(None, "dp", None),
        P(None, "dp", None),
        P(None, "dp", None),
        P(None, "dp"),
        P(None, "dp", None),
        P(None, "dp", None),
        P(None, "dp", None),
    )
    out_specs = (
        P("dp", "seq", None),
        P("dp", "seq", None),
        P(None, "dp"),
        P(None, "dp", None),
        P(None, "dp", None),
        P(None, "dp", None),
        P(None, "dp", None),
        P(None, "dp"),
        P(None, "dp", None),
        P(None, "dp", None),
        P(None, "dp", None),
    )
    return jax.shard_map(body, mesh=mesh, in_specs=in_specs, out_specs=out_specs, check_vma=False)
```

profile of v0, /device:TPU:0, one launch (start us, length us, event | category | flops | bytes accessed | tf_op | source)
XLA Modules:
  0.0 4117.9 jit_solution(17302845049543519249)
XLA Ops:
  30.8 40.0 all-reduce.9
  132.0 68.7 %all-gather.37.cloned.1.call-done = bf16[1,1536,1536]{2,1,0:T(8,128)(2,1)} async-done(((bf16[1,192,1536]{2,1,0:T(8,128)(2,1)}), bf16[1,1536,1536]{2,1,0:T(8,128)(2,1)}) %all-gather.37.cloned.1.call-update) | async-done | bytes 4718608 | tf_op jit(solution)/shard_map/all_gather | solution.py:302
  313.9 144.1 %all-gather.41.cloned.1.call-done = bf16[1,1536,4096]{2,1,0:T(8,128)(2,1)} async-done(((bf16[1,192,4096]{2,1,0:T(8,128)(2,1)}), bf16[1,1536,4096]{2,1,0:T(8,128)(2,1)}) %all-gather.41.cloned.1.call-update) | async-done | bytes 12582928 | tf_op jit(solution)/shard_map/all_gather | solution.py:307
  469.7 165.0 %all-gather.43.cloned.1.call-done = bf16[1,1536,4096]{2,1,0:T(8,128)(2,1)} async-done(((bf16[1,192,4096]{2,1,0:T(8,128)(2,1)}), bf16[1,1536,4096]{2,1,0:T(8,128)(2,1)}) %all-gather.43.cloned.1.call-update) | async-done | bytes 12582928 | tf_op jit(solution)/shard_map/all_gather | solution.py:308
  649.2 162.3 %all-gather.45.cloned.1.call-done = bf16[1,4096,1536]{2,1,0:T(8,128)(2,1)} async-done(((bf16[1,512,1536]{2,1,0:T(8,128)(2,1)}), bf16[1,4096,1536]{2,1,0:T(8,128)(2,1)}) %all-gather.45.cloned.1.call-update) | async-done | bytes 12582928 | tf_op jit(solution)/shard_map/all_gather | solution.py:309
  824.3 68.1 %all-gather.51.cloned.1.call-done = bf16[1,1536,1536]{2,1,0:T(8,128)(2,1)} async-done(((bf16[1,192,1536]{2,1,0:T(8,128)(2,1)}), bf16[1,1536,1536]{2,1,0:T(8,128)(2,1)}) %all-gather.51.cloned.1.call-update) | async-done | bytes 4718608 | tf_op jit(solution)/shard_map/all_gather | solution.py:302
  953.1 44.5 %all-gather.49.cloned.1.call-done = bf16[1,1536,768]{2,1,0:T(8,128)(2,1)} async-done(((bf16[1,192,768]{2,1,0:T(8,128)(2,1)}), bf16[1,1536,768]{2,1,0:T(8,128)(2,1)}) %all-gather.49.cloned.1.call-update) | async-done | bytes 2359312 | tf_op jit(solution)/shard_map/all_gather | solution.py:304
  1079.5 95.3 %all-gather.59.cloned.1.call-done = bf16[1,4096,1536]{2,1,0:T(8,128)(2,1)} async-done(((bf16[1,512,1536]{2,1,0:T(8,128)(2,1)}), bf16[1,4096,1536]{2,1,0:T(8,128)(2,1)}) %all-gather.59.cloned.1.call-update) | async-done | bytes 12582928 | tf_op jit(solution)/shard_map/all_gather | solution.py:309
  1191.1 63.9 %all-gather.53.cloned.1.call-done = bf16[1,1536,1536]{2,1,0:T(8,128)(2,1)} async-done(((bf16[1,192,1536]{2,1,0:T(8,128)(2,1)}), bf16[1,1536,1536]{2,1,0:T(8,128)(2,1)}) %all-gather.53.cloned.1.call-update) | async-done | bytes 4718608 | tf_op jit(solution)/shard_map/all_gather | solution.py:305
  1264.5 167.8 %all-gather.57.cloned.1.call-done = bf16[1,1536,4096]{2,1,0:T(8,128)(2,1)} async-done(((bf16[1,192,4096]{2,1,0:T(8,128)(2,1)}), bf16[1,1536,4096]{2,1,0:T(8,128)(2,1)}) %all-gather.57.cloned.1.call-update) | async-done | bytes 12582928 | tf_op jit(solution)/shard_map/all_gather | solution.py:308
  1444.4 165.2 %all-gather.55.cloned.1.call-done = bf16[1,1536,4096]{2,1,0:T(8,128)(2,1)} async-done(((bf16[1,192,4096]{2,1,0:T(8,128)(2,1)}), bf16[1,1536,4096]{2,1,0:T(8,128)(2,1)}) %all-gather.55.cloned.1.call-update) | async-done | bytes 12582928 | tf_op jit(solution)/shard_map/all_gather | solution.py:307
  1702.3 85.9 %while.50 = (s32[]{:T(128)}, bf16[2,1024,384]{1,2,0:T(8,128)(2,1)}, bf16[2,1024,384]{1,2,0:T(8,128)(2,1)}, bf16[2,1024,2,96]{1,3,2,0:T(8,128)(2,1)S(1)}, bf16[2,...) while((s32[]{:T(128)}, bf16[2,1024,384]{1,2,0:T(8,128)(2,1)}, ...), condition=%wide.region_15.16_spmd, body=%wide.region_13.15_spmd.sunk | while | flops 4093440000 | bytes 256953328 | solution.py:230
  1950.7 82.2 %while.51 = (s32[]{:T(128)}, bf16[2,1024,384]{1,2,0:T(8,128)(2,1)}, bf16[2,1024,384]{1,2,0:T(8,128)(2,1)}, bf16[2,1024,2,96]{1,3,2,0:T(8,128)(2,1)}, bf16[2,1024...) while((s32[]{:T(128)}, bf16[2,1024,384]{1,2,0:T(8,128)(2,1)}, ...), condition=%wide.region_20.21_spmd, body=%wide.region_18.20_spmd.sunk | while | flops 4093440000 | bytes 247253360 | solution.py:230
  2210.5 93.1 %reduce-scatter.29.cloned.1.call-done = bf16[192,1536]{1,0:T(8,128)(2,1)} async-done(((bf16[1536,1536]{1,0:T(8,128)(2,1)}), bf16[192,1536]{1,0:T(8,128)(2,1)}) %reduce-scatter.29.cloned.1.call-update) | async-done | bytes 589840 | tf_op jit(solution)/shard_map/reduce_scatter | solution.py:346
  2303.5 98.5 %reduce-scatter.27.cloned.1.call-done = bf16[192,1536]{1,0:T(8,128)(2,1)} async-done(((bf16[1536,1536]{1,0:T(8,128)(2,1)}), bf16[192,1536]{1,0:T(8,128)(2,1)}) %reduce-scatter.27.cloned.1.call-update) | async-done | bytes 589840 | tf_op jit(solution)/shard_map/reduce_scatter | solution.py:346
  2402.1 99.3 %reduce-scatter.17.cloned.1.call-done = bf16[192,1536]{1,0:T(8,128)(2,1)} async-done(((bf16[1536,1536]{1,0:T(8,128)(2,1)}), bf16[192,1536]{1,0:T(8,128)(2,1)}) %reduce-scatter.17.cloned.1.call-update) | async-done | bytes 589840 | tf_op jit(solution)/shard_map/reduce_scatter | solution.py:337
  2501.3 99.4 %reduce-scatter.15.cloned.1.call-done = bf16[192,1536]{1,0:T(8,128)(2,1)} async-done(((bf16[1536,1536]{1,0:T(8,128)(2,1)}), bf16[192,1536]{1,0:T(8,128)(2,1)}) %reduce-scatter.15.cloned.1.call-update) | async-done | bytes 589840 | tf_op jit(solution)/shard_map/reduce_scatter | solution.py:337
  2600.8 210.6 %reduce-scatter.33.cloned.1.call-done = bf16[192,4096]{1,0:T(8,128)(2,1)} async-done(((bf16[1536,4096]{1,0:T(8,128)(2,1)}), bf16[192,4096]{1,0:T(8,128)(2,1)}) %reduce-scatter.33.cloned.1.call-update) | async-done | bytes 1572880 | tf_op jit(solution)/shard_map/reduce_scatter | solution.py:352
  2811.4 209.8 %reduce-scatter.37.cloned.1.call-done = bf16[192,4096]{1,0:T(8,128)(2,1)} async-done(((bf16[1536,4096]{1,0:T(8,128)(2,1)}), bf16[192,4096]{1,0:T(8,128)(2,1)}) %reduce-scatter.37.cloned.1.call-update) | async-done | bytes 1572880 | tf_op jit(solution)/shard_map/reduce_scatter | solution.py:355
  3021.2 210.0 %reduce-scatter.41.cloned.1.call-done = bf16[512,1536]{1,0:T(8,128)(2,1)} async-done(((bf16[4096,1536]{1,0:T(8,128)(2,1)}), bf16[512,1536]{1,0:T(8,128)(2,1)}) %reduce-scatter.41.cloned.1.call-update) | async-done | bytes 1572880 | tf_op jit(solution)/shard_map/reduce_scatter | solution.py:358
  3231.2 209.8 %reduce-scatter.39.cloned.1.call-done = bf16[512,1536]{1,0:T(8,128)(2,1)} async-done(((bf16[4096,1536]{1,0:T(8,128)(2,1)}), bf16[512,1536]{1,0:T(8,128)(2,1)}) %reduce-scatter.39.cloned.1.call-update) | async-done | bytes 1572880 | tf_op jit(solution)/shard_map/reduce_scatter | solution.py:358
  3441.0 209.8 %reduce-scatter.31.cloned.1.call-done = bf16[192,4096]{1,0:T(8,128)(2,1)} async-done(((bf16[1536,4096]{1,0:T(8,128)(2,1)}), bf16[192,4096]{1,0:T(8,128)(2,1)}) %reduce-scatter.31.cloned.1.call-update) | async-done | bytes 1572880 | tf_op jit(solution)/shard_map/reduce_scatter | solution.py:352
  3650.8 210.0 %reduce-scatter.35.cloned.1.call-done = bf16[192,4096]{1,0:T(8,128)(2,1)} async-done(((bf16[1536,4096]{1,0:T(8,128)(2,1)}), bf16[192,4096]{1,0:T(8,128)(2,1)}) %reduce-scatter.35.cloned.1.call-update) | async-done | bytes 1572880 | tf_op jit(solution)/shard_map/reduce_scatter | solution.py:355
  3933.4 162.5 %all-reduce.14.cloned.1.call-done = (bf16[1,192,1536]{2,1,0:T(8,128)(2,1)}, bf16[1,192,1536]{2,1,0:T(8,128)(2,1)}, bf16[1,192,768]{2,1,0:T(8,128)(2,1)}, bf16[1,...) async-done(((bf16[1,192,1536]{2,1,0:T(8,128)(2,1)}, ...) | async-done | bytes 12976144 | tf_op jit(solution)/shard_map/psum | solution.py:375
  (636 shorter events, 1155.8 us)
Async XLA Ops:
  13.7 293.0 %all-gather.39.cloned.1.call-start = ((), (), s32[]{:S(2)}) async-start(), calls=%async_computation.43 | async-start | bytes 5308416 | tf_op jit(solution)/shard_map/all_gather | solution.py:305
  16.1 441.9 %all-gather.41.cloned.1.call-start = ((), (), s32[]{:S(2)}) async-start(), calls=%async_computation.44 | async-start | bytes 14155776 | tf_op jit(solution)/shard_map/all_gather | solution.py:307
  18.1 616.7 %all-gather.43.cloned.1.call-start = ((), (), s32[]{:S(2)}) async-start(), calls=%async_computation.45 | async-start | bytes 14155776 | tf_op jit(solution)/shard_map/all_gather | solution.py:308
  22.2 789.4 %all-gather.45.cloned.1.call-start = ((), (), s32[]{:S(2)}) async-start(), calls=%async_computation.46 | async-start | bytes 14155776 | tf_op jit(solution)/shard_map/all_gather | solution.py:309
  24.3 868.2 %all-gather.51.cloned.1.call-start = ((), (), s32[]{:S(2)}) async-start(), calls=%async_computation.49 | async-start | bytes 5308416 | tf_op jit(solution)/shard_map/all_gather | solution.py:302
  25.0 919.9 %all-gather.47.cloned.1.call-start = ((), (), s32[]{:S(2)}) async-start(), calls=%async_computation.47 | async-start | bytes 2654208 | tf_op jit(solution)/shard_map/all_gather | solution.py:303
  25.7 971.8 %all-gather.49.cloned.1.call-start = ((), (), s32[]{:S(2)}) async-start(), calls=%async_computation.48 | async-start | bytes 2654208 | tf_op jit(solution)/shard_map/all_gather | solution.py:304
  26.3 1148.5 %all-gather.59.cloned.1.call-start = ((), (), s32[]{:S(2)}) async-start(), calls=%async_computation.53 | async-start | bytes 14155776 | tf_op jit(solution)/shard_map/all_gather | solution.py:309
  27.1 1227.9 %all-gather.53.cloned.1.call-start = ((), (), s32[]{:S(2)}) async-start(), calls=%async_computation.50 | async-start | bytes 5308416 | tf_op jit(solution)/shard_map/all_gather | solution.py:305
  27.6 1404.7 %all-gather.57.cloned.1.call-start = ((), (), s32[]{:S(2)}) async-start(), calls=%async_computation.52 | async-start | bytes 14155776 | tf_op jit(solution)/shard_map/all_gather | solution.py:308
  283.5 1326.1 %all-gather.55.cloned.1.call-start = ((), (), s32[]{:S(2)}) async-start(), calls=%async_computation.51 | async-start | bytes 14155776 | tf_op jit(solution)/shard_map/all_gather | solution.py:307
  1821.5 388.9 %reduce-scatter.21.cloned.1.call-start = ((), (), s32[]{:S(2)}) async-start(), calls=%async_computation.29 | async-start | bytes 2654208 | tf_op jit(solution)/shard_map/reduce_scatter | solution.py:340
  1924.4 286.0 %reduce-scatter.25.cloned.1.call-start = ((), (), s32[]{:S(2)}) async-start(), calls=%async_computation.31 | async-start | bytes 2654208 | tf_op jit(solution)/shard_map/reduce_scatter | solution.py:343
  1928.7 281.7 %reduce-scatter.19.cloned.1.call-start = ((), (), s32[]{:S(2)}) async-start(), calls=%async_computation.28 | async-start | bytes 2654208 | tf_op jit(solution)/shard_map/reduce_scatter | solution.py:340
  2078.9 323.1 %reduce-scatter.27.cloned.1.call-start = ((), (), s32[]{:S(2)}) async-start(), calls=%async_computation.32 | async-start | bytes 5308416 | tf_op jit(solution)/shard_map/reduce_scatter | solution.py:346
  2086.7 414.7 %reduce-scatter.17.cloned.1.call-start = ((), (), s32[]{:S(2)}) async-start(), calls=%async_computation.27 | async-start | bytes 5308416 | tf_op jit(solution)/shard_map/reduce_scatter | solution.py:337
  2092.9 507.9 %reduce-scatter.15.cloned.1.call-start = ((), (), s32[]{:S(2)}) async-start(), calls=%async_computation.26 | async-start | bytes 5308416 | tf_op jit(solution)/shard_map/reduce_scatter | solution.py:337
  2132.0 679.4 %reduce-scatter.33.cloned.1.call-start = ((), (), s32[]{:S(2)}) async-start(), calls=%async_computation.35 | async-start | bytes 14155776 | tf_op jit(solution)/shard_map/reduce_scatter | solution.py:352
  2145.3 875.9 %reduce-scatter.37.cloned.1.call-start = ((), (), s32[]{:S(2)}) async-start(), calls=%async_computation.37 | async-start | bytes 14155776 | tf_op jit(solution)/shard_map/reduce_scatter | solution.py:355
  2157.3 1073.9 %reduce-scatter.41.cloned.1.call-start = ((), (), s32[]{:S(2)}) async-start(), calls=%async_computation.39 | async-start | bytes 14155776 | tf_op jit(solution)/shard_map/reduce_scatter | solution.py:358
  2171.0 1270.0 %reduce-scatter.39.cloned.1.call-start = ((), (), s32[]{:S(2)}) async-start(), calls=%async_computation.38 | async-start | bytes 14155776 | tf_op jit(solution)/shard_map/reduce_scatter | solution.py:358
  2184.9 1466.0 %reduce-scatter.31.cloned.1.call-start = ((), (), s32[]{:S(2)}) async-start(), calls=%async_computation.34 | async-start | bytes 14155776 | tf_op jit(solution)/shard_map/reduce_scatter | solution.py:352
  2198.1 1662.7 %reduce-scatter.35.cloned.1.call-start = ((), (), s32[]{:S(2)}) async-start(), calls=%async_computation.36 | async-start | bytes 14155776 | tf_op jit(solution)/shard_map/reduce_scatter | solution.py:355
  2210.3 1885.6 %all-reduce.14.cloned.1.call-start = ((), (), s32[]{:S(2)}) async-start(), calls=%async_computation.54 | async-start | bytes 25952256 | tf_op jit(solution)/shard_map/psum | solution.py:375
  (162 other events, 3557.2 us)
Sparse Core Ops, SparseCore 0:
  122.3 78.4 all-gather.36
  202.8 78.0 all-gather.38
  283.4 174.5 all-gather.40
  460.1 174.6 all-gather.42
  636.9 174.6 all-gather.44
  814.3 78.0 all-gather.50
  999.8 175.0 all-gather.58
  1176.9 78.0 all-gather.52
  1257.7 174.5 all-gather.56
  1434.9 174.6 all-gather.54
  1934.8 68.0 reduce-scatter.24
  2066.9 66.3 reduce-scatter.18
  2136.7 68.0 reduce-scatter.22
  2209.0 94.4 reduce-scatter.28
  2307.0 95.0 reduce-scatter.26
  2406.3 95.0 reduce-scatter.16
  2505.6 95.1 reduce-scatter.14
  2604.4 206.9 reduce-scatter.32
  2814.8 206.3 reduce-scatter.36
  3024.8 206.3 reduce-scatter.40
  3234.6 206.3 reduce-scatter.38
  3444.5 206.3 reduce-scatter.30
  3654.4 206.3 reduce-scatter.34
  3865.0 230.9 all-reduce.13
  (5 shorter events, 272.7 us)
where the time goes:
time: 4130 us; the launch traced here: 4120 us
  waiting for transfers between devices  3150 us (76%)
  matrix products  480 us (12%)
  local copies, waits for them, and re-layouts  199 us (5%)
  blocking collectives  128 us (3%)
  other arithmetic  96.3 us (2%)
  starting transfers between devices  42.2 us (1%)
    reduce_scatter x2, waiting for transfers between devices, body(): lax.psum_scatter(gate_g.astype(jnp.bfloat16), 'dp', scatter_dimension=0,...  420 us
    reduce_scatter x2, waiting for transfers between devices, body(): lax.psum_scatter(down_g.astype(jnp.bfloat16), 'dp', scatter_dimension=0,...  420 us
    reduce_scatter x2, waiting for transfers between devices, body(): lax.psum_scatter(up_g.astype(jnp.bfloat16), 'dp', scatter_dimension=0, ti...  420 us
    all_gather x2, waiting for transfers between devices, body(): lax.all_gather(w_up[layer_idx], 'dp', axis=0, tiled=True)  333 us
    all_gather x2, waiting for transfers between devices, body(): lax.all_gather(w_gate[layer_idx], 'dp', axis=0, tiled=True)  309 us
    all_gather x2, waiting for transfers between devices, body(): lax.all_gather(w_down[layer_idx], 'dp', axis=0, tiled=True)  258 us
    reduce_scatter x2, waiting for transfers between devices, body(): lax.psum_scatter(query_g.astype(jnp.bfloat16), 'dp', scatter_dimension=0,...  199 us
    reduce_scatter x2, waiting for transfers between devices, body(): lax.psum_scatter(out_g.astype(jnp.bfloat16), 'dp', scatter_dimension=0, t...  192 us
  transfers between devices with their start and end apart: 39, of which 30 were waited for; matrix products, arithmetic and copies ran while one was open for 13% of the time, Pallas kernels for 0%

commit v1 on v0

v1 whole, which is shorter than its diff:
```python
import jax
import jax.numpy as jnp
from jax import lax
from jax.sharding import PartitionSpec as P

HD = 96
SCALE = HD ** (-0.5)
EPSILON = 1e-05
ROPE_BASE = 100000.0

CORE_SWAP = [(0, 1), (1, 0), (2, 3), (3, 2)]
Y_SWAP = [(0, 2), (2, 0), (1, 3), (3, 1)]


def other_core(value):
    return lax.ppermute(value, "seq", CORE_SWAP)


def other_y(value):
    return lax.ppermute(value, "seq", Y_SWAP)


def gather_dp(piece):
    return lax.all_gather(piece, "dp", axis=0, tiled=True)


def scatter_dp(full):
    return lax.psum_scatter(full, "dp", scatter_dimension=0, tiled=True)


def dot(left, right):
    return jnp.dot(left, right, preferred_element_type=jnp.float32)


def dot_t(left, right):
    return lax.dot_general(
        left, right, (((1,), (1,)), ((), ())), preferred_element_type=jnp.float32
    )


def tdot(left, right):
    return lax.dot_general(
        left, right, (((0,), (0,)), ((), ())), preferred_element_type=jnp.float32
    )


def pair(flag, mine, other, axis=0):
    return jnp.where(
        flag == 0,
        jnp.concatenate([mine, other], axis=axis),
        jnp.concatenate([other, mine], axis=axis),
    )


def rotate(values, cosine, sine):
    middle = values.shape[-1] // 2
    first = values[..., :middle]
    second = values[..., middle:]
    cos_b = cosine[:, None, :]
    sin_b = sine[:, None, :]
    return jnp.concatenate(
        [first * cos_b - second * sin_b, second * cos_b + first * sin_b], axis=-1
    )


def norm_rows(stream, gain):
    inverse = lax.rsqrt(jnp.mean(stream * stream, axis=-1, keepdims=True) + EPSILON)
    normed = stream * inverse
    return (normed, inverse, (normed * gain).astype(jnp.bfloat16))


def norm_back(grad_out, normed, inverse, gain):
    gain_grad = jnp.sum(grad_out * normed, axis=0)
    scaled = grad_out * gain
    grad_in = inverse * (scaled - normed * jnp.mean(scaled * normed, axis=-1, keepdims=True))
    return (grad_in, gain_grad)


def scores_of(queries, keys, allowed):
    raw = jnp.einsum("qgah,kgh->gaqk", queries, keys, preferred_element_type=jnp.float32) * SCALE
    return jnp.where(allowed, raw, -1e30)


def attend_forward(queries, keys, values, allowed):
    scores = scores_of(queries, keys, allowed)
    maxima = jnp.max(scores, axis=-1, keepdims=True)
    exponent_vals = jnp.exp(scores - maxima)
    totals = jnp.sum(exponent_vals, axis=-1, keepdims=True)
    softened = (exponent_vals / totals).astype(jnp.bfloat16)
    mixed = jnp.einsum("gaqk,kgh->qgah", softened, values, preferred_element_type=jnp.float32)
    return (
        mixed.astype(jnp.bfloat16).reshape(mixed.shape[0], -1),
        (maxima + jnp.log(totals))[..., 0],
    )


def attend_backward(queries, keys, values, log_total, grad_out, allowed):
    scores = scores_of(queries, keys, allowed)
    softened = jnp.exp(scores - log_total[..., None])
    soft_low = softened.astype(jnp.bfloat16)
    grad_values = jnp.einsum(
        "gaqk,qgah->kgh", soft_low, grad_out, preferred_element_type=jnp.float32
    )
    grad_soft = jnp.einsum("qgah,kgh->gaqk", grad_out, values, preferred_element_type=jnp.float32)
    grad_scores = softened * (grad_soft - jnp.sum(softened * grad_soft, axis=-1, keepdims=True))
    scores_low = grad_scores.astype(jnp.bfloat16)
    grad_queries = (
        jnp.einsum("gaqk,kgh->qgah", scores_low, keys, preferred_element_type=jnp.float32) * SCALE
    )
    grad_keys = (
        jnp.einsum("gaqk,qgah->kgh", scores_low, queries, preferred_element_type=jnp.float32)
        * SCALE
    )
    return (
        grad_queries.astype(jnp.bfloat16),
        grad_keys.astype(jnp.bfloat16),
        grad_values.astype(jnp.bfloat16),
    )


def body(
    tokens, cotangent, attn_norm, w_query, w_key, w_value, w_out, mlp_norm, w_gate, w_up, w_down
):
    dp_size = lax.axis_size("dp")
    index = lax.axis_index("seq")
    core = index % 2
    side = index // 2
    _, span, features = tokens.shape
    layers = w_query.shape[0]
    rows = w_query.shape[1]
    q_half = w_query.shape[2] // 2
    k_half = w_key.shape[2] // 2
    ff = w_gate.shape[2]
    part = ff // (4 * dp_size)
    ff_quarter = ff // 4
    out_half = features // 2
    heads = q_half // HD
    kv_heads = k_half // HD
    mine_rows = 2 * span
    length = 4 * span

    def regroup(block):
        kept = lax.dynamic_index_in_dim(block, side, 0, keepdims=False)
        sent = lax.dynamic_index_in_dim(block, 1 - side, 0, keepdims=False)
        return pair(side, kept, other_y(sent))

    def ungroup(block):
        halves = block.reshape(2, span, features)
        kept = lax.dynamic_index_in_dim(halves, side, 0, keepdims=False)
        sent = lax.dynamic_index_in_dim(halves, 1 - side, 0, keepdims=False)
        got = other_y(sent)
        return pair(side, kept[None], got[None])

    def both_cores(value):
        return pair(core, value, other_core(value))

    def own_rows(total):
        kept = lax.dynamic_slice_in_dim(total, core * mine_rows, mine_rows, 0)
        sent = lax.dynamic_slice_in_dim(total, (1 - core) * mine_rows, mine_rows, 0)
        got = other_core(sent.astype(jnp.bfloat16))
        return kept + got.astype(jnp.float32)

    block_order = jnp.array([0, 2, 1, 3], jnp.int32)
    positions = (block_order[:, None] * span + jnp.arange(span)[None, :]).reshape(-1)
    middle = HD // 2
    frequency = ROPE_BASE ** (-jnp.arange(middle, dtype=jnp.float32) / middle)
    angles = positions.astype(jnp.float32)[:, None] * frequency[None, :]
    cosine = jnp.cos(angles)
    sine = jnp.sin(angles)
    allowed = positions[:, None] >= positions[None, :]

    gains = gather_dp(jnp.stack([attn_norm, mlp_norm]).reshape(2 * layers, rows).T)
    gains = gains.T.astype(jnp.float32).reshape(2, layers, features)

    def gather_layer(layer):
        qkv_local = jnp.concatenate(
            [
                lax.dynamic_slice_in_dim(w_query[layer], core * q_half, q_half, 1),
                lax.dynamic_slice_in_dim(w_key[layer], core * k_half, k_half, 1),
                lax.dynamic_slice_in_dim(w_value[layer], core * k_half, k_half, 1),
            ],
            axis=1,
        )
        qkv = gather_dp(qkv_local)
        out_cols = gather_dp(lax.dynamic_slice_in_dim(w_out[layer], core * out_half, out_half, 1))
        kept = lax.dynamic_slice_in_dim(out_cols, core * q_half, q_half, 0)
        sent = lax.dynamic_slice_in_dim(out_cols, (1 - core) * q_half, q_half, 0)
        out = pair(core, kept, other_core(sent), axis=1)

        def quarter(weight):
            cut = weight.reshape(rows, dp_size, 4, part)
            return lax.dynamic_index_in_dim(cut, index, 2, keepdims=False).reshape(rows, ff_quarter)

        gate_up = gather_dp(
            jnp.concatenate([quarter(w_gate[layer]), quarter(w_up[layer])], axis=1)
        )
        down = gather_dp(lax.dynamic_slice_in_dim(w_down[layer], index * part, part, 0))
        return qkv, out, ((gate_up, down), (other_y(gate_up), other_y(down)))

    def forward(stream, weights, gain_one, gain_two):
        qkv_w, out_w, mlp_w = weights
        normed_one, inverse_one, input_one = norm_rows(stream, gain_one)
        full_one = both_cores(input_one)
        raw = dot(full_one, qkv_w)
        queries = rotate(raw[:, :q_half].reshape(length, heads, HD), cosine, sine)
        keys = rotate(
            raw[:, q_half : q_half + k_half].reshape(length, kv_heads, HD), cosine, sine
        ).astype(jnp.bfloat16)
        queries = queries.astype(jnp.bfloat16).reshape(length, kv_heads, 2, HD)
        values = raw[:, q_half + k_half :].astype(jnp.bfloat16).reshape(length, kv_heads, HD)
        mixed, log_total = attend_forward(queries, keys, values, allowed)
        stream_two = stream + own_rows(dot(mixed, out_w))
        normed_two, inverse_two, input_two = norm_rows(stream_two, gain_two)
        full_two = both_cores(input_two)
        total = None
        kept_mlp = []
        for gate_up_w, down_w in mlp_w:
            gate_up = dot(full_two, gate_up_w)
            gate, up = gate_up[:, :ff_quarter], gate_up[:, ff_quarter:]
            hidden = (jax.nn.silu(gate) * up).astype(jnp.bfloat16)
            term = dot(hidden, down_w)
            total = term if total is None else total + term
            kept_mlp.append((gate, up, hidden))
        result = stream_two + own_rows(total)
        saved = (
            normed_one,
            inverse_one,
            full_one,
            queries,
            keys,
            values,
            log_total,
            mixed,
            normed_two,
            inverse_two,
            full_two,
            kept_mlp,
        )
        return result, saved

    def backward(grad, saved, weights, gain_one, gain_two):
        (
            normed_one,
            inverse_one,
            full_one,
            queries,
            keys,
            values,
            log_total,
            mixed,
            normed_two,
            inverse_two,
            full_two,
            kept_mlp,
        ) = saved
        qkv_w, out_w, mlp_w = weights
        grad_full = both_cores(grad.astype(jnp.bfloat16))
        total = None
        mlp_grads = []
        for (gate_up_w, down_w), (gate, up, hidden) in zip(mlp_w, kept_mlp):
            grad_down = tdot(hidden, grad_full).astype(jnp.bfloat16)
            grad_hidden = dot_t(grad_full, down_w)
            sig = jax.nn.sigmoid(gate)
            grad_gate = grad_hidden * up * sig * (1.0 + gate * (1.0 - sig))
            grad_up = grad_hidden * gate * sig
            grad_gate_up = jnp.concatenate([grad_gate, grad_up], axis=1).astype(jnp.bfloat16)
            grad_gate_up_w = tdot(full_two, grad_gate_up).astype(jnp.bfloat16)
            term = dot_t(grad_gate_up, gate_up_w)
            total = term if total is None else total + term
            mlp_grads.append((grad_gate_up_w, grad_down))
        grad_two = own_rows(total)
        norm_two_in, gain_two_g = norm_back(grad_two, normed_two, inverse_two, gain_two)
        grad_mid = grad + norm_two_in
        mid_full = both_cores(grad_mid.astype(jnp.bfloat16))
        grad_out_w = tdot(mixed, mid_full).astype(jnp.bfloat16)
        grad_mixed = dot_t(mid_full, out_w).astype(jnp.bfloat16)
        grad_heads = grad_mixed.reshape(length, kv_heads, 2, HD)
        grad_q, grad_k, grad_v = attend_backward(
            queries, keys, values, log_total, grad_heads, allowed
        )
        grad_q = rotate(
            grad_q.reshape(length, heads, HD).astype(jnp.float32), cosine, -sine
        ).astype(jnp.bfloat16)
        grad_k = rotate(grad_k.astype(jnp.float32), cosine, -sine).astype(jnp.bfloat16)
        grad_qkv = jnp.concatenate(
            [
                grad_q.reshape(length, q_half),
                grad_k.reshape(length, k_half),
                grad_v.reshape(length, k_half),
            ],
            axis=1,
        )
        grad_qkv_w = tdot(full_one, grad_qkv).astype(jnp.bfloat16)
        grad_one = own_rows(dot_t(grad_qkv, qkv_w))
        norm_one_in, gain_one_g = norm_back(grad_one, normed_one, inverse_one, gain_one)
        return grad_mid + norm_one_in, (mlp_grads, grad_out_w, grad_qkv_w, gain_one_g, gain_two_g)

    def seq_pieces(piece):
        cores = pair(core, piece[None], other_core(piece)[None])
        return pair(side, cores, other_y(cores))

    def reduce_mlp(grads):
        (mine_gu, mine_down), (far_gu, far_down) = grads
        gu = scatter_dp(mine_gu + other_y(far_gu))
        down = scatter_dp(mine_down + other_y(far_down))
        gu = seq_pieces(gu).reshape(4, rows, 2, dp_size, part)
        gu = gu.transpose(2, 1, 3, 0, 4).reshape(2, rows, ff).astype(jnp.float32)
        down = seq_pieces(down).reshape(4 * part, features).astype(jnp.float32)
        return gu[0], gu[1], down

    def reduce_out(grad):
        cut = grad.reshape(q_half, 2, out_half)
        kept = lax.dynamic_index_in_dim(cut, core, 1, keepdims=False)
        sent = lax.dynamic_index_in_dim(cut, 1 - core, 1, keepdims=False)
        cols = pair(core, kept, other_core(sent), axis=0)
        piece = scatter_dp(cols)
        summed = (piece.astype(jnp.float32) + other_y(piece).astype(jnp.float32)).astype(
            jnp.bfloat16
        )
        return pair(core, summed, other_core(summed), axis=1).astype(jnp.float32)

    def reduce_qkv(grad):
        piece = scatter_dp(grad)
        summed = (piece.astype(jnp.float32) + other_y(piece).astype(jnp.float32)).astype(
            jnp.bfloat16
        )
        got = other_core(summed)

        def joined(start, size):
            return pair(
                core, summed[:, start : start + size], got[:, start : start + size], axis=1
            ).astype(jnp.float32)

        return (
            joined(0, q_half),
            joined(q_half, k_half),
            joined(q_half + k_half, k_half),
            (summed[:, q_half + 2 * k_half :], got[:, q_half + 2 * k_half :]),
        )

    stream = regroup(tokens).astype(jnp.float32)
    all_weights = [gather_layer(layer) for layer in range(layers)]
    all_saved = []
    for layer in range(layers):
        stream, saved = forward(stream, all_weights[layer], gains[0, layer], gains[1, layer])
        all_saved.append(saved)
    output = ungroup(stream.astype(jnp.bfloat16))
    grad = regroup(cotangent).astype(jnp.float32)
    reduced = [None] * layers
    gain_grads = []
    for layer in reversed(range(layers)):
        grad, (mlp_g, out_g, qkv_g, one_g, two_g) = backward(
            grad, all_saved[layer], all_weights[layer], gains[0, layer], gains[1, layer]
        )
        gain_grads = [one_g, two_g] + gain_grads
        if layer == 0:
            extra = jnp.stack(gain_grads, axis=1)
            extra = jnp.pad(extra, ((0, 0), (0, 128 - extra.shape[1])))
            qkv_g = jnp.concatenate([qkv_g, extra.astype(jnp.bfloat16)], axis=1)
        reduced[layer] = (reduce_mlp(mlp_g), reduce_out(out_g), reduce_qkv(qkv_g))
    d_tokens = ungroup(grad)
    first, second = reduced[0][2][3]
    gain_out = first.astype(jnp.float32) + second.astype(jnp.float32)
    gain_out = gain_out[:, : 2 * layers].T.reshape(layers, 2, rows)

    def stacked(pick):
        return jnp.stack([pick(reduced[layer]) for layer in range(layers)])

    return (
        output,
        d_tokens,
        gain_out[:, 0],
        stacked(lambda r: r[2][0]),
        stacked(lambda r: r[2][1]),
        stacked(lambda r: r[2][2]),
        stacked(lambda r: r[1]),
        gain_out[:, 1],
        stacked(lambda r: r[0][0]),
        stacked(lambda r: r[0][1]),
        stacked(lambda r: r[0][2]),
    )


def solution(mesh):
    in_specs = (
        P("dp", "seq", None),
        P("dp", "seq", None),
        P(None, "dp"),
        P(None, "dp", None),
        P(None, "dp", None),
        P(None, "dp", None),
        P(None, "dp", None),
        P(None, "dp"),
        P(None, "dp", None),
        P(None, "dp", None),
        P(None, "dp", None),
    )
    return jax.shard_map(
        body, mesh=mesh, in_specs=in_specs, out_specs=in_specs, check_vma=False
    )
```

time: 4130 us -> 1890 us (0.46)
  waiting for transfers between devices: 3150 us -> 878 us
  other arithmetic: 96.3 us -> 204 us
  blocking collectives: 128 us -> 27.1 us
    reduce_scatter x14 -> x6, waiting for transfers between devices: 1650 us -> 0.07 us  [scatter_dp(): return lax.psum_scatter(full, 'dp', scatter_dimension=0, tiled=True)]
    all_gather x14 -> x8, waiting for transfers between devices: 1220 us -> 200 us  [gather_dp(): return lax.all_gather(piece, 'dp', axis=0, tiled=True)]
    ppermute x0 -> x48, waiting for transfers between devices: none -> 678 us  [the longest x20 659 us: other_y(): return lax.ppermute(value, 'seq', Y_SWAP)]
    psum x1 -> x0, waiting for transfers between devices: 163 us -> none  [body(): lax.psum(part_two.astype(jnp.bfloat16), 'seq').astype(jnp.float32)]
    all_to_all x10 -> x0, waiting for transfers between devices: 120 us -> none  [the longest x2 35.8 us: layer_backward(): lax.all_to_all(grad_mixed.reshape(seq_dev, span_rows, groups, -1), 'seq',...]
    unnamed x2 -> x0, blocking collectives: 75.2 us -> none
    dynamic_slice x0 -> x20, local copies, waits for them, and re-layouts: none -> 61.3 us  [the longest x4 22.8 us: reduce_out(): kept = lax.dynamic_index_in_dim(cut, core, 1, keepdims=False)]
    slice x15 -> x38, local copies, waits for them, and re-layouts: 21 us -> 70.3 us  [the longest x10 30.3 us: reduce_mlp(): return (gu[0], gu[1], down)]
  transfers between devices with their start and end apart: 39 -> 64, of which waited for: 30 -> 26; matrix products, arithmetic and copies ran while one was open for 13% -> 45% of each run, Pallas kernels for 0% -> 0%
where the time goes in v1:
time: 1890 us; the launch traced here: 1880 us
  waiting for transfers between devices  878 us (46%)
  matrix products  497 us (26%)
  local copies, waits for them, and re-layouts  225 us (12%)
  other arithmetic  204 us (11%)
  starting transfers between devices  32.8 us (2%)
  blocking collectives  27.1 us (1%)
    ppermute x20, waiting for transfers between devices, other_y(): return lax.ppermute(value, 'seq', Y_SWAP)  659 us
    all_gather x8, waiting for transfers between devices, gather_dp(): return lax.all_gather(piece, 'dp', axis=0, tiled=True)  200 us
    dot_general x12, matrix products, dot_t(): lax.dot_general(left, right, (((1,), (1,)), ((), ())), preferred_element_...  117 us
    dot_general x12, matrix products, tdot(): lax.dot_general(left, right, (((0,), (0,)), ((), ())), preferred_element_...  105 us
    dot_general x12, matrix products, dot(): return jnp.dot(left, right, preferred_element_type=jnp.float32)  88.7 us
    unnamed x313, local copies, waits for them, and re-layouts  58.4 us
    convert_element_type x2, other arithmetic, attend_backward(): scores_low = grad_scores.astype(jnp.bfloat16)  58.2 us
    dot_general x2, matrix products, attend_backward(): jnp.einsum('qgah,kgh->gaqk', grad_out, values, preferred_element_type=jnp...  49.9 us
  transfers between devices with their start and end apart: 64, of which 26 were waited for; matrix products, arithmetic and copies ran while one was open for 45% of the time, Pallas kernels for 0%

profile of v1, /device:TPU:0, one launch (start us, length us, event | category | flops | bytes accessed | tf_op | source)
XLA Modules:
  0.0 1880.7 jit_solution(16793113790261461939)
XLA Ops:
  39.5 27.1 %all-gather.4 = bf16[8,192,4]{1,2,0:T(4,128)(2,1)S(1)} all-gather(bf16[1,192,4]{1,2,0:T(4,128)(2,1)S(1)} %bitcast.417), channel_id=1, replica_groups=mesh['dp'=8,'seq'=4] {'dp'}, dimensions={0}, use_global_device_ids=true | all-gather | bytes 13824 | tf_op jit(solution)/shard_map/all_gather | solution.py:24
  91.5 55.5 %all-gather.14.cloned.1.call-done = bf16[1536,1536]{1,0:T(8,128)(2,1)} async-done(((bf16[192,1536]{1,0:T(8,128)(2,1)}), bf16[1536,1536]{1,0:T(8,128)(2,1)}) %all-gather.14.cloned.1.call-update) | async-done | bytes 4718608 | tf_op jit(solution)/shard_map/all_gather | solution.py:24
  201.7 16.4 fusion.38
  227.1 19.8 %all-gather.16.cloned.1.call-done = bf16[1536,2048]{1,0:T(8,128)(2,1)} async-done(((bf16[192,2048]{1,0:T(8,128)(2,1)}), bf16[1536,2048]{1,0:T(8,128)(2,1)}) %all-gather.16.cloned.1.call-update) | async-done | bytes 6291472 | tf_op jit(solution)/shard_map/all_gather | solution.py:24
  255.0 52.6 %all-gather.24.cloned.1.call-done = bf16[1,1024,1536]{2,1,0:T(8,128)(2,1)} async-done(((bf16[1,128,1536]{2,1,0:T(8,128)(2,1)}), bf16[1,1024,1536]{2,1,0:T(8,128)(2,1)}) %all-gather.24.cloned.1.call-update) | async-done | bytes 3145744 | tf_op jit(solution)/shard_map/all_gather | solution.py:24
  327.4 58.3 %collective-permute-done.5 = bf16[1536,2048]{1,0:T(8,128)(2,1)} collective-permute-done((bf16[1536,2048]{1,0:T(8,128)(2,1)}, bf16[1536,2048]{1,0:T(8,128)(2,1)}, u32[]{:S(2)}, u32[]{:S(2)}) %collective-permute-start.5) | collective-permute-done | bytes 6291488 | tf_op jit(solution)/shard_map/ppermute | solution.py:20
  399.6 51.6 %collective-permute-done.6 = bf16[1024,1536]{1,0:T(8,128)(2,1)S(1)} collective-permute-done((bf16[1024,1536]{1,0:T(8,128)(2,1)}, bf16[1024,1536]{1,0:T(8,128)(2,1)S(1)}, u32[]{:S(2)}, u32[]{:S(2)}) %collective-permute-start.6) | collective-permute-done | bytes 3145760 | tf_op jit(solution)/shard_map/ppermute | solution.py:20
  468.3 72.4 %all-gather.18.cloned.1.call-done = bf16[1536,1536]{1,0:T(8,128)(2,1)} async-done(((bf16[192,1536]{1,0:T(8,128)(2,1)}), bf16[1536,1536]{1,0:T(8,128)(2,1)}) %all-gather.18.cloned.1.call-update) | async-done | bytes 4718608 | tf_op jit(solution)/shard_map/all_gather | solution.py:24
  565.1 15.8 fusion.19
  595.4 15.2 fusion.37
  625.1 83.9 %collective-permute-done.16 = bf16[256,1536]{1,0:T(8,128)(2,1)S(1)} collective-permute-done((bf16[256,1536]{1,0:T(8,128)(2,1)S(1)}, bf16[256,1536]{1,0:T(8,128)(2,1)S(1)}, u32[]{:S(2)}, u32[]{:S(2)}) %collective-permute-start.16) | collective-permute-done | bytes 786464 | tf_op jit(solution)/shard_map/ppermute | solution.py:20
  863.3 25.0 %fusion.3 = (f32[4,2,1024]{2,1,0:T(2,128)S(1)}, f32[4,1024,1024,2]{2,1,3,0:T(8,128)}) fusion(f32[4,2,1024]{2,1,0:T(2,128)S(1)} %bitcast.404, f32[4,1024,1024,2]{2,1,3,0:T(8,128)} %get-tuple-element.167, pred[1024,1024]{0,1:T(8,128)(4,1)S(1)} %copy-done.1, bf16[1024,4,96,1]{0,2,3,1:T(8,128)(2,1)S(1)} %bitcast.352, bf16[1024,4,2,96]{0,3,2,1:T(8,128)(2,1)S(1)} %bitcast.389), kind=kOutput, calls=%fused_computation.7 | convolution fusion | flops 1652547584 | bytes 70582272 | tf_op jit(solution)/shard_map/qgah,kgh->gaqk/dot_general | solution.py:104
  888.4 28.9 %fusion.5 = bf16[4,2,1024,1024]{2,3,1,0:T(8,128)(2,1)} fusion(f32[4,1024,1024,2]{2,1,3,0:T(8,128)} %get-tuple-element.169, f32[4,2,1024]{2,1,0:T(2,128)S(1)} %get-tuple-element.168, f32[4,2,1024]{2,1,0:T(2,128)S(1)} %bitcast.405, f32[4,1024,1024,2]{2,1,3,0:T(8,128)} %get-tuple-element.167, pred[1024,1024]{0,1:T(8,128)(4,1)S(1)} %copy-done.1), kind=kLoop, calls=%fused_computation.9 | loop fusion | flops 50331648 | bytes 85000192 | tf_op jit(solution)/shard_map/convert_element_type | solution.py:106
  940.4 16.6 bitcast_convert_fusion.1
  1101.3 56.9 %collective-permute-done.42 = bf16[1024,1536]{1,0:T(8,128)(2,1)S(1)} collective-permute-done((bf16[1024,1536]{1,0:T(8,128)(2,1)S(1)}, bf16[1024,1536]{1,0:T(8,128)(2,1)S(1)}, u32[]{:S(2)}, u32[]{:S(2)}) %collective-permute-start.42) | collective-permute-done | bytes 3145760 | tf_op jit(solution)/shard_map/ppermute | solution.py:20
  1167.4 125.1 %collective-permute-done.39 = bf16[1536,2048]{1,0:T(8,128)(2,1)} collective-permute-done((bf16[1536,2048]{1,0:T(8,128)(2,1)}, bf16[1536,2048]{1,0:T(8,128)(2,1)}, u32[]{:S(2)}, u32[]{:S(2)}) %collective-permute-start.39) | collective-permute-done | bytes 6291488 | tf_op jit(solution)/shard_map/ppermute | solution.py:20
  1312.2 25.0 %fusion = (f32[4,2,1024]{2,1,0:T(2,128)S(1)}, f32[4,1024,1024,2]{2,1,3,0:T(8,128)}) fusion(f32[4,2,1024]{2,1,0:T(2,128)S(1)} %bitcast.407, f32[4,1024,1024,2]{2,1,3,0:T(8,128)} %get-tuple-element.165, pred[1024,1024]{0,1:T(8,128)(4,1)S(1)} %copy-done.2, bf16[1024,4,96,1]{0,2,3,1:T(8,128)(2,1)S(1)} %bitcast.350, bf16[1024,4,2,96]{0,3,2,1:T(8,128)(2,1)S(1)} %bitcast.387), kind=kOutput, calls=%fused_computation.2 | convolution fusion | flops 1652547584 | bytes 70582272 | tf_op jit(solution)/shard_map/qgah,kgh->gaqk/dot_general | solution.py:104
  1337.1 29.3 %fusion.2 = bf16[4,2,1024,1024]{2,3,1,0:T(8,128)(2,1)} fusion(f32[4,1024,1024,2]{2,1,3,0:T(8,128)} %get-tuple-element.171, f32[4,2,1024]{2,1,0:T(2,128)S(1)} %get-tuple-element.170, f32[4,2,1024]{2,1,0:T(2,128)S(1)} %bitcast.408, f32[4,1024,1024,2]{2,1,3,0:T(8,128)} %get-tuple-element.165, pred[1024,1024]{0,1:T(8,128)(4,1)S(1)} %copy-done.2), kind=kLoop, calls=%fused_computation.4 | loop fusion | flops 50331648 | bytes 85000192 | tf_op jit(solution)/shard_map/convert_element_type | solution.py:106
  1390.1 17.1 bitcast_convert_fusion
  1451.4 135.4 %collective-permute-done.36 = bf16[1536,2048]{1,0:T(8,128)(2,1)S(1)} collective-permute-done((bf16[1536,2048]{1,0:T(8,128)(2,1)S(1)}, bf16[1536,2048]{1,0:T(8,128)(2,1)S(1)}, u32[]{:S(2)}, u32[]{:S(2)}) %collective-permute-start.36) | collective-permute-done | bytes 6291488 | tf_op jit(solution)/shard_map/ppermute | solution.py:20
  1614.2 14.8 collective-permute-done.34
  1649.6 40.8 %collective-permute-done.28 = bf16[192,1536]{1,0:T(8,128)(2,1)} collective-permute-done((bf16[192,1536]{1,0:T(8,128)(2,1)}, bf16[192,1536]{1,0:T(8,128)(2,1)}, u32[]{:S(2)}, u32[]{:S(2)}) %collective-permute-start.28) | collective-permute-done | bytes 589856 | tf_op jit(solution)/shard_map/ppermute | solution.py:20
  1744.6 26.3 %collective-permute-done.41 = bf16[2,192,2048]{2,1,0:T(8,128)(2,1)} collective-permute-done((bf16[2,192,2048]{2,1,0:T(8,128)(2,1)}, bf16[2,192,2048]{2,1,0:T(8,128)(2,1)}, u32[]{:S(2)}, u32[]{:S(2)}) %collective-permute-start.41) | collective-permute-done | bytes 1572896 | tf_op jit(solution)/shard_map/ppermute | solution.py:20
  1828.7 19.4 %collective-permute-done.38 = bf16[2,192,2048]{2,1,0:T(8,128)(2,1)} collective-permute-done((bf16[2,192,2048]{2,1,0:T(8,128)(2,1)}, bf16[2,192,2048]{2,1,0:T(8,128)(2,1)}, u32[]{:S(2)}, u32[]{:S(2)}) %collective-permute-start.38) | collective-permute-done | bytes 1572896 | tf_op jit(solution)/shard_map/ppermute | solution.py:20
  (666 shorter events, 835.0 us)
Async XLA Ops:
  10.3 136.6 %all-gather.14.cloned.1.call-start = ((), (), s32[]{:S(2)}) async-start(), calls=%async_computation.8 | async-start | bytes 5308416 | tf_op jit(solution)/shard_map/all_gather | solution.py:24
  13.8 233.2 %all-gather.16.cloned.1.call-start = ((), (), s32[]{:S(2)}) async-start(), calls=%async_computation.9 | async-start | bytes 7077888 | tf_op jit(solution)/shard_map/all_gather | solution.py:24
  31.1 276.5 %all-gather.24.cloned.1.call-start = ((), (), s32[]{:S(2)}) async-start(), calls=%async_computation.17 | async-start | bytes 3538944 | tf_op jit(solution)/shard_map/all_gather | solution.py:24
  34.3 429.1 %all-gather.26.cloned.1.call-start = ((), (), s32[]{:S(2)}) async-start(), calls=%async_computation.18 | async-start | bytes 2654208 | tf_op jit(solution)/shard_map/all_gather | solution.py:24
  36.1 430.7 %all-gather.20.cloned.1.call-start = ((), (), s32[]{:S(2)}) async-start(), calls=%async_computation.11 | async-start | bytes 7077888 | tf_op jit(solution)/shard_map/all_gather | solution.py:24
  85.1 455.6 %all-gather.18.cloned.1.call-start = ((), (), s32[]{:S(2)}) async-start(), calls=%async_computation.10 | async-start | bytes 5308416 | tf_op jit(solution)/shard_map/all_gather | solution.py:24
  91.0 127.2 %collective-permute-start.2 = (bf16[768,768]{1,0:T(8,128)(2,1)}, bf16[768,768]{1,0:T(8,128)(2,1)}, u32[]{:S(2)}, u32[]{:S(2)}) collective-permute-start(bf16[768,768]{1,0:T(8,128)(2,1)} %get-tuple-element.128), channel_id=1, source_target_pairs={{0,1},{1,0},{2,3},{3,2},{4,5},{5,4},{6,7},{7,6},{8,9},{9,8},{10,11... | collective-permute-start | bytes 3538952 | tf_op jit(solution)/shard_map/ppermute | solution.py:16
  246.9 138.8 %collective-permute-start.5 = (bf16[1536,2048]{1,0:T(8,128)(2,1)}, bf16[1536,2048]{1,0:T(8,128)(2,1)}, u32[]{:S(2)}, u32[]{:S(2)}) collective-permute-start(bf16[1536,2048]{1,0:T(8,128)(2,1)} %all-gather.16.cloned.1.call-done), channel_id=1, source_target_pairs={{0,2},{2,0},{1,3},{3,1},{4,6},{6,4},{5,7},{7,5},{8,10},{10,8},{9,1... | collective-permute-start | bytes 18874376 | tf_op jit(solution)/shard_map/ppermute | solution.py:20
  254.9 366.6 %all-gather.28.cloned.1.call-start = ((), (), s32[]{:S(2)}) async-start(), calls=%async_computation.19 | async-start | bytes 3538944 | tf_op jit(solution)/shard_map/all_gather | solution.py:24
  307.6 143.7 %collective-permute-start.6 = (bf16[1024,1536]{1,0:T(8,128)(2,1)}, bf16[1024,1536]{1,0:T(8,128)(2,1)S(1)}, u32[]{:S(2)}, u32[]{:S(2)}) collective-permute-start(bf16[1024,1536]{1,0:T(8,128)(2,1)} %bitcast.426), channel_id=1, source_target_pairs={{0,2},{2,0},{1,3},{3,1},{4,6},{6,4},{5,7},{7,5},{8,10},{10,8},{9,1... | collective-permute-start | bytes 9437192 | tf_op jit(solution)/shard_map/ppermute | solution.py:20
  463.4 1133.9 %reduce-scatter.23.cloned.1.call-start = ((), (), s32[]{:S(2)}) async-start(), calls=%async_computation.15 | async-start | bytes 3538944 | tf_op jit(solution)/shard_map/reduce_scatter | solution.py:28
  466.6 144.0 %collective-permute-start.9 = (bf16[768,768]{1,0:T(8,128)(2,1)}, bf16[768,768]{1,0:T(8,128)(2,1)}, u32[]{:S(2)}, u32[]{:S(2)}) collective-permute-start(bf16[768,768]{1,0:T(8,128)(2,1)} %get-tuple-element.126), channel_id=1, source_target_pairs={{0,1},{1,0},{2,3},{3,2},{4,5},{5,4},{6,7},{7,6},{8,9},{9,8},{10,11... | collective-permute-start | bytes 3538952 | tf_op jit(solution)/shard_map/ppermute | solution.py:16
  466.8 242.8 %collective-permute-start.12 = (bf16[1536,2048]{1,0:T(8,128)(2,1)}, bf16[1536,2048]{1,0:T(8,128)(2,1)}, u32[]{:S(2)}, u32[]{:S(2)}) collective-permute-start(bf16[1536,2048]{1,0:T(8,128)(2,1)} %all-gather.20.cloned.1.call-done), channel_id=1, source_target_pairs={{0,2},{2,0},{1,3},{3,1},{4,6},{6,4},{5,7},{7,5},{8,10},{10,8},{9,1... | collective-permute-start | bytes 18874376 | tf_op jit(solution)/shard_map/ppermute | solution.py:20
  621.5 102.9 %collective-permute-start.13 = (bf16[1024,1536]{1,0:T(8,128)(2,1)}, bf16[1024,1536]{1,0:T(8,128)(2,1)S(1)}, u32[]{:S(2)}, u32[]{:S(2)}) collective-permute-start(bf16[1024,1536]{1,0:T(8,128)(2,1)} %bitcast.427), channel_id=1, source_target_pairs={{0,2},{2,0},{1,3},{3,1},{4,6},{6,4},{5,7},{7,5},{8,10},{10,8},{9,1... | collective-permute-start | bytes 9437192 | tf_op jit(solution)/shard_map/ppermute | solution.py:20
  825.5 775.8 %reduce-scatter.31.cloned.1.call-start = ((), (), s32[]{:S(2)}) async-start(), calls=%async_computation.23 | async-start | bytes 2654208
  856.8 110.1 %collective-permute-start.33 = (bf16[768,768]{0,1:T(8,128)(2,1)}, bf16[768,768]{0,1:T(8,128)(2,1)}, u32[]{:S(2)}, u32[]{:S(2)}) collective-permute-start(bf16[768,768]{0,1:T(8,128)(2,1)} %bitcast.391), channel_id=1, source_target_pairs={{0,1},{1,0},{2,3},{3,2},{4,5},{5,4},{6,7},{7,6},{8,9},{9,8},{10,11... | collective-permute-start | bytes 3538952 | tf_op jit(solution)/shard_map/ppermute | solution.py:16
  971.6 657.6 %reduce-scatter.27.cloned.1.call-start = ((), (), s32[]{:S(2)}) async-start(), calls=%async_computation.21 | async-start | bytes 5308416 | tf_op jit(solution)/shard_map/reduce_scatter | solution.py:28
  994.0 706.0 %reduce-scatter.29.cloned.1.call-start = ((), (), s32[]{:S(2)}) async-start(), calls=%async_computation.22 | async-start | bytes 2654208
  1079.9 622.6 %reduce-scatter.21.cloned.1.call-start = ((), (), s32[]{:S(2)}) async-start(), calls=%async_computation.14 | async-start | bytes 3538944 | tf_op jit(solution)/shard_map/reduce_scatter | solution.py:28
  1100.9 191.6 %collective-permute-start.39 = (bf16[1536,2048]{1,0:T(8,128)(2,1)}, bf16[1536,2048]{1,0:T(8,128)(2,1)}, u32[]{:S(2)}, u32[]{:S(2)}) collective-permute-start(bf16[1536,2048]{1,0:T(8,128)(2,1)} %convolution_convert_fusion.2), channel_id=1, source_target_pairs={{0,2},{2,0},{1,3},{3,1},{4,6},{6,4},{5,7},{7,5},{8,10},{10,8},{9,1... | collective-permute-start | bytes 18874376 | tf_op jit(solution)/shard_map/ppermute | solution.py:20
  1166.6 536.1 %reduce-scatter.19.cloned.1.call-start = ((), (), s32[]{:S(2)}) async-start(), calls=%async_computation.13 | async-start | bytes 7077888 | tf_op jit(solution)/shard_map/reduce_scatter | solution.py:28
  1304.7 434.7 %reduce-scatter.25.cloned.1.call-start = ((), (), s32[]{:S(2)}) async-start(), calls=%async_computation.20 | async-start | bytes 5750784 | tf_op jit(solution)/shard_map/reduce_scatter | solution.py:28
  1438.5 349.5 %reduce-scatter.17.cloned.1.call-start = ((), (), s32[]{:S(2)}) async-start(), calls=%async_computation.12 | async-start | bytes 7077888 | tf_op jit(solution)/shard_map/reduce_scatter | solution.py:28
  1449.8 137.0 %collective-permute-start.36 = (bf16[1536,2048]{1,0:T(8,128)(2,1)S(1)}, bf16[1536,2048]{1,0:T(8,128)(2,1)S(1)}, u32[]{:S(2)}, u32[]{:S(2)}) collective-permute-start(bf16[1536,2048]{1,0:T(8,128)(2,1)S(1)} %convolution_convert_fusion.4), channel_id=1, source_target_pairs={{0,2},{2,0},{1,3},{3,1},{4,6},{6,4},{5,7},{7,5},{8,10},{10,8},{9,1... | collective-permute-start | bytes 18874376 | tf_op jit(solution)/shard_map/ppermute | solution.py:20
  (182 other events, 5059.9 us)
Sparse Core Ops, SparseCore 0:
  10.8 54.8 all-gather.21
  68.4 78.4 all-gather.13
  149.7 97.1 all-gather.15
  248.9 58.6 all-gather.23
  309.6 50.5 all-gather.25
  362.3 97.5 all-gather.19
  462.6 78.0 all-gather.17
  542.9 58.5 all-gather.27
  825.6 72.9 reduce-scatter.22
  971.7 67.4 reduce-scatter.30
  1042.9 94.4 reduce-scatter.26
  1141.3 68.8 reduce-scatter.28
  1213.8 73.1 reduce-scatter.20
  1304.8 116.3 reduce-scatter.18
  1438.7 99.4 reduce-scatter.24
  1597.4 116.6 reduce-scatter.16

commit v2 on v1

v2 whole, which is shorter than its diff:
```python
import functools

import jax
import jax.numpy as jnp
from jax import lax
from jax.experimental import layout
from jax.experimental import pallas as pl
from jax.experimental.pallas import tpu as pltpu
from jax.sharding import PartitionSpec as P

HD = 96
SCALE = HD ** (-0.5)
EPSILON = 1e-05
ROPE_BASE = 100000.0

CORE_SWAP = [(0, 1), (1, 0), (2, 3), (3, 2)]
Y_SWAP = [(0, 2), (2, 0), (1, 3), (3, 1)]


BLOCKS = (0, 2, 1, 3)


def nt(left, right):
    return lax.dot_general(
        left, right, (((1,), (1,)), ((), ())), preferred_element_type=jnp.float32
    )


def nn(left, right):
    return lax.dot_general(
        left, right, (((1,), (0,)), ((), ())), preferred_element_type=jnp.float32
    )


def swap_halves(value):
    half = value.shape[1] // 2
    return jnp.concatenate([value[:, half:], value[:, :half]], axis=1)


def rope(value, cos, sin):
    return value * cos + swap_halves(value) * sin


def masked(scores, top):
    span = scores.shape[1] // 2
    key = lax.broadcasted_iota(jnp.int32, (span, 2 * span), 0)
    query = lax.broadcasted_iota(jnp.int32, (span, 2 * span), 1)
    query = jnp.where(query >= span, query - span, query)
    last = jnp.where(key <= query, scores[top:], -1e30)
    return last if top == 0 else jnp.concatenate([scores[:top], last], axis=0)


def masked_rows(scores, top):
    span = scores.shape[0] // 2
    key = lax.broadcasted_iota(jnp.int32, (2 * span, span), 1)
    query = lax.broadcasted_iota(jnp.int32, (2 * span, span), 0)
    query = jnp.where(query >= span, query - span, query)
    last = jnp.where(key <= query, scores[:, top:], -1e30)
    return last if top == 0 else jnp.concatenate([scores[:, :top], last], axis=1)


def forward_kernel(raw_ref, cos_ref, sin_ref, mixed_ref, q_ref, k_ref, v_ref, lse_ref, o_ref):
    heads = pl.program_id(0)
    span = raw_ref.shape[0] // 4
    count = mixed_ref.shape[1] // (2 * HD)
    for g in range(count):

        @pl.when(heads == g)
        def _(g=g):
            for part, block in enumerate(BLOCKS):
                here = pl.ds(part * span, span)
                there = pl.ds(block * span, span)
                cos, sin = cos_ref[here, :], sin_ref[here, :]
                for a in range(2):
                    at = (2 * g + a) * HD
                    q = rope(raw_ref[here, at : at + HD], cos, sin)
                    q_ref[0, pl.ds((2 * block + a) * span, span), :] = q.astype(jnp.bfloat16)
                at = (2 * count + g) * HD
                k_ref[0, there, :] = rope(raw_ref[here, at : at + HD], cos, sin).astype(
                    jnp.bfloat16
                )
                at = (3 * count + g) * HD
                v_ref[0, there, :] = raw_ref[here, at : at + HD].astype(jnp.bfloat16)

    for block in range(4):
        top, end = block * span, (block + 1) * span
        rows = pl.ds(2 * block * span, 2 * span)
        scores = masked_rows(nt(q_ref[0, rows, :], k_ref[0, :end, :]) * SCALE, top)
        highest = jnp.max(scores, axis=1, keepdims=True)
        powers = jnp.exp(scores - highest)
        total = jnp.sum(powers, axis=1, keepdims=True)
        probs = (powers * (1.0 / total)).astype(jnp.bfloat16)
        lse = jnp.broadcast_to(highest + jnp.log(total), (2 * span, 128))
        lse_ref[0, block : block + 1, :] = lse.T[:1]
        o_ref[rows, :] = nn(probs, v_ref[0, :end, :])
    for g in range(count):

        @pl.when(heads == g)
        def _(g=g):
            for part, block in enumerate(BLOCKS):
                here = pl.ds(part * span, span)
                both = [
                    o_ref[pl.ds((2 * block + a) * span, span), :].astype(jnp.bfloat16)
                    for a in range(2)
                ]
                mixed_ref[here, 2 * g * HD : (2 * g + 2) * HD] = jnp.concatenate(both, axis=1)


def attend_forward(raw, cos, sin):
    rows, width = raw.shape
    groups = width // (4 * HD)
    span = rows // 4
    whole = lambda shape: pl.BlockSpec(shape, lambda g: (0,) * len(shape))
    each = lambda shape: pl.BlockSpec((1,) + shape, lambda g: (g,) + (0,) * len(shape))
    return pl.pallas_call(
        forward_kernel,
        grid=(groups,),
        in_specs=[whole(raw.shape), whole(cos.shape), whole(sin.shape)],
        out_specs=[
            whole((rows, 2 * groups * HD)),
            each((2 * rows, HD)),
            each((rows, HD)),
            each((rows, HD)),
            each((4, 2 * span)),
        ],
        out_shape=[
            jax.ShapeDtypeStruct((rows, 2 * groups * HD), jnp.bfloat16),
            jax.ShapeDtypeStruct((groups, 2 * rows, HD), jnp.bfloat16),
            jax.ShapeDtypeStruct((groups, rows, HD), jnp.bfloat16),
            jax.ShapeDtypeStruct((groups, rows, HD), jnp.bfloat16),
            jax.ShapeDtypeStruct((groups, 4, 2 * span), jnp.float32),
        ],
        scratch_shapes=[pltpu.VMEM((2 * rows, HD), jnp.float32)],
        compiler_params=pltpu.CompilerParams(vmem_limit_bytes=48 * 1024 * 1024),
        cost_estimate=pl.CostEstimate(
            flops=20 * 10**9, bytes_accessed=15 * 10**6, transcendentals=6 * 10**6
        ),
        name="attention_forward",
    )(raw, cos, sin)


def backward_kernel(
    q_ref, k_ref, v_ref, lse_ref, grad_ref, cos_ref, sin_ref, out_ref, do_ref, dq_ref, dk_ref, dv_ref
):
    heads = pl.program_id(0)
    rows = k_ref.shape[1]
    span = rows // 4
    count = grad_ref.shape[1] // (2 * HD)
    for g in range(count):

        @pl.when(heads == g)
        def _(g=g):
            for part, block in enumerate(BLOCKS):
                here = pl.ds(part * span, span)
                for a in range(2):
                    at = (2 * g + a) * HD
                    do_ref[pl.ds((2 * block + a) * span, span), :] = grad_ref[
                        here, at : at + HD
                    ]

    key_t = k_ref[0].astype(jnp.float32).T.astype(jnp.bfloat16)
    for block in reversed(range(4)):
        top, end = block * span, (block + 1) * span
        at = pl.ds(2 * block * span, 2 * span)
        queries, grads = q_ref[0, at, :], do_ref[at, :]
        scores = masked(nt(k_ref[0, :end, :], queries) * SCALE, top)
        probs = jnp.exp(scores - lse_ref[0, block : block + 1, :])
        grad_probs = nt(v_ref[0, :end, :], grads)
        weighted = probs * grad_probs
        delta = jnp.sum(weighted, axis=0, keepdims=True)
        grad_scores = (probs * (grad_probs - delta)).astype(jnp.bfloat16)
        dv = nn(probs.astype(jnp.bfloat16), grads)
        dk = nn(grad_scores, queries)
        if block == 3:
            dv_ref[...] = dv
            dk_ref[...] = dk
        else:
            dv_ref[:end, :] += dv
            dk_ref[:end, :] += dk
        dq_ref[at, :] = nn(key_t[:, :end], grad_scores).T

    def low(value):
        return value.astype(jnp.bfloat16).astype(jnp.float32)

    for g in range(count):

        @pl.when(heads == g)
        def _(g=g):
            for part, block in enumerate(BLOCKS):
                here = pl.ds(part * span, span)
                there = pl.ds(block * span, span)
                cos, sin = cos_ref[here, :], -sin_ref[here, :]
                both = [
                    rope(low(dq_ref[pl.ds((2 * block + a) * span, span), :] * SCALE), cos, sin)
                    for a in range(2)
                ]
                out_ref[here, 2 * g * HD : (2 * g + 2) * HD] = jnp.concatenate(
                    both, axis=1
                ).astype(jnp.bfloat16)
                at = (2 * count + g) * HD
                out_ref[here, at : at + HD] = rope(
                    low(dk_ref[there, :] * SCALE), cos, sin
                ).astype(jnp.bfloat16)
                at = (3 * count + g) * HD
                out_ref[here, at : at + HD] = dv_ref[there, :].astype(jnp.bfloat16)


def attend_backward(q, k, v, lse, grad_mixed, cos, sin):
    groups, rows, _ = k.shape
    span = rows // 4
    whole = lambda shape: pl.BlockSpec(shape, lambda g: (0,) * len(shape))
    each = lambda shape: pl.BlockSpec((1,) + shape, lambda g: (g,) + (0,) * len(shape))
    return pl.pallas_call(
        backward_kernel,
        grid=(groups,),
        in_specs=[
            each((2 * rows, HD)),
            each((rows, HD)),
            each((rows, HD)),
            each((4, 2 * span)),
            whole(grad_mixed.shape),
            whole(cos.shape),
            whole(sin.shape),
        ],
        out_specs=whole((rows, 4 * groups * HD)),
        out_shape=jax.ShapeDtypeStruct((rows, 4 * groups * HD), jnp.bfloat16),
        scratch_shapes=[
            pltpu.VMEM((2 * rows, HD), jnp.bfloat16),
            pltpu.VMEM((2 * rows, HD), jnp.float32),
            pltpu.VMEM((rows, HD), jnp.float32),
            pltpu.VMEM((rows, HD), jnp.float32),
        ],
        compiler_params=pltpu.CompilerParams(vmem_limit_bytes=48 * 1024 * 1024),
        cost_estimate=pl.CostEstimate(
            flops=40 * 10**9, bytes_accessed=15 * 10**6, transcendentals=6 * 10**6
        ),
        name="attention_backward",
    )(q, k, v, lse, grad_mixed, cos, sin)


def other_core(value):
    return lax.ppermute(value, "seq", CORE_SWAP)


def other_y(value):
    return lax.ppermute(value, "seq", Y_SWAP)


def tie(value, *after):
    flat = value.reshape(-1, value.shape[-1])
    spec = pl.BlockSpec(memory_space=pltpu.HBM)
    tied = pl.pallas_call(
        lambda *refs: None,
        in_specs=[spec] * (1 + len(after)),
        out_specs=spec,
        out_shape=jax.ShapeDtypeStruct(flat.shape, flat.dtype),
        input_output_aliases={0: 0},
        name="tie",
    )(flat, *after)
    return tied.reshape(value.shape)


def gather_dp(piece):
    return lax.all_gather(piece, "dp", axis=0, tiled=True)


def dp_bits():
    count = lax.axis_size("dp").bit_length() - 1
    return [0] + list(range(count - 1, 0, -1))


def dp_swap(value, bit):
    size = lax.axis_size("dp")
    return lax.ppermute(value, "dp", [(d, d ^ (1 << bit)) for d in range(size)])


def by_bits(full):
    size = lax.axis_size("dp")
    count = size.bit_length() - 1
    return full.reshape((2,) * count + (full.shape[0] // size,) + full.shape[1:])


def halve(value, bit, left):
    axis = sorted(left, reverse=True).index(bit)
    own = (lax.axis_index("dp") >> bit) & 1
    kept = lax.dynamic_index_in_dim(value, own, axis, keepdims=False)
    sent = lax.dynamic_index_in_dim(value, 1 - own, axis, keepdims=False)
    return kept + dp_swap(sent, bit)


def halve_tied(value, bit, left, before):
    axis = sorted(left, reverse=True).index(bit)
    own = (lax.axis_index("dp") >> bit) & 1
    kept = lax.dynamic_index_in_dim(value, own, axis, keepdims=False)
    sent = lax.dynamic_index_in_dim(value, 1 - own, axis, keepdims=False)
    if before is not None:
        sent = tie(sent, before)
    got = dp_swap(sent, bit)
    return kept + got, got


def halve_all(value, order):
    for step, bit in enumerate(order):
        value = halve(value, bit, order[step:])
    return value


def scatter_dp(full):
    order = dp_bits()
    return halve_all(by_bits(full), order)


def double_dp(piece):
    order = dp_bits()[::-1]
    value = piece
    done = []
    for bit in order:
        got = dp_swap(value, bit)
        done.append(bit)
        axis = sorted(done, reverse=True).index(bit)
        own = (lax.axis_index("dp") >> bit) & 1
        value = pair(own, jnp.expand_dims(value, axis), jnp.expand_dims(got, axis), axis)
    return value.reshape((-1,) + piece.shape[1:])


def dot(left, right):
    return jnp.dot(left, right, preferred_element_type=jnp.float32)


def dot_t(left, right):
    return lax.dot_general(
        left, right, (((1,), (1,)), ((), ())), preferred_element_type=jnp.float32
    )


def tdot(left, right):
    out = lax.dot_general(
        left, right, (((0,), (0,)), ((), ())), preferred_element_type=jnp.float32
    ).astype(jnp.bfloat16)
    return layout.with_layout_constraint(out, layout.Layout(major_to_minor=(0, 1)))


def pair(flag, mine, other, axis=0):
    return jnp.where(
        flag == 0,
        jnp.concatenate([mine, other], axis=axis),
        jnp.concatenate([other, mine], axis=axis),
    )


def norm_rows(stream, gain):
    inverse = lax.rsqrt(jnp.mean(stream * stream, axis=-1, keepdims=True) + EPSILON)
    normed = stream * inverse
    return (normed, inverse, (normed * gain).astype(jnp.bfloat16))


def norm_back(grad_out, normed, inverse, gain):
    gain_grad = jnp.sum(grad_out * normed, axis=0)
    scaled = grad_out * gain
    grad_in = inverse * (scaled - normed * jnp.mean(scaled * normed, axis=-1, keepdims=True))
    return (grad_in, gain_grad)


def spread_kernel(part, *refs):
    ins, outs = refs[:-2], refs[-2:]
    layers = len(ins) // 2
    for layer in range(layers):

        @pl.when(pl.program_id(0) == layer)
        def _(pieces=(ins[layer], ins[layers + layer])):
            for piece, out in zip(pieces, outs):
                width = piece.shape[1] // 4
                for quarter in range(4):
                    for at in range(0, width, part):
                        to = 4 * at + quarter * part
                        start = quarter * width + at
                        out[0, :, to : to + part] = piece[:, start : start + part].astype(
                            jnp.float32
                        )


def spread_quarters(gates, ups, part):
    layers = len(gates)
    rows, width = gates[0].shape
    out = jax.ShapeDtypeStruct((layers, rows, width), jnp.float32)
    spec = pl.BlockSpec((1, rows, width), lambda layer: (layer, 0, 0))
    return pl.pallas_call(
        functools.partial(spread_kernel, part),
        grid=(layers,),
        in_specs=[pl.BlockSpec((rows, width), lambda layer: (0, 0))] * (2 * layers),
        out_specs=[spec, spec],
        out_shape=[out, out],
        compiler_params=pltpu.CompilerParams(vmem_limit_bytes=48 * 1024 * 1024),
        name="spread_quarters",
    )(*gates, *ups)


def body(
    tokens, cotangent, attn_norm, w_query, w_key, w_value, w_out, mlp_norm, w_gate, w_up, w_down
):
    dp_size = lax.axis_size("dp")
    index = lax.axis_index("seq")
    core = index % 2
    side = index // 2
    _, span, features = tokens.shape
    layers = w_query.shape[0]
    rows = w_query.shape[1]
    q_half = w_query.shape[2] // 2
    k_half = w_key.shape[2] // 2
    ff = w_gate.shape[2]
    part = ff // (4 * dp_size)
    ff_quarter = ff // 4
    out_half = features // 2
    heads = q_half // HD
    kv_heads = k_half // HD
    mine_rows = 2 * span
    length = 4 * span

    def regroup(*blocks):
        kept = [lax.dynamic_index_in_dim(block, side, 0, keepdims=False) for block in blocks]
        sent = [lax.dynamic_index_in_dim(block, 1 - side, 0, keepdims=False) for block in blocks]
        got = other_y(jnp.stack(sent))
        return [pair(side, mine, other) for mine, other in zip(kept, got)], got

    def ungroup(*blocks):
        halves = [block.reshape(2, span, features) for block in blocks]
        kept = [lax.dynamic_index_in_dim(half, side, 0, keepdims=False) for half in halves]
        sent = [lax.dynamic_index_in_dim(half, 1 - side, 0, keepdims=False) for half in halves]
        got = other_y(jnp.stack(sent).astype(jnp.bfloat16))
        return [
            pair(side, mine[None], other[None].astype(mine.dtype))
            for mine, other in zip(kept, got)
        ]

    def both_cores(value):
        return pair(core, value, other_core(value))

    def own_rows(total):
        kept = lax.dynamic_slice_in_dim(total, core * mine_rows, mine_rows, 0)
        sent = lax.dynamic_slice_in_dim(total, (1 - core) * mine_rows, mine_rows, 0)
        got = other_core(sent.astype(jnp.bfloat16))
        return kept + got.astype(jnp.float32)

    block_order = jnp.array([0, 2, 1, 3], jnp.int32)
    positions = (block_order[:, None] * span + jnp.arange(span)[None, :]).reshape(-1)
    middle = HD // 2
    frequency = ROPE_BASE ** (-jnp.arange(middle, dtype=jnp.float32) / middle)
    angles = positions.astype(jnp.float32)[:, None] * frequency[None, :]
    cosine = jnp.tile(jnp.cos(angles), (1, 2))
    sine = jnp.concatenate([-jnp.sin(angles), jnp.sin(angles)], axis=1)

    qkv_width = q_half + 2 * k_half
    gain_cols = jnp.pad(
        jnp.stack([attn_norm, mlp_norm]).reshape(2 * layers, rows).T,
        ((0, 0), (0, 128 - 2 * layers)),
    )

    def gather_layer(layer, before):
        local = [
            lax.dynamic_slice_in_dim(w_query[layer], core * q_half, q_half, 1),
            lax.dynamic_slice_in_dim(w_key[layer], core * k_half, k_half, 1),
            lax.dynamic_slice_in_dim(w_value[layer], core * k_half, k_half, 1),
            lax.dynamic_slice_in_dim(w_out[layer], core * out_half, out_half, 1),
        ]
        if layer == 0:
            local.append(gain_cols)

        def quarter(weight):
            cut = weight.reshape(rows, dp_size, 4, part)
            return lax.dynamic_index_in_dim(cut, index, 2, keepdims=False).reshape(rows, ff_quarter)

        local = jnp.concatenate(local, axis=1).reshape(2, rows // 2, -1)
        local = lax.dynamic_index_in_dim(local, side, 0, keepdims=False)
        near = gather_dp(local).reshape(dp_size, 1, rows // 2, -1)
        attention = pair(side, near, other_y(near), axis=1).reshape(features, -1)
        gate_up = jnp.concatenate([quarter(w_gate[layer]), quarter(w_up[layer])], axis=1)
        gate_up = gather_dp(gate_up if before is None else tie(gate_up, before))
        far_gate = other_y(gate_up[:, :ff_quarter])
        far_up = other_y(tie(gate_up[:, ff_quarter:], far_gate))
        qkv = attention[:, :qkv_width]
        out_cols = attention[:, qkv_width : qkv_width + out_half]
        kept = lax.dynamic_slice_in_dim(out_cols, core * q_half, q_half, 0)
        sent = lax.dynamic_slice_in_dim(out_cols, (1 - core) * q_half, q_half, 0)
        out = pair(core, kept, other_core(sent), axis=1)
        both = jnp.concatenate(
            [
                lax.dynamic_slice_in_dim(w_down[layer], index * part, part, 0),
                lax.dynamic_slice_in_dim(w_down[layer], (index ^ 2) * part, part, 0),
            ],
            axis=1,
        )
        both = gather_dp(both)
        down, far_down = both[:, :features], both[:, features:]
        weights = (qkv, out, (((gate_up,), down), ((far_gate, far_up), far_down)))
        return weights, attention[:, qkv_width + out_half :]

    def forward(stream, weights, gain_one, gain_two, ahead):
        qkv_w, out_w, mlp_w = weights
        normed_one, inverse_one, input_one = norm_rows(stream, gain_one)
        full_one = both_cores(input_one)
        if not ahead:
            full_one = tie(full_one, mlp_w[1][0][1])
        raw = dot(full_one, qkv_w)
        mixed, *attended = attend_forward(raw, cosine, sine)
        if ahead:
            mixed = tie(mixed, mlp_w[1][0][0])
        stream_two = stream + own_rows(dot(mixed, out_w))
        normed_two, inverse_two, input_two = norm_rows(stream_two, gain_two)
        full_two = both_cores(input_two)
        total = None
        kept_mlp = []
        for gate_up_w, down_w in mlp_w:
            if total is not None and ahead:
                full_two = tie(full_two, ahead[0])
            gate_up = [dot(full_two, weight) for weight in gate_up_w]
            if len(gate_up) == 1:
                gate_up = gate_up[0][:, :ff_quarter], gate_up[0][:, ff_quarter:]
            gate, up = gate_up
            hidden = (jax.nn.silu(gate) * up).astype(jnp.bfloat16)
            if total is not None and ahead:
                hidden = tie(hidden, ahead[1])
            term = dot(hidden, down_w)
            total = term if total is None else total + term
            kept_mlp.append((gate, up, hidden))
        result = stream_two + own_rows(total)
        saved = (
            normed_one,
            inverse_one,
            full_one,
            attended,
            mixed,
            normed_two,
            inverse_two,
            full_two,
            kept_mlp,
        )
        return result, saved

    def backward(grad, saved, weights, gain_one, gain_two):
        (
            normed_one,
            inverse_one,
            full_one,
            attended,
            mixed,
            normed_two,
            inverse_two,
            full_two,
            kept_mlp,
        ) = saved
        qkv_w, out_w, mlp_w = weights
        grad_full = both_cores(grad.astype(jnp.bfloat16))
        total = None
        down_grads = []
        gate_up_grads = []
        for (gate_up_w, down_w), (gate, up, hidden) in zip(mlp_w[::-1], kept_mlp[::-1]):
            down_grads.append(tdot(hidden, grad_full))
            grad_hidden = dot_t(grad_full, down_w)
            sig = jax.nn.sigmoid(gate)
            grad_gate = grad_hidden * up * sig * (1.0 + gate * (1.0 - sig))
            grad_up = grad_hidden * gate * sig
            grad_gate_up = jnp.concatenate([grad_gate, grad_up], axis=1).astype(jnp.bfloat16)
            gate_up_grads.append(tdot(full_two, grad_gate_up))
            if len(gate_up_w) == 1:
                terms = [dot_t(grad_gate_up, gate_up_w[0])]
            else:
                terms = [
                    dot_t(grad_gate_up[:, :ff_quarter], gate_up_w[0]),
                    dot_t(grad_gate_up[:, ff_quarter:], gate_up_w[1]),
                ]
            for term in terms:
                total = term if total is None else total + term
        mlp_grads = (gate_up_grads[::-1], down_grads[::-1])
        grad_two = own_rows(total)
        norm_two_in, gain_two_g = norm_back(grad_two, normed_two, inverse_two, gain_two)
        grad_mid = grad + norm_two_in
        mid_full = both_cores(grad_mid.astype(jnp.bfloat16))
        grad_out_w = tdot(mixed, mid_full)
        grad_mixed = dot_t(mid_full, out_w).astype(jnp.bfloat16)
        grad_qkv = attend_backward(*attended, grad_mixed, cosine, sine)
        grad_qkv_w = tdot(full_one, grad_qkv)
        grad_one = own_rows(dot_t(grad_qkv, qkv_w))
        norm_one_in, gain_one_g = norm_back(grad_one, normed_one, inverse_one, gain_one)
        points = (total, grad_qkv, grad_one, grad_full)
        parts = (mlp_grads, grad_out_w, grad_qkv_w, gain_one_g, gain_two_g)
        return grad_mid + norm_one_in, parts, points

    def finish(quarters, sums):
        joint = jnp.concatenate(quarters + sums, axis=1)
        got = other_y(joint)
        at = 0
        both = []
        for piece in quarters:
            width = piece.shape[1]
            both.append(pair(side, piece, got[:, at : at + width], axis=1))
            at += width
        if sums:
            added = joint[:, at:].astype(jnp.float32) + got[:, at:].astype(jnp.float32)
            both.append(added.astype(jnp.bfloat16))
        joint = jnp.concatenate(both, axis=1)
        got = other_core(joint)
        at = 0
        out = []
        for piece in quarters:
            width = 2 * piece.shape[1]
            cut = [v[:, at : at + width].reshape(-1, 2, 1, width // 2) for v in (joint, got)]
            out.append(pair(core, *cut, axis=2).reshape(-1, 2 * width))
            at += width
        for piece in sums:
            width = piece.shape[1]
            out.append(pair(core, joint[:, at : at + width], got[:, at : at + width], axis=1))
            at += width
        return out

    def finish_down(piece):
        (down,) = finish([piece], [])
        return (
            down.reshape(part, 4, features)
            .transpose(1, 0, 2)
            .reshape(4 * part, features)
            .astype(jnp.float32)
        )

    def cut_qkv(piece):
        halves = piece.reshape(piece.shape[0], 2, -1)
        at = 0
        cut = []
        for size in (q_half, k_half, k_half, halves.shape[2] - qkv_width):
            cut.append(halves[:, :, at : at + size].reshape(piece.shape[0], -1))
            at += size
        return cut

    def reduce_last(grads, out_grad, qkv_grad, points):
        after_mlp, after_attention, after_all, _ = points
        (mine_gu, far_gu), (mine_down, far_down) = grads
        order = dp_bits()

        def first(value, before):
            return halve_tied(by_bits(value), order[0], order, before)

        def rest(value, before):
            value, came = halve_tied(value, order[1], order[1:], before)
            for step in range(2, len(order)):
                value = halve(value, order[step], order[step:])
            return value, came

        got = other_y(far_down)
        down = mine_down + tie(got, after_mlp)
        got = other_y(tie(far_gu[:, :ff_quarter], got))
        gate = mine_gu[:, :ff_quarter] + tie(got, after_attention)
        got = other_y(tie(far_gu[:, ff_quarter:], got))
        up = mine_gu[:, ff_quarter:] + tie(got, after_all)
        down, came = first(down, None)
        out, came = first(out_grad, came)
        gate, came = first(gate, came)
        qkv, came = first(qkv_grad, came)
        up, came = first(up, came)
        down, came = rest(down, None)
        out, came = rest(out, came)
        gate, came = rest(gate, came)
        qkv, came = rest(qkv, came)
        up, came = rest(up, came)
        down = finish_down(down)
        gate, out, qkv = finish([gate], [out, qkv])
        (up,) = finish([up], [])
        return gate, up, down, out, cut_qkv(qkv)

    def reduce_first(grads, out_grad, qkv_grad, after):
        (mine_gu, far_gu), (mine_down, far_down) = grads
        width = mine_down.shape[1]
        piece = lax.psum_scatter(
            jnp.concatenate([mine_down, far_down], axis=1), "dp", scatter_dimension=0, tiled=True
        )
        down = piece[:, :width].astype(jnp.float32) + other_y(piece[:, width:]).astype(
            jnp.float32
        )
        gate_up = mine_gu + tie(other_y(far_gu), after)
        joint = jnp.concatenate([gate_up, out_grad, qkv_grad], axis=1)
        piece = lax.psum_scatter(joint, "dp", scatter_dimension=0, tiled=True)
        at = gate_up.shape[1]
        gate, up, out, qkv = finish(
            [piece[:, :ff_quarter], piece[:, ff_quarter:at]],
            [piece[:, at : at + out_half], piece[:, at + out_half :]],
        )
        return gate, up, finish_down(down.astype(jnp.bfloat16)), out, cut_qkv(qkv)

    def columns_of_core(grad):
        kept = lax.dynamic_slice_in_dim(grad, core * out_half, out_half, 1)
        sent = lax.dynamic_slice_in_dim(grad, (1 - core) * out_half, out_half, 1)
        return pair(core, kept, other_core(sent), axis=0)

    (stream, grad), came = regroup(tokens, cotangent)
    came = came.reshape(-1, features)
    gathered = [gather_layer(layer, came if layer == 0 else None) for layer in range(layers)]
    all_weights = [weights for weights, _ in gathered]
    gains = gathered[0][1][:, : 2 * layers].T.astype(jnp.float32)
    gains = gains.reshape(2, layers, features)
    stream, grad = stream.astype(jnp.float32), grad.astype(jnp.float32)
    all_saved = []
    for layer in range(layers):
        ahead = ()
        if layer + 1 < layers:
            near, far = all_weights[layer + 1][2]
            ahead = (near[0][0], far[0][0])
        stream, saved = forward(stream, all_weights[layer], gains[0, layer], gains[1, layer], ahead)
        all_saved.append(saved)
    reduced = [None] * layers
    gain_grads = []
    pending = []
    for layer in reversed(range(layers)):
        grad, (mlp_g, out_g, qkv_g, one_g, two_g), points = backward(
            grad, all_saved[layer], all_weights[layer], gains[0, layer], gains[1, layer]
        )
        gain_grads = [one_g, two_g] + gain_grads
        if layer == 0:
            extra = jnp.stack(gain_grads, axis=1)
            extra = jnp.pad(extra, ((0, 0), (0, 128 - extra.shape[1])))
            qkv_g = jnp.concatenate([qkv_g, extra.astype(jnp.bfloat16)], axis=1)
        pending.append((mlp_g, columns_of_core(out_g), qkv_g))
    *firsts, last = pending
    for layer, parts in zip(range(layers - 1, 0, -1), firsts):
        reduced[layer] = reduce_first(*parts, points[3])
    reduced[0] = reduce_last(*last, points)
    output, d_tokens = ungroup(stream, grad)
    output = output.astype(jnp.bfloat16)
    gain_out = reduced[0][4][3].reshape(rows, 2, -1)[:, :, : 2 * layers].astype(jnp.float32)
    gain_out = (gain_out[:, 0] + gain_out[:, 1]).T.reshape(layers, 2, rows)

    def stacked(pick):
        return jnp.stack([pick(reduced[layer]).astype(jnp.float32) for layer in range(layers)])

    return (
        output,
        d_tokens,
        gain_out[:, 0],
        stacked(lambda r: r[4][0]),
        stacked(lambda r: r[4][1]),
        stacked(lambda r: r[4][2]),
        stacked(lambda r: r[3]),
        gain_out[:, 1],
        *spread_quarters([r[0] for r in reduced], [r[1] for r in reduced], part),
        stacked(lambda r: r[2]),
    )


def solution(mesh):
    in_specs = (
        P("dp", "seq", None),
        P("dp", "seq", None),
        P(None, "dp"),
        P(None, "dp", None),
        P(None, "dp", None),
        P(None, "dp", None),
        P(None, "dp", None),
        P(None, "dp"),
        P(None, "dp", None),
        P(None, "dp", None),
        P(None, "dp", None),
    )
    return jax.shard_map(
        body, mesh=mesh, in_specs=in_specs, out_specs=in_specs, check_vma=False
    )
```

time: 1890 us -> 1540 us (0.81)
  waiting for transfers between devices: 878 us -> 612 us
  matrix products: 497 us -> 332 us
  Pallas kernels: 0 us -> 118 us
  other arithmetic: 204 us -> 169 us
  blocking collectives: 27.1 us -> 0 us
    ppermute x20 -> x18, waiting for transfers between devices: 659 us -> 279 us  [other_y(): return lax.ppermute(value, 'seq', Y_SWAP)]
    dot_general x12 -> x0, matrix products: 186 us -> none  [the longest x2 49.9 us: attend_backward(): jnp.einsum('qgah,kgh->gaqk', grad_out, values, preferred_element_type=jnp...]
    ppermute x0 -> x15, waiting for transfers between devices: none -> 169 us  [dp_swap(): return lax.ppermute(value, 'dp', [(d, d ^ 1 << bit) for d in range(size)])]
    pallas_call x0 -> x26, Pallas kernels: none -> 118 us  [the longest x2 60.2 us: attend_forward(): pl.pallas_call(forward_kernel, grid=(groups,), in_specs=[whole(raw.shape)...]
    convert_element_type x9 -> x6, other arithmetic: 66.3 us -> 9.67 us  [the longest x1 3.32 us: body(): output = output.astype(jnp.bfloat16)]
    all_gather x8 -> x6, waiting for transfers between devices: 200 us -> 158 us  [gather_dp(): return lax.all_gather(piece, 'dp', axis=0, tiled=True)]
    reduce_sum x2 -> x0, other arithmetic: 29.1 us -> none  [attend_forward(): totals = jnp.sum(exponent_vals, axis=-1, keepdims=True)]
    all_gather x1 -> x0, blocking collectives: 27.1 us -> none  [gather_dp(): return lax.all_gather(piece, 'dp', axis=0, tiled=True)]
  transfers between devices with their start and end apart: 64 -> 66, of which waited for: 26 -> 26; matrix products, arithmetic and copies ran while one was open for 45% -> 36% of each run, Pallas kernels for 0% -> 7%
where the time goes in v2:
time: 1540 us; the launch traced here: 1530 us
  waiting for transfers between devices  612 us (40%)
  matrix products  332 us (22%)
  local copies, waits for them, and re-layouts  241 us (16%)
  other arithmetic  169 us (11%)
  Pallas kernels  118 us (8%)
  starting transfers between devices  41.9 us (3%)
  between operations  16.7 us (1%)
    ppermute x18, waiting for transfers between devices, other_y(): return lax.ppermute(value, 'seq', Y_SWAP)  279 us
    ppermute x15, waiting for transfers between devices, dp_swap(): return lax.ppermute(value, 'dp', [(d, d ^ 1 << bit) for d in range(size)])  169 us
    all_gather x6, waiting for transfers between devices, gather_dp(): return lax.all_gather(piece, 'dp', axis=0, tiled=True)  158 us
    dot_general x14, matrix products, dot_t(): lax.dot_general(left, right, (((1,), (1,)), ((), ())), preferred_element_...  119 us
    dot_general x14, matrix products, dot(): return jnp.dot(left, right, preferred_element_type=jnp.float32)  112 us
    dot_general x12, matrix products, tdot(): lax.dot_general(left, right, (((0,), (0,)), ((), ())), preferred_element_...  99.9 us
    pallas_call x2, Pallas kernels, attend_forward(): pl.pallas_call(forward_kernel, grid=(groups,), in_specs=[whole(raw.shape)...  60.2 us
    unnamed x334, local copies, waits for them, and re-layouts  58.7 us
  transfers between devices with their start and end apart: 66, of which 26 were waited for; matrix products, arithmetic and copies ran while one was open for 36% of the time, Pallas kernels for 7%

profile of v2, /device:TPU:0, one launch (start us, length us, event | category | flops | bytes accessed | tf_op | source)
XLA Modules:
  0.0 1529.4 jit_solution(16053261901693871525)
XLA Ops:
  49.7 13.3 collective-permute-done
  100.8 72.8 %collective-permute-done.1 = bf16[8,1,96,2432]{3,2,1,0:T(8,128)(2,1)} collective-permute-done((bf16[8,1,96,2432]{3,2,1,0:T(8,128)(2,1)}, bf16[8,1,96,2432]{3,2,1,0:T(8,128)(2,1)}, u32[]{:S(2)}, u32[]{:S(2)}) %collective-permute-start.1) | collective-permute-done | bytes 3735584 | tf_op jit(solution)/shard_map/ppermute | solution.py:246
  204.9 12.1 fusion.19.raw_ref
  217.0 30.1 %attention_forward.2 = (bf16[1024,768]{1,0:T(8,128)(2,1)S(1)}, bf16[4,2048,96]{2,1,0:T(8,128)(2,1)}, bf16[4,1024,96]{2,1,0:T(8,128)(2,1)S(1)}, bf16[4,1024,96]{2,1,0:T(8,128)(2,1)S(1)}, f32[4,4,512]{2,1,0:T(4,128)S(1)}) custom-call(f32[1024,1536]{1,0:T(8,128)} %fusion.19.raw_ref, f32[1024,96]{1,0:T(8,128)S(1)} %copy.283.cos_ref, ...), custom_call_target="tpu_custom_call" | custom-call | flops 20000000000 | bytes 15000000 | tf_op jit(solution)/shard_map/attention_forward/pallas_call | solution.py:115
  250.3 17.6 %collective-permute-done.3.refs_1_ = bf16[1536,1024]{1,0:T(8,128)(2,1)} collective-permute-done((bf16[1536,1024]{1,0:T(8,128)(2,1)}, bf16[1536,1024]{1,0:T(8,128)(2,1)}, u32[]{:S(2)}, u32[]{:S(2)}) %collective-permute-start.3) | collective-permute-done | bytes 3145760 | tf_op jit(solution)/shard_map/ppermute | solution.py:246
  288.4 69.5 %all-gather.13.cloned.1.call-done.refs_1_ = bf16[1536,2048]{1,0:T(8,128)(2,1)} async-done(((bf16[192,2048]{1,0:T(8,128)(2,1)}), bf16[1536,2048]{1,0:T(8,128)(2,1)}) %all-gather.13.cloned.1.call-update) | async-done | bytes 6291472 | tf_op jit(solution)/shard_map/all_gather | solution.py:264
  383.9 73.3 %all-gather.11.cloned.1.call-done = bf16[1024,3072]{1,0:T(8,128)(2,1)} async-done(((bf16[128,3072]{1,0:T(8,128)(2,1)}), bf16[1024,3072]{1,0:T(8,128)(2,1)}) %all-gather.11.cloned.1.call-update) | async-done | bytes 6291472 | tf_op jit(solution)/shard_map/all_gather | solution.py:264
  469.9 31.3 %collective-permute-done.7 = bf16[1536,1024]{1,0:T(8,128)(2,1)} collective-permute-done((bf16[1536,1024]{1,0:T(8,128)(2,1)}, bf16[1536,1024]{1,0:T(8,128)(2,1)}, u32[]{:S(2)}, u32[]{:S(2)}) %collective-permute-start.7) | collective-permute-done | bytes 3145760 | tf_op jit(solution)/shard_map/ppermute | solution.py:246
  541.4 50.8 %collective-permute-done.11.refs_1_ = bf16[1536,1024]{1,0:T(8,128)(2,1)} collective-permute-done((bf16[1536,1024]{1,0:T(8,128)(2,1)}, bf16[1536,1024]{1,0:T(8,128)(2,1)}, u32[]{:S(2)}, u32[]{:S(2)}) %collective-permute-start.11) | collective-permute-done | bytes 3145760 | tf_op jit(solution)/shard_map/ppermute | solution.py:246
  602.0 30.2 %attention_forward.3 = (bf16[1024,768]{1,0:T(8,128)(2,1)S(1)}, bf16[4,2048,96]{2,1,0:T(8,128)(2,1)}, bf16[4,1024,96]{2,1,0:T(8,128)(2,1)S(1)}, bf16[4,1024,96]{2,1,0:T(8,128)(2,1)S(1)}, f32[4,4,512]{2,1,0:T(4,128)S(1)}) custom-call(f32[1024,1536]{1,0:T(8,128)} %fusion.15.raw_ref, f32[1024,96]{1,0:T(8,128)S(1)} %copy.283.cos_ref, ...), custom_call_target="tpu_custom_call" | custom-call | flops 20000000000 | bytes 15000000 | tf_op jit(solution)/shard_map/attention_forward/pallas_call | solution.py:115
  654.0 14.1 fusion.69
  689.1 12.5 multiply_convert_fusion.8
  740.3 13.3 convolution_convert_fusion.2
  780.8 25.5 %attention_backward.2 = bf16[1024,1536]{1,0:T(8,128)(2,1)} custom-call(bf16[4,2048,96]{2,1,0:T(8,128)(2,1)} %get-tuple-element.25.q_ref, bf16[4,1024,96]{2,1,0:T(8,128)(2,1)S(1)} %get-tuple-element.26.k_ref, bf16[4,1024,96]{2,1,0:T(8,128)(2,1)S(1)} %get-tuple-element.27.v_ref, f32[4,4,512]{2,1,0:T(4,128)S(1)} %get-tuple-element.28.lse_ref, ...), custom_call_target="tpu_custom_call" | custom-call | flops 40000000000 | bytes 15000000 | tf_op jit(solution)/shard_map/attention_backward/pallas_call | solution.py:213
  889.3 11.8 add_add_fusion.refs_1_
  970.6 25.4 %attention_backward.3.refs_1_ = bf16[1024,1536]{1,0:T(8,128)(2,1)} custom-call(bf16[4,2048,96]{2,1,0:T(8,128)(2,1)} %get-tuple-element.29.q_ref, bf16[4,1024,96]{2,1,0:T(8,128)(2,1)S(1)} %copy-done.6, bf16[4,1024,96]{2,1,0:T(8,128)(2,1)S(1)} %copy-done.8, f32[4,4,512]{2,1,0:T(4,128)S(1)} %get-tuple-element.32.lse_ref, ...), custom_call_target="tpu_custom_call" | custom-call | flops 40000000000 | bytes 15000000 | tf_op jit(solution)/shard_map/attention_backward/pallas_call | solution.py:213
  1044.7 32.3 %collective-permute-done.33.refs_0_.refs_1_ = bf16[1536,1024]{1,0:T(8,128)(2,1)} collective-permute-done((bf16[1536,1024]{1,0:T(8,128)(2,1)}, bf16[1536,1024]{1,0:T(8,128)(2,1)}, u32[]{:S(2)}, u32[]{:S(2)}) %collective-permute-start.33) | collective-permute-done | bytes 3145760 | tf_op jit(solution)/shard_map/ppermute | solution.py:246
  1095.3 28.6 %collective-permute-done.30.refs_1_ = bf16[2,128,1536]{2,1,0:T(8,128)(2,1)S(1)} collective-permute-done((bf16[2,128,1536]{2,1,0:T(8,128)(2,1)S(1)}, bf16[2,128,1536]{2,1,0:T(8,128)(2,1)S(1)}, u32[]{:S(2)}, u32[]{:S(2)}) %collective-permute-start.30) | collective-permute-done | bytes 786464 | tf_op jit(solution)/shard_map/ppermute | solution.py:274
  1125.0 23.4 %collective-permute-done.46.refs_0_ = bf16[1536,1024]{1,0:T(8,128)(2,1)} collective-permute-done((bf16[1536,1024]{1,0:T(8,128)(2,1)}, bf16[1536,1024]{1,0:T(8,128)(2,1)}, u32[]{:S(2)}, u32[]{:S(2)}) %collective-permute-start.46) | collective-permute-done | bytes 3145760 | tf_op jit(solution)/shard_map/ppermute | solution.py:246
  1163.3 26.7 %collective-permute-done.52 = bf16[128,1536]{1,0:T(8,128)(2,1)S(1)} collective-permute-done((bf16[128,1536]{1,0:T(8,128)(2,1)S(1)}, bf16[128,1536]{1,0:T(8,128)(2,1)S(1)}, u32[]{:S(2)}, u32[]{:S(2)}) %collective-permute-start.52) | collective-permute-done | bytes 393248 | tf_op jit(solution)/shard_map/ppermute | solution.py:274
  1231.5 21.6 %collective-permute-done.35.refs_1_ = bf16[2,2,192,1664]{3,2,1,0:T(8,128)(2,1)} collective-permute-done((bf16[2,2,192,1664]{3,2,1,0:T(8,128)(2,1)}, bf16[2,2,192,1664]{3,2,1,0:T(8,128)(2,1)}, u32[]{:S(2)}, u32[]{:S(2)}) %collective-permute-start.35) | collective-permute-done | bytes 2555936 | tf_op jit(solution)/shard_map/ppermute | solution.py:274
  1280.4 42.7 %collective-permute-done.37.refs_1_ = bf16[2,192,1664]{2,1,0:T(8,128)(2,1)} collective-permute-done((bf16[2,192,1664]{2,1,0:T(8,128)(2,1)}, bf16[2,192,1664]{2,1,0:T(8,128)(2,1)}, u32[]{:S(2)}, u32[]{:S(2)}) %collective-permute-start.37) | collective-permute-done | bytes 1277984 | tf_op jit(solution)/shard_map/ppermute | solution.py:274
  1330.4 22.2 %collective-permute-done.38 = bf16[192,1664]{1,0:T(8,128)(2,1)} collective-permute-done((bf16[192,1664]{1,0:T(8,128)(2,1)}, bf16[192,1664]{1,0:T(8,128)(2,1)}, u32[]{:S(2)}, u32[]{:S(2)}) %collective-permute-start.38) | collective-permute-done | bytes 639008 | tf_op jit(solution)/shard_map/ppermute | solution.py:274
  1408.5 28.0 %collective-permute-done.44 = bf16[192,4352]{1,0:T(8,128)(2,1)} collective-permute-done((bf16[192,4352]{1,0:T(8,128)(2,1)}, bf16[192,4352]{1,0:T(8,128)(2,1)}, u32[]{:S(2)}, u32[]{:S(2)}) %collective-permute-start.44) | collective-permute-done | bytes 1671200 | tf_op jit(solution)/shard_map/ppermute | solution.py:246
  (755 shorter events, 783.5 us)
Async XLA Ops:
  7.2 84.6 %all-gather.17.cloned.1.call-start = ((), (), s32[]{:S(2)}) async-start(), calls=%async_computation.8 | async-start | bytes 4202496 | tf_op jit(solution)/shard_map/all_gather | solution.py:264
  21.3 170.7 %all-gather.9.cloned.1.call-start = ((), (), s32[]{:S(2)}) async-start(), calls=%async_computation.2 | async-start | bytes 7077888 | tf_op jit(solution)/shard_map/all_gather | solution.py:264
  64.3 222.6 %all-gather.19.cloned.1.call-start = ((), (), s32[]{:S(2)}) async-start(), calls=%async_computation.9 | async-start | bytes 3981312 | tf_op jit(solution)/shard_map/all_gather | solution.py:264
  67.1 290.7 %all-gather.13.cloned.1.call-start = ((), (), s32[]{:S(2)}) async-start(), calls=%async_computation.4 | async-start | bytes 7077888 | tf_op jit(solution)/shard_map/all_gather | solution.py:264
  81.2 375.9 %all-gather.11.cloned.1.call-start = ((), (), s32[]{:S(2)}) async-start(), calls=%async_computation.3 | async-start | bytes 7077888 | tf_op jit(solution)/shard_map/all_gather | solution.py:264
  91.8 81.8 %collective-permute-start.1 = (bf16[8,1,96,2432]{3,2,1,0:T(8,128)(2,1)}, bf16[8,1,96,2432]{3,2,1,0:T(8,128)(2,1)}, u32[]{:S(2)}, u32[]{:S(2)}) collective-permute-start(bf16[8,1,96,2432]{3,2,1,0:T(8,128)(2,1)} %bitcast.277), channel_id=1, source_target_pairs={{0,2},{2,0},{1,3},{3,1},{4,6},{6,4},{5,7},{7,5},{8,10},{10,8},{9,1... | collective-permute-start | bytes 11206664 | tf_op jit(solution)/shard_map/ppermute | solution.py:246
  97.4 547.2 %all-gather.15.cloned.1.call-start = ((), (), s32[]{:S(2)}) async-start(), calls=%async_computation.5 | async-start | bytes 7077888 | tf_op jit(solution)/shard_map/all_gather | solution.py:264
  198.3 69.6 %collective-permute-start.3 = (bf16[1536,1024]{1,0:T(8,128)(2,1)}, bf16[1536,1024]{1,0:T(8,128)(2,1)}, u32[]{:S(2)}, u32[]{:S(2)}) collective-permute-start(bf16[1536,1024]{1,0:T(8,128)(2,1)} %get-tuple-element.77), channel_id=1, source_target_pairs={{0,2},{2,0},{1,3},{3,1},{4,6},{6,4},{5,7},{7,5},{8,10},{10,8},{9,1... | collective-permute-start | bytes 9437192 | tf_op jit(solution)/shard_map/ppermute | solution.py:246
  286.6 79.5 %collective-permute-start.6 = (bf16[512,1536]{1,0:T(8,128)(2,1)S(1)}, bf16[512,1536]{1,0:T(8,128)(2,1)}, u32[]{:S(2)}, u32[]{:S(2)}) collective-permute-start(bf16[512,1536]{1,0:T(8,128)(2,1)S(1)} %multiply_convert_fusion.14), channel_id=1, source_target_pairs={{0,1},{1,0},{2,3},{3,2},{4,5},{5,4},{6,7},{7,6},{8,9},{9,8},{10,11... | collective-permute-start | bytes 4718600 | tf_op jit(solution)/shard_map/ppermute | solution.py:242
  286.8 241.1 %collective-permute-start.12 = (bf16[8,1,96,2304]{3,2,1,0:T(8,128)(2,1)}, bf16[8,1,96,2304]{3,2,1,0:T(8,128)(2,1)}, u32[]{:S(2)}, u32[]{:S(2)}) collective-permute-start(bf16[8,1,96,2304]{3,2,1,0:T(8,128)(2,1)} %bitcast.281), channel_id=1, source_target_pairs={{0,2},{2,0},{1,3},{3,1},{4,6},{6,4},{5,7},{7,5},{8,10},{10,8},{9,1... | collective-permute-start | bytes 10616840 | tf_op jit(solution)/shard_map/ppermute | solution.py:246
  364.1 144.4 %collective-permute-start.8 = (bf16[1536,1024]{1,0:T(8,128)(2,1)}, bf16[1536,1024]{1,0:T(8,128)(2,1)}, u32[]{:S(2)}, u32[]{:S(2)}) collective-permute-start(bf16[1536,1024]{1,0:T(8,128)(2,1)} %get-tuple-element.75), channel_id=1, source_target_pairs={{0,2},{2,0},{1,3},{3,1},{4,6},{6,4},{5,7},{7,5},{8,10},{10,8},{9,1... | collective-permute-start | bytes 9437192 | tf_op jit(solution)/shard_map/ppermute | solution.py:246
  365.6 135.6 %collective-permute-start.7 = (bf16[1536,1024]{1,0:T(8,128)(2,1)}, bf16[1536,1024]{1,0:T(8,128)(2,1)}, u32[]{:S(2)}, u32[]{:S(2)}) collective-permute-start(bf16[1536,1024]{1,0:T(8,128)(2,1)} %tie.24), channel_id=1, source_target_pairs={{0,2},{2,0},{1,3},{3,1},{4,6},{6,4},{5,7},{7,5},{8,10},{10,8},{9,1... | collective-permute-start | bytes 9437192 | tf_op jit(solution)/shard_map/ppermute | solution.py:246
  521.3 673.5 %reduce-scatter.5.cloned.1.call-start = ((), (), s32[]{:S(2)}) async-start(), calls=%async_computation.7 | async-start | bytes 7077888 | tf_op jit(solution)/shard_map/reduce_scatter | solution.py:671
  521.4 70.9 %collective-permute-start.11 = (bf16[1536,1024]{1,0:T(8,128)(2,1)}, bf16[1536,1024]{1,0:T(8,128)(2,1)}, u32[]{:S(2)}, u32[]{:S(2)}) collective-permute-start(bf16[1536,1024]{1,0:T(8,128)(2,1)} %tie.26), channel_id=1, source_target_pairs={{0,2},{2,0},{1,3},{3,1},{4,6},{6,4},{5,7},{7,5},{8,10},{10,8},{9,1... | collective-permute-start | bytes 9437192 | tf_op jit(solution)/shard_map/ppermute | solution.py:246
  539.2 93.0 %collective-permute-start.13 = (bf16[768,768]{1,0:T(8,128)(2,1)}, bf16[768,768]{1,0:T(8,128)(2,1)}, u32[]{:S(2)}, u32[]{:S(2)}) collective-permute-start(bf16[768,768]{1,0:T(8,128)(2,1)} %get-tuple-element.91), channel_id=1, source_target_pairs={{0,1},{1,0},{2,3},{3,2},{4,5},{5,4},{6,7},{7,6},{8,9},{9,8},{10,11... | collective-permute-start | bytes 3538952 | tf_op jit(solution)/shard_map/ppermute | solution.py:242
  739.9 82.2 %collective-permute-start.16 = (bf16[512,1536]{1,0:T(8,128)(2,1)}, bf16[512,1536]{1,0:T(8,128)(2,1)}, u32[]{:S(2)}, u32[]{:S(2)}) collective-permute-start(bf16[512,1536]{1,0:T(8,128)(2,1)} %dynamic-slice_convert_fusion.4), channel_id=1, source_target_pairs={{0,1},{1,0},{2,3},{3,2},{4,5},{5,4},{6,7},{7,6},{8,9},{9,8},{10,11... | collective-permute-start | bytes 4718600 | tf_op jit(solution)/shard_map/ppermute | solution.py:242
  753.6 171.0 %collective-permute-start.42 = (bf16[1536,2048]{1,0:T(8,128)(2,1)}, bf16[1536,2048]{1,0:T(8,128)(2,1)}, u32[]{:S(2)}, u32[]{:S(2)}) collective-permute-start(bf16[1536,2048]{1,0:T(8,128)(2,1)} %convolution_convert_fusion.2), channel_id=1, source_target_pairs={{0,2},{2,0},{1,3},{3,1},{4,6},{6,4},{5,7},{7,5},{8,10},{10,8},{9,1... | collective-permute-start | bytes 18874376 | tf_op jit(solution)/shard_map/ppermute | solution.py:246
  822.1 575.7 %reduce-scatter.3.cloned.1.call-start = ((), (), s32[]{:S(2)}) async-start(), calls=%async_computation.6 | async-start | bytes 15040512 | tf_op jit(solution)/shard_map/reduce_scatter | solution.py:679
  924.0 81.1 %collective-permute-start.27 = (bf16[1024,1536]{1,0:T(8,128)(2,1)}, bf16[1024,1536]{1,0:T(8,128)(2,1)}, u32[]{:S(2)}, u32[]{:S(2)}) collective-permute-start(bf16[1024,1536]{1,0:T(8,128)(2,1)} %convolution_convert_fusion.8), channel_id=1, source_target_pairs={{0,2},{2,0},{1,3},{3,1},{4,6},{6,4},{5,7},{7,5},{8,10},{10,8},{9,1... | collective-permute-start | bytes 9437192 | tf_op jit(solution)/shard_map/ppermute | solution.py:246
  1006.3 70.8 %collective-permute-start.33 = (bf16[1536,1024]{1,0:T(8,128)(2,1)}, bf16[1536,1024]{1,0:T(8,128)(2,1)}, u32[]{:S(2)}, u32[]{:S(2)}) collective-permute-start(bf16[1536,1024]{1,0:T(8,128)(2,1)} %tie.31), channel_id=1, source_target_pairs={{0,2},{2,0},{1,3},{3,1},{4,6},{6,4},{5,7},{7,5},{8,10},{10,8},{9,1... | collective-permute-start | bytes 9437192 | tf_op jit(solution)/shard_map/ppermute | solution.py:246
  1077.0 71.3 %collective-permute-start.46 = (bf16[1536,1024]{1,0:T(8,128)(2,1)}, bf16[1536,1024]{1,0:T(8,128)(2,1)}, u32[]{:S(2)}, u32[]{:S(2)}) collective-permute-start(bf16[1536,1024]{1,0:T(8,128)(2,1)} %tie.38), channel_id=1, source_target_pairs={{0,2},{2,0},{1,3},{3,1},{4,6},{6,4},{5,7},{7,5},{8,10},{10,8},{9,1... | collective-permute-start | bytes 9437192 | tf_op jit(solution)/shard_map/ppermute | solution.py:246
  1083.7 122.4 %collective-permute-start.25 = (bf16[2,256,1536]{2,1,0:T(8,128)(2,1)}, bf16[2,256,1536]{2,1,0:T(8,128)(2,1)}, u32[]{:S(2)}, u32[]{:S(2)}) collective-permute-start(bf16[2,256,1536]{2,1,0:T(8,128)(2,1)} %pad_maximum_fusion.13), channel_id=1, source_target_pairs={{0,2},{2,0},{1,3},{3,1},{4,6},{6,4},{5,7},{7,5},{8,10},{10,8},{9,1... | collective-permute-start | bytes 4718600 | tf_op jit(solution)/shard_map/ppermute | solution.py:246
  1203.8 154.3 %collective-permute-start.54 = (bf16[128,3072]{1,0:T(8,128)(2,1)}, bf16[128,3072]{1,0:T(8,128)(2,1)}, u32[]{:S(2)}, u32[]{:S(2)}) collective-permute-start(bf16[128,3072]{1,0:T(8,128)(2,1)} %maximum_select_fusion.35), channel_id=1, source_target_pairs={{0,1},{1,0},{2,3},{3,2},{4,5},{5,4},{6,7},{7,6},{8,9},{9,8},{10,11... | collective-permute-start | bytes 2359304 | tf_op jit(solution)/shard_map/ppermute | solution.py:242
  1275.9 92.3 %collective-permute-start.57 = (bf16[128,3072]{1,0:T(8,128)(2,1)}, bf16[128,3072]{1,0:T(8,128)(2,1)}, u32[]{:S(2)}, u32[]{:S(2)}) collective-permute-start(bf16[128,3072]{1,0:T(8,128)(2,1)} %maximum_select_fusion.37), channel_id=1, source_target_pairs={{0,1},{1,0},{2,3},{3,2},{4,5},{5,4},{6,7},{7,6},{8,9},{9,8},{10,11... | collective-permute-start | bytes 2359304 | tf_op jit(solution)/shard_map/ppermute | solution.py:242
  (203 other events, 3828.8 us)
Sparse Core Ops, SparseCore 0:
  21.4 70.3 all-gather.16
  94.5 97.4 all-gather.8
  194.2 63.3 all-gather.18
  260.2 97.5 all-gather.12
  359.9 97.1 all-gather.10
  521.4 97.9 all-gather.14
  822.2 115.9 reduce-scatter.4
  950.9 243.1 reduce-scatter.2

commit v3 on v2

--- a/solution.py
+++ b/solution.py
@@ -18,6 +18,9 @@
 
 
 BLOCKS = (0, 2, 1, 3)
+
+
+SMALL = pl.CostEstimate(flops=10**6, bytes_accessed=10**6, transcendentals=0)
 
 
 def nt(left, right):
@@ -132,9 +135,7 @@
         ],
         scratch_shapes=[pltpu.VMEM((2 * rows, HD), jnp.float32)],
         compiler_params=pltpu.CompilerParams(vmem_limit_bytes=48 * 1024 * 1024),
-        cost_estimate=pl.CostEstimate(
-            flops=20 * 10**9, bytes_accessed=15 * 10**6, transcendentals=6 * 10**6
-        ),
+        cost_estimate=SMALL,
         name="attention_forward",
     )(raw, cos, sin)
 
@@ -231,9 +232,7 @@
             pltpu.VMEM((rows, HD), jnp.float32),
         ],
         compiler_params=pltpu.CompilerParams(vmem_limit_bytes=48 * 1024 * 1024),
-        cost_estimate=pl.CostEstimate(
-            flops=40 * 10**9, bytes_accessed=15 * 10**6, transcendentals=6 * 10**6
-        ),
+        cost_estimate=SMALL,
         name="attention_backward",
     )(q, k, v, lse, grad_mixed, cos, sin)
 
@@ -361,38 +360,139 @@
     return (grad_in, gain_grad)
 
 
-def spread_kernel(part, *refs):
-    ins, outs = refs[:-2], refs[-2:]
-    layers = len(ins) // 2
-    for layer in range(layers):
-
-        @pl.when(pl.program_id(0) == layer)
-        def _(pieces=(ins[layer], ins[layers + layer])):
-            for piece, out in zip(pieces, outs):
-                width = piece.shape[1] // 4
-                for quarter in range(4):
-                    for at in range(0, width, part):
-                        to = 4 * at + quarter * part
-                        start = quarter * width + at
-                        out[0, :, to : to + part] = piece[:, start : start + part].astype(
-                            jnp.float32
-                        )
-
-
-def spread_quarters(gates, ups, part):
-    layers = len(gates)
-    rows, width = gates[0].shape
-    out = jax.ShapeDtypeStruct((layers, rows, width), jnp.float32)
-    spec = pl.BlockSpec((1, rows, width), lambda layer: (layer, 0, 0))
+def mlp_back_kernel(*refs):
+    grad_ref, input_t_ref, gate_ref, up_ref, gate_w_ref, up_w_ref, down_w_ref = refs[:7]
+    before = refs[7:-4]
+    total_ref, *out_refs = refs[-4:]
+    step = pl.program_id(0)
+    gate, up = gate_ref[...], up_ref[...]
+    grad_hidden = nt(grad_ref[...], down_w_ref[...])
+    sig = 1.0 / (1.0 + jnp.exp(-gate))
+    swish = gate * sig
+    grad_gate = (grad_hidden * up * (sig + swish * (1.0 - sig))).astype(jnp.bfloat16)
+    grad_up = (grad_hidden * swish).astype(jnp.bfloat16)
+    hidden_t = (swish * up).T.astype(jnp.bfloat16)
+    term = nt(
+        jnp.concatenate([grad_gate, grad_up], axis=1),
+        jnp.concatenate([gate_w_ref[...], up_w_ref[...]], axis=1),
+    )
+
+    @pl.when(step == 0)
+    def _():
+        total_ref[...] = term
+
+    @pl.when(step > 0)
+    def _():
+        total_ref[...] += term
+
+    sums = [
+        nn(input_t_ref[...], grad_gate),
+        nn(input_t_ref[...], grad_up),
+        nn(hidden_t, grad_ref[...]),
+    ]
+    for at, (out, value) in enumerate(zip(out_refs, sums)):
+        if before:
+            value = value + before[at][...].astype(jnp.float32)
+        out[...] = value.astype(jnp.bfloat16)
+
+
+def mlp_back(grad, input_t, gate_up, gate_up_w, down_w, before):
+    tokens, features = grad.shape
+    tile = 256
+    width = down_w.shape[0]
+    steps = width // tile
+
+    def whole(shape):
+        return pl.BlockSpec(shape, lambda t: (0, 0), pipeline_mode=pl.Buffered(1))
+
+    def column(rows, first):
+        return pl.BlockSpec((rows, tile), lambda t: (0, first + t))
+
+    row = pl.BlockSpec((tile, features), lambda t: (t, 0))
+    weight_specs = [column(features, 0), column(features, 0), row]
     return pl.pallas_call(
-        functools.partial(spread_kernel, part),
-        grid=(layers,),
-        in_specs=[pl.BlockSpec((rows, width), lambda layer: (0, 0))] * (2 * layers),
-        out_specs=[spec, spec],
-        out_shape=[out, out],
-        compiler_params=pltpu.CompilerParams(vmem_limit_bytes=48 * 1024 * 1024),
-        name="spread_quarters",
-    )(*gates, *ups)
+        mlp_back_kernel,
+        grid=(steps,),
+        in_specs=[
+            whole(grad.shape),
+            whole(input_t.shape),
+            column(tokens, 0),
+            column(tokens, steps),
+            column(features, 0),
+            column(features, steps),
+            row,
+            *(weight_specs if before else []),
+        ],
+        out_specs=[pl.BlockSpec((tokens, features), lambda t: (0, 0)), *weight_specs],
+        out_shape=[
+            jax.ShapeDtypeStruct((tokens, features), jnp.float32),
+            jax.ShapeDtypeStruct((features, width), jnp.bfloat16),
+            jax.ShapeDtypeStruct((features, width), jnp.bfloat16),
+            jax.ShapeDtypeStruct((width, features), jnp.bfloat16),
+        ],
+        compiler_params=pltpu.CompilerParams(vmem_limit_bytes=60 * 1024 * 1024),
+        cost_estimate=SMALL,
+        name="mlp_backward",
+    )(grad, input_t, gate_up, gate_up, gate_up_w, gate_up_w, down_w, *before)
+
+
+def assemble_kernel(part, cuts, place_ref, *refs):
+    groups = [refs[4 * i : 4 * i + 4] for i in range(len(cuts))]
+    outs = refs[-cuts_outputs(cuts) :]
+    for place in range(4):
+
+        @pl.when(place_ref[0] == place)
+        def _(place=place):
+            for pieces, parts in zip(groups, cuts):
+                by_place = {place ^ swap: ref for swap, ref in zip((0, 2, 1, 3), pieces)}
+                for kind, at, size, out in parts:
+                    here = slice(at, at + size)
+                    if kind == "columns":
+                        for quarter in range(4):
+                            for start in range(0, size, part):
+                                to = 4 * start + quarter * part
+                                value = by_place[quarter][:, at + start : at + start + part]
+                                outs[out][0, :, to : to + part] = value.astype(jnp.float32)
+                    elif kind == "rows":
+                        for quarter in range(4):
+                            value = by_place[quarter][:, here].astype(jnp.float32)
+                            outs[out][0, quarter * part : (quarter + 1) * part, :] = value
+                    else:
+                        halves = [
+                            by_place[half][:, here].astype(jnp.float32)
+                            + by_place[half + 2][:, here].astype(jnp.float32)
+                            for half in range(2)
+                        ]
+                        if kind == "sum":
+                            outs[out][0, :, :] = halves[0] + halves[1]
+                        else:
+                            for half in range(2):
+                                outs[out][0, :, half * size : (half + 1) * size] = halves[half]
+
+
+def cuts_outputs(cuts):
+    return 1 + max(out for parts in cuts for *_, out in parts)
+
+
+def assemble(place, layer, groups, cuts, shapes, part, before):
+    operands = [piece for group in groups for piece in group]
+    in_specs = [pl.BlockSpec(memory_space=pltpu.SMEM)]
+    in_specs += [pl.BlockSpec(piece.shape, lambda i: (0, 0)) for piece in operands]
+    aliases = {}
+    if before is not None:
+        aliases = {1 + len(operands) + i: i for i in range(len(before))}
+        operands += before
+        in_specs += [pl.BlockSpec(memory_space=pl.ANY)] * len(before)
+    return pl.pallas_call(
+        functools.partial(assemble_kernel, part, cuts),
+        grid=(1,),
+        in_specs=in_specs,
+        out_specs=[pl.BlockSpec((1,) + shape[1:], lambda i: (layer, 0, 0)) for shape in shapes],
+        out_shape=[jax.ShapeDtypeStruct(shape, jnp.float32) for shape in shapes],
+        input_output_aliases=aliases,
+        compiler_params=pltpu.CompilerParams(vmem_limit_bytes=60 * 1024 * 1024),
+        name="assemble",
+    )(place, *operands)
 
 
 def body(
@@ -422,15 +522,15 @@
         got = other_y(jnp.stack(sent))
         return [pair(side, mine, other) for mine, other in zip(kept, got)], got
 
-    def ungroup(*blocks):
-        halves = [block.reshape(2, span, features) for block in blocks]
-        kept = [lax.dynamic_index_in_dim(half, side, 0, keepdims=False) for half in halves]
-        sent = [lax.dynamic_index_in_dim(half, 1 - side, 0, keepdims=False) for half in halves]
-        got = other_y(jnp.stack(sent).astype(jnp.bfloat16))
-        return [
-            pair(side, mine[None], other[None].astype(mine.dtype))
-            for mine, other in zip(kept, got)
-        ]
+    def swapped(block):
+        halves = block.reshape(2, span, features)
+        sent = lax.dynamic_index_in_dim(halves, 1 - side, 0, keepdims=False)
+        return other_y(sent.astype(jnp.bfloat16))
+
+    def ungroup(block, got):
+        halves = block.reshape(2, span, features)
+        kept = lax.dynamic_index_in_dim(halves, side, 0, keepdims=False)
+        return pair(side, kept[None], got[None].astype(kept.dtype))
 
     def both_cores(value):
         return pair(core, value, other_core(value))
@@ -455,7 +555,10 @@
         ((0, 0), (0, 128 - 2 * layers)),
     )
 
-    def gather_layer(layer, before):
+    (stream, grad), came = regroup(tokens, cotangent)
+    came = came.reshape(-1, features)
+
+    def attention_half(layer):
         local = [
             lax.dynamic_slice_in_dim(w_query[layer], core * q_half, q_half, 1),
             lax.dynamic_slice_in_dim(w_key[layer], core * k_half, k_half, 1),
@@ -464,65 +567,59 @@
         ]
         if layer == 0:
             local.append(gain_cols)
-
+        local = jnp.concatenate(local, axis=1).reshape(2, rows // 2, -1)
+        local = lax.dynamic_index_in_dim(local, side, 0, keepdims=False)
+        return gather_dp(tie(local, came) if layer else local)
+
+    def gather_layer(layer, near, far, before):
         def quarter(weight):
             cut = weight.reshape(rows, dp_size, 4, part)
             return lax.dynamic_index_in_dim(cut, index, 2, keepdims=False).reshape(rows, ff_quarter)
 
-        local = jnp.concatenate(local, axis=1).reshape(2, rows // 2, -1)
-        local = lax.dynamic_index_in_dim(local, side, 0, keepdims=False)
-        near = gather_dp(local).reshape(dp_size, 1, rows // 2, -1)
-        attention = pair(side, near, other_y(near), axis=1).reshape(features, -1)
+        near, far = (half.reshape(dp_size, 1, rows // 2, -1) for half in (near, far))
+        attention = pair(side, near, far, axis=1).reshape(features, -1)
         gate_up = jnp.concatenate([quarter(w_gate[layer]), quarter(w_up[layer])], axis=1)
         gate_up = gather_dp(gate_up if before is None else tie(gate_up, before))
-        far_gate = other_y(gate_up[:, :ff_quarter])
-        far_up = other_y(tie(gate_up[:, ff_quarter:], far_gate))
         qkv = attention[:, :qkv_width]
         out_cols = attention[:, qkv_width : qkv_width + out_half]
         kept = lax.dynamic_slice_in_dim(out_cols, core * q_half, q_half, 0)
         sent = lax.dynamic_slice_in_dim(out_cols, (1 - core) * q_half, q_half, 0)
         out = pair(core, kept, other_core(sent), axis=1)
-        both = jnp.concatenate(
-            [
-                lax.dynamic_slice_in_dim(w_down[layer], index * part, part, 0),
-                lax.dynamic_slice_in_dim(w_down[layer], (index ^ 2) * part, part, 0),
-            ],
-            axis=1,
-        )
-        both = gather_dp(both)
-        down, far_down = both[:, :features], both[:, features:]
-        weights = (qkv, out, (((gate_up,), down), ((far_gate, far_up), far_down)))
-        return weights, attention[:, qkv_width + out_half :]
-
-    def forward(stream, weights, gain_one, gain_two, ahead):
-        qkv_w, out_w, mlp_w = weights
+        down = gather_dp(lax.dynamic_slice_in_dim(w_down[layer], index * part, part, 0))
+        return (qkv, out, gate_up, down), attention[:, qkv_width + out_half :]
+
+    def forward(stream, weights, gain_one, gain_two, ready):
+        qkv_w, out_w, gate_up_w, down_w = weights
         normed_one, inverse_one, input_one = norm_rows(stream, gain_one)
         full_one = both_cores(input_one)
-        if not ahead:
-            full_one = tie(full_one, mlp_w[1][0][1])
         raw = dot(full_one, qkv_w)
         mixed, *attended = attend_forward(raw, cosine, sine)
-        if ahead:
-            mixed = tie(mixed, mlp_w[1][0][0])
+        mixed = tie(mixed, ready)
         stream_two = stream + own_rows(dot(mixed, out_w))
         normed_two, inverse_two, input_two = norm_rows(stream_two, gain_two)
-        full_two = both_cores(input_two)
-        total = None
-        kept_mlp = []
-        for gate_up_w, down_w in mlp_w:
-            if total is not None and ahead:
-                full_two = tie(full_two, ahead[0])
-            gate_up = [dot(full_two, weight) for weight in gate_up_w]
-            if len(gate_up) == 1:
-                gate_up = gate_up[0][:, :ff_quarter], gate_up[0][:, ff_quarter:]
-            gate, up = gate_up
-            hidden = (jax.nn.silu(gate) * up).astype(jnp.bfloat16)
-            if total is not None and ahead:
-                hidden = tie(hidden, ahead[1])
-            term = dot(hidden, down_w)
-            total = term if total is None else total + term
-            kept_mlp.append((gate, up, hidden))
-        result = stream_two + own_rows(total)
+        def turned(inputs):
+            return layout.with_layout_constraint(
+                inputs.T, layout.Layout(major_to_minor=(0, 1))
+            )
+
+        def hidden_of(gate_up):
+            gate, up = gate_up[:, :ff_quarter], gate_up[:, ff_quarter:]
+            return (jax.nn.silu(gate) * up).astype(jnp.bfloat16)
+
+        far = other_y(input_two)
+        near_in = both_cores(input_two)
+        near_turned = turned(near_in)
+        near_gate_up = dot(near_in, gate_up_w)
+        near_total = dot(hidden_of(near_gate_up), down_w)
+        far_in = both_cores(tie(far, near_gate_up, near_turned))
+        far_gate_up = dot(far_in, gate_up_w)
+        far_total = dot(hidden_of(far_gate_up), down_w)
+        far_rows = own_rows(far_total).astype(jnp.bfloat16)
+        far_turned = turned(far_in)
+        far = tie(other_y(far_rows), far_turned)
+        near = own_rows(tie(near_total, far_total))
+        result = stream_two + (near + far.astype(jnp.float32))
+        kept_mlp = [(near_turned, near_gate_up), (far_turned, far_gate_up)]
         saved = (
             normed_one,
             inverse_one,
@@ -531,12 +628,11 @@
             mixed,
             normed_two,
             inverse_two,
-            full_two,
             kept_mlp,
         )
         return result, saved
 
-    def backward(grad, saved, weights, gain_one, gain_two):
+    def backward(grad, saved, weights, gain_one, gain_two, far, also):
         (
             normed_one,
             inverse_one,
@@ -545,201 +641,191 @@
             mixed,
             normed_two,
             inverse_two,
-            full_two,
             kept_mlp,
         ) = saved
-        qkv_w, out_w, mlp_w = weights
-        grad_full = both_cores(grad.astype(jnp.bfloat16))
-        total = None
-        down_grads = []
-        gate_up_grads = []
-        for (gate_up_w, down_w), (gate, up, hidden) in zip(mlp_w[::-1], kept_mlp[::-1]):
-            down_grads.append(tdot(hidden, grad_full))
-            grad_hidden = dot_t(grad_full, down_w)
-            sig = jax.nn.sigmoid(gate)
-            grad_gate = grad_hidden * up * sig * (1.0 + gate * (1.0 - sig))
-            grad_up = grad_hidden * gate * sig
-            grad_gate_up = jnp.concatenate([grad_gate, grad_up], axis=1).astype(jnp.bfloat16)
-            gate_up_grads.append(tdot(full_two, grad_gate_up))
-            if len(gate_up_w) == 1:
-                terms = [dot_t(grad_gate_up, gate_up_w[0])]
-            else:
-                terms = [
-                    dot_t(grad_gate_up[:, :ff_quarter], gate_up_w[0]),
-                    dot_t(grad_gate_up[:, ff_quarter:], gate_up_w[1]),
-                ]
-            for term in terms:
-                total = term if total is None else total + term
-        mlp_grads = (gate_up_grads[::-1], down_grads[::-1])
-        grad_two = own_rows(total)
+        qkv_w, out_w, gate_up_w, down_w = weights
+        grad_low = grad.astype(jnp.bfloat16)
+        if far is None:
+            far = other_y(grad_low)
+        far, *mlp_grads = mlp_back(both_cores(far), *kept_mlp[1], gate_up_w, down_w, [])
+        far_rows = own_rows(far).astype(jnp.bfloat16)
+        far = other_y(far_rows)
+        near = tie(both_cores(grad_low), far_rows)
+        near, *mlp_grads = mlp_back(near, *kept_mlp[0], gate_up_w, down_w, mlp_grads)
+        grad_two = own_rows(tie(near, far)) + far.astype(jnp.float32)
         norm_two_in, gain_two_g = norm_back(grad_two, normed_two, inverse_two, gain_two)
         grad_mid = grad + norm_two_in
         mid_full = both_cores(grad_mid.astype(jnp.bfloat16))
         grad_out_w = tdot(mixed, mid_full)
         grad_mixed = dot_t(mid_full, out_w).astype(jnp.bfloat16)
+        grad_mixed = tie(grad_mixed, *also) if also else grad_mixed
         grad_qkv = attend_backward(*attended, grad_mixed, cosine, sine)
         grad_qkv_w = tdot(full_one, grad_qkv)
         grad_one = own_rows(dot_t(grad_qkv, qkv_w))
         norm_one_in, gain_one_g = norm_back(grad_one, normed_one, inverse_one, gain_one)
-        points = (total, grad_qkv, grad_one, grad_full)
+        grad = grad_mid + norm_one_in
+        points = (mid_full, grad_qkv, grad_one)
         parts = (mlp_grads, grad_out_w, grad_qkv_w, gain_one_g, gain_two_g)
-        return grad_mid + norm_one_in, parts, points
-
-    def finish(quarters, sums):
-        joint = jnp.concatenate(quarters + sums, axis=1)
-        got = other_y(joint)
-        at = 0
-        both = []
-        for piece in quarters:
-            width = piece.shape[1]
-            both.append(pair(side, piece, got[:, at : at + width], axis=1))
-            at += width
-        if sums:
-            added = joint[:, at:].astype(jnp.float32) + got[:, at:].astype(jnp.float32)
-            both.append(added.astype(jnp.bfloat16))
-        joint = jnp.concatenate(both, axis=1)
-        got = other_core(joint)
-        at = 0
-        out = []
-        for piece in quarters:
-            width = 2 * piece.shape[1]
-            cut = [v[:, at : at + width].reshape(-1, 2, 1, width // 2) for v in (joint, got)]
-            out.append(pair(core, *cut, axis=2).reshape(-1, 2 * width))
-            at += width
-        for piece in sums:
-            width = piece.shape[1]
-            out.append(pair(core, joint[:, at : at + width], got[:, at : at + width], axis=1))
-            at += width
-        return out
-
-    def finish_down(piece):
-        (down,) = finish([piece], [])
-        return (
-            down.reshape(part, 4, features)
-            .transpose(1, 0, 2)
-            .reshape(4 * part, features)
-            .astype(jnp.float32)
-        )
-
-    def cut_qkv(piece):
-        halves = piece.reshape(piece.shape[0], 2, -1)
-        at = 0
-        cut = []
-        for size in (q_half, k_half, k_half, halves.shape[2] - qkv_width):
-            cut.append(halves[:, :, at : at + size].reshape(piece.shape[0], -1))
-            at += size
-        return cut
-
-    def reduce_last(grads, out_grad, qkv_grad, points):
-        after_mlp, after_attention, after_all, _ = points
-        (mine_gu, far_gu), (mine_down, far_down) = grads
+        return grad, parts, points
+
+    def four(piece):
+        got = other_y(piece)
+        return [piece, got, other_core(piece), other_core(got)]
+
+    def reduce_last(grads, out_grad, qkv_grad, points, earlier, grad):
+        _, after_attention, after_all = points
+        gate, up, down = grads
         order = dp_bits()
-
-        def first(value, before):
-            return halve_tied(by_bits(value), order[0], order, before)
-
-        def rest(value, before):
-            value, came = halve_tied(value, order[1], order[1:], before)
+        last = {"x": None, "z": None, "any": after_attention}
+
+        def send(value, step, link):
+            value = by_bits(value) if step == 0 else value
+            left = order[step:]
+            axis = sorted(left, reverse=True).index(left[0])
+            own = (lax.axis_index("dp") >> left[0]) & 1
+            kept = lax.dynamic_index_in_dim(value, own, axis, keepdims=False)
+            sent = lax.dynamic_index_in_dim(value, 1 - own, axis, keepdims=False)
+            if link and last[link] is not None:
+                sent = tie(sent, last[link])
+            got = dp_swap(sent, left[0])
+            if link:
+                last[link] = got
+            return kept, got
+
+        def take(got):
+            got = tie(got, last["any"])
+            last["any"] = got
+            return got
+
+        def add(pending):
+            return pending[0] + take(pending[1])
+
+        def four_taken(piece):
+            got = take(other_y(piece))
+            return [piece, got, other_core(piece), other_core(got)]
+
+        def finish(value):
             for step in range(2, len(order)):
-                value = halve(value, order[step], order[step:])
-            return value, came
-
-        got = other_y(far_down)
-        down = mine_down + tie(got, after_mlp)
-        got = other_y(tie(far_gu[:, :ff_quarter], got))
-        gate = mine_gu[:, :ff_quarter] + tie(got, after_attention)
-        got = other_y(tie(far_gu[:, ff_quarter:], got))
-        up = mine_gu[:, ff_quarter:] + tie(got, after_all)
-        down, came = first(down, None)
-        out, came = first(out_grad, came)
-        gate, came = first(gate, came)
-        qkv, came = first(qkv_grad, came)
-        up, came = first(up, came)
-        down, came = rest(down, None)
-        out, came = rest(out, came)
-        gate, came = rest(gate, came)
-        qkv, came = rest(qkv, came)
-        up, came = rest(up, came)
-        down = finish_down(down)
-        gate, out, qkv = finish([gate], [out, qkv])
-        (up,) = finish([up], [])
-        return gate, up, down, out, cut_qkv(qkv)
-
-    def reduce_first(grads, out_grad, qkv_grad, after):
-        (mine_gu, far_gu), (mine_down, far_down) = grads
-        width = mine_down.shape[1]
-        piece = lax.psum_scatter(
-            jnp.concatenate([mine_down, far_down], axis=1), "dp", scatter_dimension=0, tiled=True
-        )
-        down = piece[:, :width].astype(jnp.float32) + other_y(piece[:, width:]).astype(
-            jnp.float32
-        )
-        gate_up = mine_gu + tie(other_y(far_gu), after)
-        joint = jnp.concatenate([gate_up, out_grad, qkv_grad], axis=1)
+                value = add(send(value, step, None))
+            return value
+
+        gate_up = send(jnp.concatenate([gate, up], axis=1), 0, "x")
+        gate_up = send(add(gate_up), 1, "z")
+        last["x"] = after_attention
+        down = send(down, 0, "x")
+        last["any"] = after_all
+        out = send(out_grad, 0, "x")
+        qkv = send(qkv_grad, 0, "x")
+        down = send(add(down), 1, "z")
+        out = send(add(out), 1, "z")
+        earlier = [[four_taken(piece) for piece in pieces] for pieces in earlier]
+        gate_up = finish(add(gate_up))
+        qkv = send(add(qkv), 1, "z")
+        grad = take(swapped(grad))
+        gate_up = four_taken(gate_up)
+        down = four_taken(finish(add(down)))
+        out = finish(add(out))
+        qkv = finish(add(qkv))
+        joint = jnp.concatenate([out, qkv], axis=1)
+        cuts = [
+            [("columns", 0, ff_quarter, 0), ("columns", ff_quarter, ff_quarter, 1)],
+            attention_cuts(0) + [("sum", joint.shape[1] - 128, 128, 7)],
+            [("rows", 0, features, 2)],
+        ]
+        return ([gate_up, four(joint), down], cuts), earlier, grad
+
+    def attention_cuts(at):
+        sizes = (out_half, q_half, k_half, k_half)
+        firsts = [at + sum(sizes[:i]) for i in range(4)]
+        return [("halves", first, size, 3 + i) for i, (first, size) in enumerate(zip(firsts, sizes))]
+
+    def reduce_first(grads, out_grad, qkv_grad, points):
+        gate, up, down = grads
+        down = lax.psum_scatter(down, "dp", scatter_dimension=0, tiled=True)
+        joint = jnp.concatenate([gate, up, out_grad, qkv_grad], axis=1)
         piece = lax.psum_scatter(joint, "dp", scatter_dimension=0, tiled=True)
-        at = gate_up.shape[1]
-        gate, up, out, qkv = finish(
-            [piece[:, :ff_quarter], piece[:, ff_quarter:at]],
-            [piece[:, at : at + out_half], piece[:, at + out_half :]],
-        )
-        return gate, up, finish_down(down.astype(jnp.bfloat16)), out, cut_qkv(qkv)
+        cuts = [
+            [("columns", 0, ff_quarter, 0), ("columns", ff_quarter, ff_quarter, 1)]
+            + attention_cuts(2 * ff_quarter),
+            [("rows", 0, features, 2)],
+        ]
+        return [piece, down], cuts
 
     def columns_of_core(grad):
         kept = lax.dynamic_slice_in_dim(grad, core * out_half, out_half, 1)
         sent = lax.dynamic_slice_in_dim(grad, (1 - core) * out_half, out_half, 1)
         return pair(core, kept, other_core(sent), axis=0)
 
-    (stream, grad), came = regroup(tokens, cotangent)
-    came = came.reshape(-1, features)
-    gathered = [gather_layer(layer, came if layer == 0 else None) for layer in range(layers)]
+    halves = [attention_half(layer) for layer in range(layers)]
+    swapped_halves = []
+    for half in halves:
+        swapped_halves.append(other_y(tie(half, swapped_halves[-1]) if swapped_halves else half))
+    swapped_halves[0] = tie(swapped_halves[0], *halves[1:])
+    gathered = [
+        gather_layer(layer, halves[layer], swapped_halves[layer], halves[1] if layer == 0 else None)
+        for layer in range(layers)
+    ]
     all_weights = [weights for weights, _ in gathered]
     gains = gathered[0][1][:, : 2 * layers].T.astype(jnp.float32)
     gains = gains.reshape(2, layers, features)
     stream, grad = stream.astype(jnp.float32), grad.astype(jnp.float32)
+    far_cotangent = other_y(grad.astype(jnp.bfloat16))
     all_saved = []
     for layer in range(layers):
-        ahead = ()
-        if layer + 1 < layers:
-            near, far = all_weights[layer + 1][2]
-            ahead = (near[0][0], far[0][0])
-        stream, saved = forward(stream, all_weights[layer], gains[0, layer], gains[1, layer], ahead)
+        ready = far_cotangent if layer == layers - 1 else swapped_halves[layer + 1]
+        stream, saved = forward(
+            stream, all_weights[layer], gains[0, layer], gains[1, layer], ready
+        )
         all_saved.append(saved)
+    also = [swapped(stream)]
+    output = ungroup(stream, also[0]).astype(jnp.bfloat16)
     reduced = [None] * layers
     gain_grads = []
-    pending = []
     for layer in reversed(range(layers)):
         grad, (mlp_g, out_g, qkv_g, one_g, two_g), points = backward(
-            grad, all_saved[layer], all_weights[layer], gains[0, layer], gains[1, layer]
+            grad,
+            all_saved[layer],
+            all_weights[layer],
+            gains[0, layer],
+            gains[1, layer],
+            far_cotangent if layer == layers - 1 else None,
+            also,
         )
         gain_grads = [one_g, two_g] + gain_grads
-        if layer == 0:
+        out_g = columns_of_core(out_g)
+        if layer > 0:
+            reduced[layer] = reduce_first(mlp_g, out_g, qkv_g, points)
+            also = []
+        else:
             extra = jnp.stack(gain_grads, axis=1)
             extra = jnp.pad(extra, ((0, 0), (0, 128 - extra.shape[1])))
             qkv_g = jnp.concatenate([qkv_g, extra.astype(jnp.bfloat16)], axis=1)
-        pending.append((mlp_g, columns_of_core(out_g), qkv_g))
-    *firsts, last = pending
-    for layer, parts in zip(range(layers - 1, 0, -1), firsts):
-        reduced[layer] = reduce_first(*parts, points[3])
-    reduced[0] = reduce_last(*last, points)
-    output, d_tokens = ungroup(stream, grad)
-    output = output.astype(jnp.bfloat16)
-    gain_out = reduced[0][4][3].reshape(rows, 2, -1)[:, :, : 2 * layers].astype(jnp.float32)
-    gain_out = (gain_out[:, 0] + gain_out[:, 1]).T.reshape(layers, 2, rows)
-
-    def stacked(pick):
-        return jnp.stack([pick(reduced[layer]).astype(jnp.float32) for layer in range(layers)])
-
+            earlier = [reduced[at][0] for at in range(1, layers)]
+            reduced[0], earlier, got = reduce_last(mlp_g, out_g, qkv_g, points, earlier, grad)
+    d_tokens = ungroup(grad, got)
+    for layer in range(1, layers):
+        reduced[layer] = earlier[layer - 1], reduced[layer][1]
+    shapes = [(layers, rows, ff)] * 2 + [(layers, 4 * part, features)]
+    shapes += [(layers, rows, 2 * size) for size in (out_half, q_half, k_half, k_half)]
+    place = index.astype(jnp.int32).reshape(1)
+    outs = None
+    for layer in range(layers - 1, 0, -1):
+        outs = assemble(place, layer, *reduced[layer], shapes, part, outs)
+    outs = assemble(place, 0, *reduced[0], shapes + [(1, rows, 128)], part, outs)
+    gate_out, up_out, down_out, out_out, query_out, key_out, value_out, gain_out = outs
+    gain_out = gain_out[0, :, : 2 * layers].T.reshape(layers, 2, rows)
     return (
         output,
         d_tokens,
         gain_out[:, 0],
-        stacked(lambda r: r[4][0]),
-        stacked(lambda r: r[4][1]),
-        stacked(lambda r: r[4][2]),
-        stacked(lambda r: r[3]),
+        query_out,
+        key_out,
+        value_out,
+        out_out,
         gain_out[:, 1],
-        *spread_quarters([r[0] for r in reduced], [r[1] for r in reduced], part),
-        stacked(lambda r: r[2]),
+        gate_out,
+        up_out,
+        down_out,
     )
 
 

time: 1540 us -> 1320 us (0.86)
  waiting for transfers between devices: 612 us -> 455 us
  matrix products: 332 us -> 176 us
  Pallas kernels: 118 us -> 274 us
  local copies, waits for them, and re-layouts: 241 us -> 179 us
  other arithmetic: 169 us -> 153 us
    pallas_call x1 -> x6, Pallas kernels: 6.94 us -> 164 us  [the longest x4 145 us: mlp_back(): pl.pallas_call(mlp_back_kernel, grid=(steps,), in_specs=[whole(grad.shape...]
    dot_general x14 -> x4, matrix products: 119 us -> 30.6 us  [dot_t(): lax.dot_general(left, right, (((1,), (1,)), ((), ())), preferred_element_...]
    ppermute x18, waiting for transfers between devices: 279 us -> 192 us  [other_y(): return lax.ppermute(value, 'seq', Y_SWAP)]
    all_gather x6, waiting for transfers between devices: 158 us -> 84.8 us  [gather_dp(): return lax.all_gather(piece, 'dp', axis=0, tiled=True)]
    dot_general x12 -> x4, matrix products: 99.9 us -> 29.7 us  [tdot(): lax.dot_general(left, right, (((0,), (0,)), ((), ())), preferred_element_...]
    slice x20 -> x4, local copies, waits for them, and re-layouts: 34 us -> 5.27 us  [the longest x1 1.91 us: attention_half(): w_key[layer]]
    ppermute x25 -> x38, waiting for transfers between devices: 5.92 us -> 29 us  [other_core(): return lax.ppermute(value, 'seq', CORE_SWAP)]
    select_n x8 -> x0, local copies, waits for them, and re-layouts: 21.9 us -> none  [pair(): jnp.where(flag == 0, jnp.concatenate([mine, other], axis=axis), jnp.conca...]
  transfers between devices with their start and end apart: 66 -> 76, of which waited for: 26 -> 34; matrix products, arithmetic and copies ran while one was open for 36% -> 32% of each run, Pallas kernels for 7% -> 18%
where the time goes in v3:
time: 1320 us; the launch traced here: 1310 us
  waiting for transfers between devices  455 us (34%)
  Pallas kernels  274 us (21%)
  local copies, waits for them, and re-layouts  179 us (14%)
  matrix products  176 us (13%)
  other arithmetic  153 us (12%)
  starting transfers between devices  56.6 us (4%)
  between operations  16.1 us (1%)
    ppermute x18, waiting for transfers between devices, other_y(): return lax.ppermute(value, 'seq', Y_SWAP)  192 us
    ppermute x12, waiting for transfers between devices, dp_swap(): return lax.ppermute(value, 'dp', [(d, d ^ 1 << bit) for d in range(size)])  149 us
    pallas_call x4, Pallas kernels, mlp_back(): pl.pallas_call(mlp_back_kernel, grid=(steps,), in_specs=[whole(grad.shape...  145 us
    dot_general x12, matrix products, dot(): return jnp.dot(left, right, preferred_element_type=jnp.float32)  116 us
    all_gather x6, waiting for transfers between devices, gather_dp(): return lax.all_gather(piece, 'dp', axis=0, tiled=True)  84.8 us
    pallas_call x2, Pallas kernels, attend_forward(): pl.pallas_call(forward_kernel, grid=(groups,), in_specs=[whole(raw.shape)...  60.1 us
    unnamed x258, local copies, waits for them, and re-layouts  58.6 us
    pallas_call x2, Pallas kernels, attend_backward(): pl.pallas_call(backward_kernel, grid=(groups,), in_specs=[each((2 * rows,...  50.6 us
  transfers between devices with their start and end apart: 76, of which 34 were waited for; matrix products, arithmetic and copies ran while one was open for 32% of the time, Pallas kernels for 18%

profile of v3, /device:TPU:0, one launch (start us, length us, event | category | flops | bytes accessed | tf_op | source)
XLA Modules:
  0.0 1310.2 jit_solution(9386246754733544206)
XLA Ops:
  28.8 33.6 %collective-permute-done = bf16[2,256,1536]{2,1,0:T(8,128)(2,1)S(1)} collective-permute-done((bf16[2,256,1536]{2,1,0:T(8,128)(2,1)S(1)}, bf16[2,256,1536]{2,1,0:T(8,128)(2,1)S(1)}, u32[]{:S(2)}, u32[]{:S(2)}) %collective-permute-start) | collective-permute-done | bytes 1572896 | tf_op jit(solution)/shard_map/ppermute | solution.py:245
  63.6 30.3 %all-gather.16.cloned.1.call-done = bf16[1,768,2432]{2,1,0:T(8,128)(2,1)} async-done(((bf16[1,96,2432]{2,1,0:T(8,128)(2,1)}), bf16[1,768,2432]{2,1,0:T(8,128)(2,1)}) %all-gather.16.cloned.1.call-update) | async-done | bytes 3735568 | tf_op jit(solution)/shard_map/all_gather | solution.py:263
  112.7 47.6 %all-gather.10.cloned.1.call-done.refs_1_ = bf16[768,2304]{1,0:T(8,128)(2,1)} async-done(((bf16[96,2304]{1,0:T(8,128)(2,1)}), bf16[768,2304]{1,0:T(8,128)(2,1)}) %all-gather.10.cloned.1.call-update) | async-done | bytes 3538960 | tf_op jit(solution)/shard_map/all_gather | solution.py:263
  208.9 30.1 %attention_forward.2 = (bf16[1024,768]{1,0:T(8,128)(2,1)S(1)}, bf16[4,2048,96]{2,1,0:T(8,128)(2,1)}, bf16[4,1024,96]{2,1,0:T(8,128)(2,1)S(1)}, bf16[4,1024,96]{2,1,0:T(8,128)(2,1)S(1)}, f32[4,4,512]{2,1,0:T(4,128)S(1)}) custom-call(f32[1024,1536]{1,0:T(8,128)} %fusion.16.raw_ref, f32[1024,96]{1,0:T(8,128)S(1)} %copy.154.cos_ref, ...), custom_call_target="tpu_custom_call" | custom-call | flops 1000000 | bytes 1000000 | tf_op jit(solution)/shard_map/attention_forward/pallas_call | solution.py:118
  287.8 13.6 %fusion.43.refs_1_.refs_2_.refs_3_ = f32[1024,2048]{1,0:T(8,128)} fusion(bf16[1536,2048]{1,0:T(8,128)(2,1)} %all-gather.12.cloned.1.call-done.refs_4_.refs_5_, bf16[512,1536]{1,0:T(8,128)(2,1)} %collective-permute-done.6, bf16[512,1536]{1,0:T(8,128)(2,1)} %multiply_convert_fusion.2, pred[]{:T(512)S(6)} %eq.7), kind=kOutput, calls=%fused_computation.152 | convolution fusion | flops 6456606720 | bytes 17825792 | tf_op jit(solution)/shard_map/dot_general | solution.py:326
  392.7 23.9 %collective-permute-done.11.refs_0_ = bf16[512,1536]{1,0:T(8,128)(2,1)} collective-permute-done((bf16[512,1536]{1,0:T(8,128)(2,1)}, bf16[512,1536]{1,0:T(8,128)(2,1)}, u32[]{:S(2)}, u32[]{:S(2)}) %collective-permute-start.11) | collective-permute-done | bytes 1572896 | tf_op jit(solution)/shard_map/ppermute | solution.py:245
  443.9 30.0 %attention_forward.3 = (bf16[1024,768]{1,0:T(8,128)(2,1)S(1)}, bf16[4,2048,96]{2,1,0:T(8,128)(2,1)}, bf16[4,1024,96]{2,1,0:T(8,128)(2,1)S(1)}, bf16[4,1024,96]{2,1,0:T(8,128)(2,1)S(1)}, f32[4,4,512]{2,1,0:T(4,128)S(1)}) custom-call(f32[1024,1536]{1,0:T(8,128)} %fusion.12.raw_ref, f32[1024,96]{1,0:T(8,128)S(1)} %copy.154.cos_ref, ...), custom_call_target="tpu_custom_call" | custom-call | flops 1000000 | bytes 1000000 | tf_op jit(solution)/shard_map/attention_forward/pallas_call | solution.py:118
  493.8 13.6 %fusion.39.refs_1_.refs_2_.refs_3_ = f32[1024,2048]{1,0:T(8,128)} fusion(bf16[1536,2048]{1,0:T(8,128)(2,1)} %all-gather.14.cloned.1.call-done.refs_4_.refs_5_, bf16[512,1536]{1,0:T(8,128)(2,1)} %collective-permute-done.16, bf16[512,1536]{1,0:T(8,128)(2,1)} %multiply_convert_fusion, pred[]{:T(512)S(6)} %eq.7), kind=kOutput, calls=%fused_computation.148 | convolution fusion | flops 6456606720 | bytes 17825792 | tf_op jit(solution)/shard_map/dot_general | solution.py:326
  516.3 12.9 collective-permute-done.17.refs_0_
  543.2 13.7 %fusion.37.refs_2_.refs_3_ = f32[1024,2048]{1,0:T(8,128)} fusion(bf16[1536,2048]{1,0:T(8,128)(2,1)} %all-gather.14.cloned.1.call-done.refs_4_.refs_5_, bf16[512,1536]{1,0:T(8,128)(2,1)} %copy-done.84, bf16[512,1536]{1,0:T(8,128)(2,1)} %tie.49, pred[]{:T(512)S(6)} %eq.7), kind=kOutput, calls=%fused_computation.146 | convolution fusion | flops 6456606720 | bytes 17825792 | tf_op jit(solution)/shard_map/dot_general | solution.py:326
  556.9 35.6 %mlp_backward.4 = (f32[1024,1536]{1,0:T(8,128)}, bf16[1536,1024]{1,0:T(8,128)(2,1)}, bf16[1536,1024]{1,0:T(8,128)(2,1)}, bf16[1024,1536]{1,0:T(8,128)(2,1)}) custom-call(bf16[1024,1536]{1,0:T(8,128)(2,1)} %maximum_select_fusion.10.refs_0_, bf16[1536,1024]{1,0:T(8,128)(2,1)} %copy.167.refs_1_, f32[1024,2048]{1,0:T(8,128)} %fusion.37.refs_2_.refs_3_, ...), custom_call_target="tpu_custom_call" | custom-call | flops 1000000 | bytes 1000000 | tf_op jit(solution)/shard_map/mlp_backward/pallas_call | solution.py:413
  612.7 36.8 %mlp_backward.5 = (f32[1024,1536]{1,0:T(8,128)}, bf16[1536,1024]{1,0:T(8,128)(2,1)}, bf16[1536,1024]{1,0:T(8,128)(2,1)}, bf16[1024,1536]{1,0:T(8,128)(2,1)}) custom-call(bf16[1024,1536]{1,0:T(8,128)(2,1)} %tie.52.refs_0_, bf16[1536,1024]{1,0:T(8,128)(2,1)} %copy.166.refs_2_.refs_1_, f32[1024,2048]{1,0:T(8,128)} %fusion.39.refs_1_.refs_2_.refs_3_, ...), custom_call_target="tpu_custom_call" | custom-call | flops 1000000 | bytes 1000000 | tf_op jit(solution)/shard_map/mlp_backward/pallas_call | solution.py:413
  677.6 30.2 %collective-permute-done.21.refs_0_ = bf16[512,1536]{1,0:T(8,128)(2,1)} collective-permute-done((bf16[512,1536]{1,0:T(8,128)(2,1)}, bf16[512,1536]{1,0:T(8,128)(2,1)}, u32[]{:S(2)}, u32[]{:S(2)}) %collective-permute-start.21) | collective-permute-done | bytes 1572896 | tf_op jit(solution)/shard_map/ppermute | solution.py:245
  737.1 25.4 %attention_backward.2 = bf16[1024,1536]{1,0:T(8,128)(2,1)} custom-call(bf16[4,2048,96]{2,1,0:T(8,128)(2,1)} %get-tuple-element.59.q_ref, bf16[4,1024,96]{2,1,0:T(8,128)(2,1)S(1)} %copy-done.6, bf16[4,1024,96]{2,1,0:T(8,128)(2,1)S(1)} %copy-done.8, f32[4,4,512]{2,1,0:T(4,128)S(1)} %get-tuple-element.62.lse_ref, bf16[1024,768]{1,0:T(8,128)(2,1)S(1)} %copy-done, ...), custom_call_target="tpu_custom_call" | custom-call | flops 1000000 | bytes 1000000 | tf_op jit(solution)/shard_map/attention_backward/pallas_call | solution.py:214
  795.3 35.5 %collective-permute-done.31 = bf16[512,1536]{1,0:T(8,128)(2,1)S(1)} collective-permute-done((bf16[512,1536]{1,0:T(8,128)(2,1)S(1)}, bf16[512,1536]{1,0:T(8,128)(2,1)S(1)}, u32[]{:S(2)}, u32[]{:S(2)}) %collective-permute-start.31) | collective-permute-done | bytes 1572896 | tf_op jit(solution)/shard_map/ppermute | solution.py:245
  836.4 35.7 %mlp_backward.6 = (f32[1024,1536]{1,0:T(8,128)}, bf16[1536,1024]{1,0:T(8,128)(2,1)}, bf16[1536,1024]{1,0:T(8,128)(2,1)}, bf16[1024,1536]{1,0:T(8,128)(2,1)}) custom-call(bf16[1024,1536]{1,0:T(8,128)(2,1)} %maximum_select_fusion.13.refs_0_, bf16[1536,1024]{1,0:T(8,128)(2,1)} %copy.158.refs_1_, f32[1024,2048]{1,0:T(8,128)} %fusion.41.refs_2_.refs_3_, ...), custom_call_target="tpu_custom_call" | custom-call | flops 1000000 | bytes 1000000 | tf_op jit(solution)/shard_map/mlp_backward/pallas_call | solution.py:413
  884.5 36.8 %mlp_backward.7 = (f32[1024,1536]{1,0:T(8,128)}, bf16[1536,1024]{1,0:T(8,128)(2,1)}, bf16[1536,1024]{1,0:T(8,128)(2,1)}, bf16[1024,1536]{1,0:T(8,128)(2,1)}) custom-call(bf16[1024,1536]{1,0:T(8,128)(2,1)} %tie.55.refs_0_, bf16[1536,1024]{1,0:T(8,128)(2,1)} %copy.157.refs_2_.refs_1_, f32[1024,2048]{1,0:T(8,128)} %fusion.43.refs_1_.refs_2_.refs_3_, ...), custom_call_target="tpu_custom_call" | custom-call | flops 1000000 | bytes 1000000 | tf_op jit(solution)/shard_map/mlp_backward/pallas_call | solution.py:413
  952.0 25.3 %attention_backward.3.refs_1_ = bf16[1024,1536]{1,0:T(8,128)(2,1)} custom-call(bf16[4,2048,96]{2,1,0:T(8,128)(2,1)} %get-tuple-element.68.q_ref, bf16[4,1024,96]{2,1,0:T(8,128)(2,1)S(1)} %get-tuple-element.69.k_ref, bf16[4,1024,96]{2,1,0:T(8,128)(2,1)S(1)} %get-tuple-element.70.v_ref, f32[4,4,512]{2,1,0:T(4,128)S(1)} %get-tuple-element.71.lse_ref, ...), custom_call_target="tpu_custom_call" | custom-call | flops 1000000 | bytes 1000000 | tf_op jit(solution)/shard_map/attention_backward/pallas_call | solution.py:214
  997.3 26.2 %collective-permute-done.43 = bf16[2,2,192,2048]{3,2,1,0:T(8,128)(2,1)} collective-permute-done((bf16[2,2,192,2048]{3,2,1,0:T(8,128)(2,1)}, bf16[2,2,192,2048]{3,2,1,0:T(8,128)(2,1)}, u32[]{:S(2)}, u32[]{:S(2)}) %collective-permute-start.43) | collective-permute-done | bytes 3145760 | tf_op jit(solution)/shard_map/ppermute | solution.py:273
  1068.3 30.4 %collective-permute-done.44.refs_1_ = bf16[2,192,2048]{2,1,0:T(8,128)(2,1)S(1)} collective-permute-done((bf16[2,192,2048]{2,1,0:T(8,128)(2,1)}, bf16[2,192,2048]{2,1,0:T(8,128)(2,1)S(1)}, u32[]{:S(2)}, u32[]{:S(2)}) %collective-permute-start.44) | collective-permute-done | bytes 1572896 | tf_op jit(solution)/shard_map/ppermute | solution.py:273
  1115.8 19.1 %collective-permute-done.48.refs_0_ = bf16[192,2048]{1,0:T(8,128)(2,1)} collective-permute-done((bf16[192,2048]{1,0:T(8,128)(2,1)S(1)}, bf16[192,2048]{1,0:T(8,128)(2,1)}, u32[]{:S(2)}, u32[]{:S(2)}) %collective-permute-start.48) | collective-permute-done | bytes 786464 | tf_op jit(solution)/shard_map/ppermute | solution.py:273
  1211.6 21.5 %collective-permute-done.57 = bf16[2,192,1664]{2,1,0:T(8,128)(2,1)S(1)} collective-permute-done((bf16[2,192,1664]{2,1,0:T(8,128)(2,1)}, bf16[2,192,1664]{2,1,0:T(8,128)(2,1)S(1)}, u32[]{:S(2)}, u32[]{:S(2)}) %collective-permute-start.57) | collective-permute-done | bytes 1277984 | tf_op jit(solution)/shard_map/ppermute | solution.py:273
  1237.5 14.1 %collective-permute-done.58.refs_0_ = bf16[192,1664]{1,0:T(8,128)(2,1)S(1)} collective-permute-done((bf16[192,1664]{1,0:T(8,128)(2,1)S(1)}, bf16[192,1664]{1,0:T(8,128)(2,1)S(1)}, u32[]{:S(2)}, u32[]{:S(2)}) %collective-permute-start.58) | collective-permute-done | bytes 639008 | tf_op jit(solution)/shard_map/ppermute | solution.py:273
  1263.1 13.1 collective-permute-done.59.refs_5_
  (616 shorter events, 659.3 us)
Async XLA Ops:
  7.2 86.7 %all-gather.16.cloned.1.call-start = ((), (), s32[]{:S(2)}) async-start(), calls=%async_computation.7 | async-start | bytes 4202496 | tf_op jit(solution)/shard_map/all_gather | solution.py:263
  23.4 136.9 %all-gather.10.cloned.1.call-start = ((), (), s32[]{:S(2)}) async-start(), calls=%async_computation.2 | async-start | bytes 3981312 | tf_op jit(solution)/shard_map/all_gather | solution.py:263
  63.6 224.3 %all-gather.12.cloned.1.call-start = ((), (), s32[]{:S(2)}) async-start(), calls=%async_computation.3 | async-start | bytes 7077888 | tf_op jit(solution)/shard_map/all_gather | solution.py:263
  93.9 81.8 %collective-permute-start.1 = (bf16[768,2432]{1,0:T(8,128)(2,1)}, bf16[768,2432]{1,0:T(8,128)(2,1)}, u32[]{:S(2)}, u32[]{:S(2)}) collective-permute-start(bf16[768,2432]{1,0:T(8,128)(2,1)} %bitcast.238), channel_id=1, source_target_pairs={{0,2},{2,0},{1,3},{3,1},{4,6},{6,4},{5,7},{7,5},{8,10},{10,8},{9,1... | collective-permute-start | bytes 11206664 | tf_op jit(solution)/shard_map/ppermute | solution.py:245
  160.3 178.3 %all-gather.18.cloned.1.call-start = ((), (), s32[]{:S(2)}) async-start(), calls=%async_computation.8 | async-start | bytes 3538944 | tf_op jit(solution)/shard_map/all_gather | solution.py:263
  175.7 76.6 %collective-permute-start.3 = (bf16[768,2304]{1,0:T(8,128)(2,1)}, bf16[768,2304]{1,0:T(8,128)(2,1)}, u32[]{:S(2)}, u32[]{:S(2)}) collective-permute-start(bf16[768,2304]{1,0:T(8,128)(2,1)} %tie.42), channel_id=1, source_target_pairs={{0,2},{2,0},{1,3},{3,1},{4,6},{6,4},{5,7},{7,5},{8,10},{10,8},{9,1... | collective-permute-start | bytes 10616840 | tf_op jit(solution)/shard_map/ppermute | solution.py:245
  195.8 56.5 %collective-permute-start.4 = (bf16[768,768]{1,0:T(8,128)(2,1)}, bf16[768,768]{1,0:T(8,128)(2,1)}, u32[]{:S(2)}, u32[]{:S(2)}) collective-permute-start(bf16[768,768]{1,0:T(8,128)(2,1)} %get-tuple-element.131), channel_id=1, source_target_pairs={{0,1},{1,0},{2,3},{3,2},{4,5},{5,4},{6,7},{7,6},{8,9},{9,8},{10,11... | collective-permute-start | bytes 3538952 | tf_op jit(solution)/shard_map/ppermute | solution.py:241
  277.1 216.2 %all-gather.14.cloned.1.call-start = ((), (), s32[]{:S(2)}) async-start(), calls=%async_computation.4 | async-start | bytes 7077888 | tf_op jit(solution)/shard_map/all_gather | solution.py:263
  365.0 191.9 %all-gather.20.cloned.1.call-start = ((), (), s32[]{:S(2)}) async-start(), calls=%async_computation.9 | async-start | bytes 3538944 | tf_op jit(solution)/shard_map/all_gather | solution.py:263
  424.5 52.6 %collective-permute-start.13 = (bf16[512,1536]{1,0:T(8,128)(2,1)S(1)}, bf16[512,1536]{1,0:T(8,128)(2,1)}, u32[]{:S(2)}, u32[]{:S(2)}) collective-permute-start(bf16[512,1536]{1,0:T(8,128)(2,1)S(1)} %maximum_select_fusion.21), channel_id=1, source_target_pairs={{0,2},{2,0},{1,3},{3,1},{4,6},{6,4},{5,7},{7,5},{8,10},{10,8},{9,1... | collective-permute-start | bytes 4718600 | tf_op jit(solution)/shard_map/ppermute | solution.py:245
  491.9 441.8 %reduce-scatter.3.cloned.1.call-start = ((), (), s32[]{:S(2)}) async-start(), calls=%async_computation.5 | async-start | bytes 3538944 | tf_op jit(solution)/shard_map/reduce_scatter | solution.py:744
  601.9 47.5 %collective-permute-start.26 = (bf16[512,1536]{1,0:T(8,128)(2,1)}, bf16[512,1536]{1,0:T(8,128)(2,1)}, u32[]{:S(2)}, u32[]{:S(2)}) collective-permute-start(bf16[512,1536]{1,0:T(8,128)(2,1)} %add_convert_fusion.1.refs_1_), channel_id=1, source_target_pairs={{0,2},{2,0},{1,3},{3,1},{4,6},{6,4},{5,7},{7,5},{8,10},{10,8},{9,1... | collective-permute-start | bytes 4718600 | tf_op jit(solution)/shard_map/ppermute | solution.py:245
  612.6 54.0 %collective-permute-start.20 = (bf16[512,1536]{1,0:T(8,128)(2,1)}, bf16[512,1536]{1,0:T(8,128)(2,1)}, u32[]{:S(2)}, u32[]{:S(2)}) collective-permute-start(bf16[512,1536]{1,0:T(8,128)(2,1)} %dynamic-slice_convert_fusion.6), channel_id=1, source_target_pairs={{0,1},{1,0},{2,3},{3,2},{4,5},{5,4},{6,7},{7,6},{8,9},{9,8},{10,11... | collective-permute-start | bytes 4718600 | tf_op jit(solution)/shard_map/ppermute | solution.py:241
  677.4 379.9 %reduce-scatter.5.cloned.1.call-start = ((), (), s32[]{:S(2)}) async-start(), calls=%async_computation.6 | async-start | bytes 15040512 | tf_op jit(solution)/shard_map/reduce_scatter | solution.py:746
  722.0 47.9 %collective-permute-start.46 = (bf16[768,768]{1,0:T(8,128)(2,1)}, bf16[768,768]{1,0:T(8,128)(2,1)}, u32[]{:S(2)}, u32[]{:S(2)}) collective-permute-start(bf16[768,768]{1,0:T(8,128)(2,1)} %get-tuple-element.125), channel_id=1, source_target_pairs={{0,1},{1,0},{2,3},{3,2},{4,5},{5,4},{6,7},{7,6},{8,9},{9,8},{10,11... | collective-permute-start | bytes 3538952 | tf_op jit(solution)/shard_map/ppermute | solution.py:241
  933.8 169.8 %collective-permute-start.45 = (bf16[128,1536]{1,0:T(8,128)(2,1)}, bf16[128,1536]{1,0:T(8,128)(2,1)}, u32[]{:S(2)}, u32[]{:S(2)}) collective-permute-start(bf16[128,1536]{1,0:T(8,128)(2,1)} %reduce-scatter.3.cloned.1.call-done.refs_4_), channel_id=1, source_target_pairs={{0,2},{2,0},{1,3},{3,1},{4,6},{6,4},{5,7},{7,5},{8,10},{10,8},{9,1... | collective-permute-start | bytes 1179656 | tf_op jit(solution)/shard_map/ppermute | solution.py:245
  944.1 79.4 %collective-permute-start.43 = (bf16[2,2,192,2048]{3,2,1,0:T(8,128)(2,1)}, bf16[2,2,192,2048]{3,2,1,0:T(8,128)(2,1)}, u32[]{:S(2)}, u32[]{:S(2)}) collective-permute-start(bf16[2,2,192,2048]{3,2,1,0:T(8,128)(2,1)} %dynamic-slice_bitcast_fusion), channel_id=1, source_target_pairs={{0,4},{4,0},{8,12},{12,8},{16,20},{20,16},{24,28},{28,24},{1,5},{5... | collective-permute-start | bytes 9437192 | tf_op jit(solution)/shard_map/ppermute | solution.py:273
  986.9 58.6 %collective-permute-start.37 = (bf16[512,1536]{1,0:T(8,128)(2,1)}, bf16[512,1536]{1,0:T(8,128)(2,1)}, u32[]{:S(2)}, u32[]{:S(2)}) collective-permute-start(bf16[512,1536]{1,0:T(8,128)(2,1)} %dynamic-slice_convert_fusion), channel_id=1, source_target_pairs={{0,1},{1,0},{2,3},{3,2},{4,5},{5,4},{6,7},{7,6},{8,9},{9,8},{10,11... | collective-permute-start | bytes 4718600 | tf_op jit(solution)/shard_map/ppermute | solution.py:241
  996.1 60.9 %collective-permute-start.40 = (bf16[2,2,128,1536]{3,2,1,0:T(8,128)(2,1)}, bf16[2,2,128,1536]{3,2,1,0:T(8,128)(2,1)}, u32[]{:S(2)}, u32[]{:S(2)}) collective-permute-start(bf16[2,2,128,1536]{3,2,1,0:T(8,128)(2,1)} %bitcast.232), channel_id=1, source_target_pairs={{0,4},{4,0},{8,12},{12,8},{16,20},{20,16},{24,28},{28,24},{1,5},{5... | collective-permute-start | bytes 4718600 | tf_op jit(solution)/shard_map/ppermute | solution.py:273
  1028.0 70.8 %collective-permute-start.44 = (bf16[2,192,2048]{2,1,0:T(8,128)(2,1)}, bf16[2,192,2048]{2,1,0:T(8,128)(2,1)S(1)}, u32[]{:S(2)}, u32[]{:S(2)}) collective-permute-start(bf16[2,192,2048]{2,1,0:T(8,128)(2,1)} %dynamic-slice_bitcast_fusion.1), channel_id=1, source_target_pairs={{0,16},{4,20},{8,24},{12,28},{16,0},{20,4},{24,8},{28,12},{1,17},{... | collective-permute-start | bytes 4718600 | tf_op jit(solution)/shard_map/ppermute | solution.py:273
  1057.3 46.3 %collective-permute-start.47 = (bf16[192,4352]{1,0:T(8,128)(2,1)}, bf16[192,4352]{1,0:T(8,128)(2,1)}, u32[]{:S(2)}, u32[]{:S(2)}) collective-permute-start(bf16[192,4352]{1,0:T(8,128)(2,1)} %reduce-scatter.5.cloned.1.call-done.refs_0_), channel_id=1, source_target_pairs={{0,2},{2,0},{1,3},{3,1},{4,6},{6,4},{5,7},{7,5},{8,10},{10,8},{9,1... | collective-permute-start | bytes 5013512 | tf_op jit(solution)/shard_map/ppermute | solution.py:245
  1103.3 56.8 %collective-permute-start.42 = (bf16[2,2,192,1664]{3,2,1,0:T(8,128)(2,1)}, bf16[2,2,192,1664]{3,2,1,0:T(8,128)(2,1)}, u32[]{:S(2)}, u32[]{:S(2)}) collective-permute-start(bf16[2,2,192,1664]{3,2,1,0:T(8,128)(2,1)} %bitcast.222), channel_id=1, source_target_pairs={{0,4},{4,0},{8,12},{12,8},{16,20},{20,16},{24,28},{28,24},{1,5},{5... | collective-permute-start | bytes 7667720 | tf_op jit(solution)/shard_map/ppermute | solution.py:273
  1112.2 47.9 %collective-permute-start.38 = (bf16[256,1536]{1,0:T(8,128)(2,1)}, bf16[256,1536]{1,0:T(8,128)(2,1)}, u32[]{:S(2)}, u32[]{:S(2)}) collective-permute-start(bf16[256,1536]{1,0:T(8,128)(2,1)} %fusion.35), channel_id=1, source_target_pairs={{0,2},{2,0},{1,3},{3,1},{4,6},{6,4},{5,7},{7,5},{8,10},{10,8},{9,1... | collective-permute-start | bytes 2359304 | tf_op jit(solution)/shard_map/ppermute | solution.py:245
  1178.1 55.0 %collective-permute-start.57 = (bf16[2,192,1664]{2,1,0:T(8,128)(2,1)}, bf16[2,192,1664]{2,1,0:T(8,128)(2,1)S(1)}, u32[]{:S(2)}, u32[]{:S(2)}) collective-permute-start(bf16[2,192,1664]{2,1,0:T(8,128)(2,1)} %bitcast.235), channel_id=1, source_target_pairs={{0,16},{4,20},{8,24},{12,28},{16,0},{20,4},{24,8},{28,12},{1,17},{... | collective-permute-start | bytes 3833864 | tf_op jit(solution)/shard_map/ppermute | solution.py:273
  (175 other events, 2161.9 us)
Sparse Core Ops, SparseCore 0:
  23.5 70.3 all-gather.15
  96.6 63.5 all-gather.9
  162.5 97.5 all-gather.11
  277.3 61.3 all-gather.17
  365.1 97.7 all-gather.13
  492.1 58.8 all-gather.19
  677.5 72.8 reduce-scatter.2
  778.0 216.5 reduce-scatter.4

commit v4 on v3

--- a/solution.py
+++ b/solution.py
@@ -365,13 +365,25 @@
     before = refs[7:-4]
     total_ref, *out_refs = refs[-4:]
     step = pl.program_id(0)
-    gate, up = gate_ref[...], up_ref[...]
-    grad_hidden = nt(grad_ref[...], down_w_ref[...])
-    sig = 1.0 / (1.0 + jnp.exp(-gate))
-    swish = gate * sig
-    grad_gate = (grad_hidden * up * (sig + swish * (1.0 - sig))).astype(jnp.bfloat16)
-    grad_up = (grad_hidden * swish).astype(jnp.bfloat16)
-    hidden_t = (swish * up).T.astype(jnp.bfloat16)
+    pieces = []
+    size = gate_ref.shape[0] // 4
+    for piece in range(4):
+        rows = pl.ds(piece * size, size)
+        gate, up = gate_ref[rows, :], up_ref[rows, :]
+        grad_hidden = nt(grad_ref[rows, :], down_w_ref[...])
+        sig = 1.0 / (1.0 + jnp.exp(-gate))
+        swish = gate * sig
+        grad_gate = grad_hidden * up * (sig + swish * (1.0 - sig))
+        pieces.append(
+            (
+                grad_gate.astype(jnp.bfloat16),
+                (grad_hidden * swish).astype(jnp.bfloat16),
+                (swish * up).T.astype(jnp.bfloat16),
+            )
+        )
+    grad_gate, grad_up, hidden_t = (
+        jnp.concatenate(part, axis=axis) for part, axis in zip(zip(*pieces), (0, 0, 1))
+    )
     term = nt(
         jnp.concatenate([grad_gate, grad_up], axis=1),
         jnp.concatenate([gate_w_ref[...], up_w_ref[...]], axis=1),
@@ -457,17 +469,25 @@
                         for quarter in range(4):
                             value = by_place[quarter][:, here].astype(jnp.float32)
                             outs[out][0, quarter * part : (quarter + 1) * part, :] = value
+                    elif kind in ("blocks", "gains"):
+                        for half in range(2):
+                            values = [by_place[2 * half + core][:, here] for core in range(2)]
+                            values = [value.astype(jnp.float32) for value in values]
+                            count = values[0].shape[0]
+                            to = slice(half * count, (half + 1) * count)
+                            if kind == "gains":
+                                outs[out][0, to, :] = values[0] + values[1]
+                            else:
+                                outs[out][0, to, :size] = values[0]
+                                outs[out][0, to, size:] = values[1]
                     else:
                         halves = [
                             by_place[half][:, here].astype(jnp.float32)
                             + by_place[half + 2][:, here].astype(jnp.float32)
                             for half in range(2)
                         ]
-                        if kind == "sum":
-                            outs[out][0, :, :] = halves[0] + halves[1]
-                        else:
-                            for half in range(2):
-                                outs[out][0, :, half * size : (half + 1) * size] = halves[half]
+                        for half in range(2):
+                            outs[out][0, :, half * size : (half + 1) * size] = halves[half]
 
 
 def cuts_outputs(cuts):
@@ -558,7 +578,11 @@
     (stream, grad), came = regroup(tokens, cotangent)
     came = came.reshape(-1, features)
 
-    def attention_half(layer):
+    def quarter(weight):
+        cut = weight.reshape(rows, dp_size, 4, part)
+        return lax.dynamic_index_in_dim(cut, index, 2, keepdims=False).reshape(rows, ff_quarter)
+
+    def attention_local(layer):
         local = [
             lax.dynamic_slice_in_dim(w_query[layer], core * q_half, q_half, 1),
             lax.dynamic_slice_in_dim(w_key[layer], core * k_half, k_half, 1),
@@ -566,29 +590,53 @@
             lax.dynamic_slice_in_dim(w_out[layer], core * out_half, out_half, 1),
         ]
         if layer == 0:
-            local.append(gain_cols)
+            local.insert(3, gain_cols)
         local = jnp.concatenate(local, axis=1).reshape(2, rows // 2, -1)
-        local = lax.dynamic_index_in_dim(local, side, 0, keepdims=False)
-        return gather_dp(tie(local, came) if layer else local)
-
-    def gather_layer(layer, near, far, before):
-        def quarter(weight):
-            cut = weight.reshape(rows, dp_size, 4, part)
-            return lax.dynamic_index_in_dim(cut, index, 2, keepdims=False).reshape(rows, ff_quarter)
-
+        return lax.dynamic_index_in_dim(local, side, 0, keepdims=False)
+
+    gate_up_locals = [
+        jnp.concatenate([quarter(w_gate[layer]), quarter(w_up[layer])], axis=1)
+        for layer in range(layers)
+    ]
+    down_locals = [
+        lax.dynamic_slice_in_dim(w_down[layer], index * part, part, 0) for layer in range(layers)
+    ]
+    halves = [gather_dp(attention_local(0))]
+    for layer in range(1, layers):
+        halves.append(gather_dp(tie(attention_local(layer), came, *gate_up_locals, *down_locals)))
+
+    def joined(near, far):
         near, far = (half.reshape(dp_size, 1, rows // 2, -1) for half in (near, far))
-        attention = pair(side, near, far, axis=1).reshape(features, -1)
-        gate_up = jnp.concatenate([quarter(w_gate[layer]), quarter(w_up[layer])], axis=1)
-        gate_up = gather_dp(gate_up if before is None else tie(gate_up, before))
-        qkv = attention[:, :qkv_width]
-        out_cols = attention[:, qkv_width : qkv_width + out_half]
+        return pair(side, near, far, axis=1).reshape(features, -1)
+
+    firsts = halves[0].shape[1] - out_half
+    far_qkv = other_y(halves[0][:, :firsts])
+    far_out = other_y(tie(halves[0][:, firsts:], far_qkv))
+    last_far = far_out
+    fars = []
+    for layer in range(1, layers):
+        last_far = other_y(tie(halves[layer], last_far))
+        fars.append(last_far)
+    far_qkv = tie(far_qkv, *halves[1:])
+    first_qkv = joined(halves[0][:, :firsts], far_qkv)
+    attention_weights = [(first_qkv[:, :qkv_width], joined(halves[0][:, firsts:], far_out))]
+    for near, far in zip(halves[1:], fars):
+        joint = joined(near, far)
+        attention_weights.append((joint[:, :qkv_width], joint[:, qkv_width:]))
+    all_weights = []
+    for layer in range(layers):
+        gate_up = gate_up_locals[layer]
+        gate_up = gather_dp(tie(gate_up, halves[1]) if layer == 0 else gate_up)
+        down = gather_dp(down_locals[layer])
+        qkv, out_cols = attention_weights[layer]
         kept = lax.dynamic_slice_in_dim(out_cols, core * q_half, q_half, 0)
         sent = lax.dynamic_slice_in_dim(out_cols, (1 - core) * q_half, q_half, 0)
         out = pair(core, kept, other_core(sent), axis=1)
-        down = gather_dp(lax.dynamic_slice_in_dim(w_down[layer], index * part, part, 0))
-        return (qkv, out, gate_up, down), attention[:, qkv_width + out_half :]
-
-    def forward(stream, weights, gain_one, gain_two, ready):
+        all_weights.append((qkv, out, gate_up, down))
+    gains = first_qkv[:, qkv_width : qkv_width + 2 * layers].T.astype(jnp.float32)
+    gains = gains.reshape(2, layers, features)
+
+    def forward(stream, weights, gain_one, gain_two, ready, last):
         qkv_w, out_w, gate_up_w, down_w = weights
         normed_one, inverse_one, input_one = norm_rows(stream, gain_one)
         full_one = both_cores(input_one)
@@ -610,15 +658,24 @@
         near_in = both_cores(input_two)
         near_turned = turned(near_in)
         near_gate_up = dot(near_in, gate_up_w)
-        near_total = dot(hidden_of(near_gate_up), down_w)
         far_in = both_cores(tie(far, near_gate_up, near_turned))
         far_gate_up = dot(far_in, gate_up_w)
-        far_total = dot(hidden_of(far_gate_up), down_w)
-        far_rows = own_rows(far_total).astype(jnp.bfloat16)
         far_turned = turned(far_in)
-        far = tie(other_y(far_rows), far_turned)
-        near = own_rows(tie(near_total, far_total))
-        result = stream_two + (near + far.astype(jnp.float32))
+
+        def down_dots(after):
+            pieces = [near_gate_up, far_gate_up]
+            if after is not None:
+                pieces = [tie(piece, after) for piece in pieces]
+            return [dot(hidden_of(piece), down_w) for piece in pieces]
+
+        def finish(totals, meanwhile):
+            near_total, far_total = totals
+            far_rows = own_rows(far_total).astype(jnp.bfloat16)
+            far = tie(other_y(far_rows), meanwhile)
+            near = own_rows(tie(near_total, far_total))
+            return stream_two + (near + far.astype(jnp.float32))
+
+        result = (down_dots, finish) if last else finish(down_dots(None), far_turned)
         kept_mlp = [(near_turned, near_gate_up), (far_turned, far_gate_up)]
         saved = (
             normed_one,
@@ -632,7 +689,7 @@
         )
         return result, saved
 
-    def backward(grad, saved, weights, gain_one, gain_two, far, also):
+    def backward(grad, saved, weights, gain_one, gain_two, far, fill):
         (
             normed_one,
             inverse_one,
@@ -645,11 +702,16 @@
         ) = saved
         qkv_w, out_w, gate_up_w, down_w = weights
         grad_low = grad.astype(jnp.bfloat16)
-        if far is None:
-            far = other_y(grad_low)
+        late = None
+        if fill is not None:
+            down_dots, finish = fill
+            totals = down_dots(grad_low)
+            far = tie(other_y(grad_low), *totals)
         far, *mlp_grads = mlp_back(both_cores(far), *kept_mlp[1], gate_up_w, down_w, [])
         far_rows = own_rows(far).astype(jnp.bfloat16)
         far = other_y(far_rows)
+        if fill is not None:
+            late = finish(totals, far)
         near = tie(both_cores(grad_low), far_rows)
         near, *mlp_grads = mlp_back(near, *kept_mlp[0], gate_up_w, down_w, mlp_grads)
         grad_two = own_rows(tie(near, far)) + far.astype(jnp.float32)
@@ -658,15 +720,19 @@
         mid_full = both_cores(grad_mid.astype(jnp.bfloat16))
         grad_out_w = tdot(mixed, mid_full)
         grad_mixed = dot_t(mid_full, out_w).astype(jnp.bfloat16)
-        grad_mixed = tie(grad_mixed, *also) if also else grad_mixed
+        if late is not None:
+            got = swapped(late)
+            grad_mixed = tie(grad_mixed, got, grad_out_w)
+            late = (late, got)
         grad_qkv = attend_backward(*attended, grad_mixed, cosine, sine)
         grad_qkv_w = tdot(full_one, grad_qkv)
-        grad_one = own_rows(dot_t(grad_qkv, qkv_w))
+        low = grad_qkv if fill is None else tie(grad_qkv, grad_qkv_w)
+        grad_one = own_rows(dot_t(low, qkv_w))
         norm_one_in, gain_one_g = norm_back(grad_one, normed_one, inverse_one, gain_one)
         grad = grad_mid + norm_one_in
         points = (mid_full, grad_qkv, grad_one)
         parts = (mlp_grads, grad_out_w, grad_qkv_w, gain_one_g, gain_two_g)
-        return grad, parts, points
+        return grad, parts, points, late
 
     def four(piece):
         got = other_y(piece)
@@ -709,35 +775,46 @@
                 value = add(send(value, step, None))
             return value
 
+        def sides(value):
+            cut = value.reshape(dp_size, 2, rows // 2, -1)
+            kept = lax.dynamic_index_in_dim(cut, side, 1, keepdims=False)
+            sent = lax.dynamic_index_in_dim(cut, 1 - side, 1, keepdims=False)
+            shape = (features // 2, -1)
+            return kept.reshape(shape), sent.reshape(shape)
+
         gate_up = send(jnp.concatenate([gate, up], axis=1), 0, "x")
+        out_near, sent = sides(out_grad)
+        out_far = other_y(sent)
+        qkv_near, sent = sides(qkv_grad)
+        qkv_far = other_y(tie(sent, out_far))
         gate_up = send(add(gate_up), 1, "z")
-        last["x"] = after_attention
+        last["x"] = tie(after_attention, last["x"].reshape(-1, last["x"].shape[-1]))
         down = send(down, 0, "x")
-        last["any"] = after_all
-        out = send(out_grad, 0, "x")
-        qkv = send(qkv_grad, 0, "x")
         down = send(add(down), 1, "z")
+        out = send(out_near + take(out_far), 0, "x")
         out = send(add(out), 1, "z")
+        gate_up = finish(add(gate_up))
+        qkv = send(qkv_near + take(qkv_far), 0, "x")
+        down = finish(add(down))
         earlier = [[four_taken(piece) for piece in pieces] for pieces in earlier]
-        gate_up = finish(add(gate_up))
+        out = finish(add(out))
         qkv = send(add(qkv), 1, "z")
-        grad = take(swapped(grad))
         gate_up = four_taken(gate_up)
-        down = four_taken(finish(add(down)))
-        out = finish(add(out))
+        down = four_taken(down)
+        got_grad = take(swapped(grad))
         qkv = finish(add(qkv))
         joint = jnp.concatenate([out, qkv], axis=1)
         cuts = [
             [("columns", 0, ff_quarter, 0), ("columns", ff_quarter, ff_quarter, 1)],
-            attention_cuts(0) + [("sum", joint.shape[1] - 128, 128, 7)],
+            attention_cuts(0, "blocks") + [("gains", joint.shape[1] - 128, 128, 7)],
             [("rows", 0, features, 2)],
         ]
-        return ([gate_up, four(joint), down], cuts), earlier, grad
-
-    def attention_cuts(at):
+        return ([gate_up, four(joint), down], cuts), earlier, got_grad
+
+    def attention_cuts(at, kind="halves"):
         sizes = (out_half, q_half, k_half, k_half)
         firsts = [at + sum(sizes[:i]) for i in range(4)]
-        return [("halves", first, size, 3 + i) for i, (first, size) in enumerate(zip(firsts, sizes))]
+        return [(kind, first, size, 3 + i) for i, (first, size) in enumerate(zip(firsts, sizes))]
 
     def reduce_first(grads, out_grad, qkv_grad, points):
         gate, up, down = grads
@@ -756,52 +833,40 @@
         sent = lax.dynamic_slice_in_dim(grad, (1 - core) * out_half, out_half, 1)
         return pair(core, kept, other_core(sent), axis=0)
 
-    halves = [attention_half(layer) for layer in range(layers)]
-    swapped_halves = []
-    for half in halves:
-        swapped_halves.append(other_y(tie(half, swapped_halves[-1]) if swapped_halves else half))
-    swapped_halves[0] = tie(swapped_halves[0], *halves[1:])
-    gathered = [
-        gather_layer(layer, halves[layer], swapped_halves[layer], halves[1] if layer == 0 else None)
-        for layer in range(layers)
-    ]
-    all_weights = [weights for weights, _ in gathered]
-    gains = gathered[0][1][:, : 2 * layers].T.astype(jnp.float32)
-    gains = gains.reshape(2, layers, features)
     stream, grad = stream.astype(jnp.float32), grad.astype(jnp.float32)
     far_cotangent = other_y(grad.astype(jnp.bfloat16))
     all_saved = []
     for layer in range(layers):
-        ready = far_cotangent if layer == layers - 1 else swapped_halves[layer + 1]
+        ready = far_cotangent if layer == layers - 1 else fars[layer]
         stream, saved = forward(
-            stream, all_weights[layer], gains[0, layer], gains[1, layer], ready
+            stream, all_weights[layer], gains[0, layer], gains[1, layer], ready, layer == layers - 1
         )
         all_saved.append(saved)
-    also = [swapped(stream)]
-    output = ungroup(stream, also[0]).astype(jnp.bfloat16)
     reduced = [None] * layers
     gain_grads = []
     for layer in reversed(range(layers)):
-        grad, (mlp_g, out_g, qkv_g, one_g, two_g), points = backward(
+        grad, (mlp_g, out_g, qkv_g, one_g, two_g), points, late = backward(
             grad,
             all_saved[layer],
             all_weights[layer],
             gains[0, layer],
             gains[1, layer],
             far_cotangent if layer == layers - 1 else None,
-            also,
+            stream if layer == 0 else None,
         )
         gain_grads = [one_g, two_g] + gain_grads
         out_g = columns_of_core(out_g)
         if layer > 0:
             reduced[layer] = reduce_first(mlp_g, out_g, qkv_g, points)
-            also = []
         else:
             extra = jnp.stack(gain_grads, axis=1)
             extra = jnp.pad(extra, ((0, 0), (0, 128 - extra.shape[1])))
             qkv_g = jnp.concatenate([qkv_g, extra.astype(jnp.bfloat16)], axis=1)
             earlier = [reduced[at][0] for at in range(1, layers)]
-            reduced[0], earlier, got = reduce_last(mlp_g, out_g, qkv_g, points, earlier, grad)
+            reduced[0], earlier, got = reduce_last(
+                mlp_g, out_g, qkv_g, points, earlier, grad
+            )
+    output = ungroup(*late).astype(jnp.bfloat16)
     d_tokens = ungroup(grad, got)
     for layer in range(1, layers):
         reduced[layer] = earlier[layer - 1], reduced[layer][1]

time: 1320 us -> 1250 us (0.947)
  waiting for transfers between devices: 455 us -> 374 us
  local copies, waits for them, and re-layouts: 179 us -> 205 us
  Pallas kernels: 274 us -> 250 us
  other arithmetic: 153 us -> 168 us
    ppermute x12, waiting for transfers between devices: 149 us -> 84.3 us  [dp_swap(): return lax.ppermute(value, 'dp', [(d, d ^ 1 << bit) for d in range(size)])]
    pallas_call x4, Pallas kernels: 145 us -> 121 us  [mlp_back(): pl.pallas_call(mlp_back_kernel, grid=(steps,), in_specs=[whole(grad.shape...]
    ppermute x18 -> x21, waiting for transfers between devices: 192 us -> 168 us  [other_y(): return lax.ppermute(value, 'seq', Y_SWAP)]
    unnamed x258 -> x281, local copies, waits for them, and re-layouts: 58.6 us -> 74.9 us
    ppermute x18 -> x21, starting transfers between devices: 32.5 us -> 25.4 us  [other_y(): return lax.ppermute(value, 'seq', Y_SWAP)]
    select_n x10 -> x11, other arithmetic: 30 us -> 35.4 us  [pair(): jnp.where(flag == 0, jnp.concatenate([mine, other], axis=axis), jnp.conca...]
  transfers between devices with their start and end apart: 76 -> 79, of which waited for: 34 -> 32; matrix products, arithmetic and copies ran while one was open for 32% -> 37% of each run, Pallas kernels for 18% -> 17%
where the time goes in v4:
time: 1250 us; the launch traced here: 1240 us
  waiting for transfers between devices  374 us (30%)
  Pallas kernels  250 us (20%)
  local copies, waits for them, and re-layouts  205 us (16%)
  matrix products  184 us (15%)
  other arithmetic  168 us (13%)
  starting transfers between devices  46.9 us (4%)
  between operations  16.1 us (1%)
    ppermute x21, waiting for transfers between devices, other_y(): return lax.ppermute(value, 'seq', Y_SWAP)  168 us
    dot_general x12, matrix products, dot(): return jnp.dot(left, right, preferred_element_type=jnp.float32)  124 us
    pallas_call x4, Pallas kernels, mlp_back(): pl.pallas_call(mlp_back_kernel, grid=(steps,), in_specs=[whole(grad.shape...  121 us
    all_gather x6, waiting for transfers between devices, gather_dp(): return lax.all_gather(piece, 'dp', axis=0, tiled=True)  92.4 us
    ppermute x12, waiting for transfers between devices, dp_swap(): return lax.ppermute(value, 'dp', [(d, d ^ 1 << bit) for d in range(size)])  84.3 us
    unnamed x281, local copies, waits for them, and re-layouts  74.9 us
    pallas_call x2, Pallas kernels, attend_forward(): pl.pallas_call(forward_kernel, grid=(groups,), in_specs=[whole(raw.shape)...  60.2 us
    pallas_call x2, Pallas kernels, attend_backward(): pl.pallas_call(backward_kernel, grid=(groups,), in_specs=[each((2 * rows,...  50.7 us
  transfers between devices with their start and end apart: 79, of which 32 were waited for; matrix products, arithmetic and copies ran while one was open for 37% of the time, Pallas kernels for 17%

profile of v4, /device:TPU:0, one launch (start us, length us, event | category | flops | bytes accessed | tf_op | source)
XLA Modules:
  0.0 1244.4 jit_solution(5369154044165715523)
XLA Ops:
  66.1 25.0 %all-gather.16.cloned.1.call-done = bf16[1,768,2432]{2,1,0:T(8,128)(2,1)} async-done(((bf16[1,96,2432]{2,1,0:T(8,128)(2,1)}), bf16[1,768,2432]{2,1,0:T(8,128)(2,1)}) %all-gather.16.cloned.1.call-update) | async-done | bytes 3735568 | tf_op jit(solution)/shard_map/all_gather | solution.py:263
  95.9 61.5 %all-gather.10.cloned.1.call-done.refs_1_ = bf16[768,2304]{1,0:T(8,128)(2,1)} async-done(((bf16[96,2304]{1,0:T(8,128)(2,1)}), bf16[768,2304]{1,0:T(8,128)(2,1)}) %all-gather.10.cloned.1.call-update) | async-done | bytes 3538960 | tf_op jit(solution)/shard_map/all_gather | solution.py:263
  215.1 30.1 %attention_forward.2 = (bf16[1024,768]{1,0:T(8,128)(2,1)S(1)}, bf16[4,2048,96]{2,1,0:T(8,128)(2,1)}, bf16[4,1024,96]{2,1,0:T(8,128)(2,1)S(1)}, bf16[4,1024,96]{2,1,0:T(8,128)(2,1)S(1)}, f32[4,4,512]{2,1,0:T(4,128)S(1)}) custom-call(f32[1024,1536]{1,0:T(8,128)} %fusion.16.raw_ref, f32[1024,96]{1,0:T(8,128)S(1)} %copy.190.cos_ref, ...), custom_call_target="tpu_custom_call" | custom-call | flops 1000000 | bytes 1000000 | tf_op jit(solution)/shard_map/attention_forward/pallas_call | solution.py:118
  248.3 18.1 %collective-permute-done.4.refs_1_ = bf16[768,2304]{1,0:T(8,128)(2,1)} collective-permute-done((bf16[768,2304]{1,0:T(8,128)(2,1)}, bf16[768,2304]{1,0:T(8,128)(2,1)}, u32[]{:S(2)}, u32[]{:S(2)}) %collective-permute-start.4) | collective-permute-done | bytes 3538976 | tf_op jit(solution)/shard_map/ppermute | solution.py:245
  299.0 13.7 %fusion.43.refs_1_.refs_2_.refs_3_ = f32[1024,2048]{1,0:T(8,128)} fusion(bf16[1536,2048]{1,0:T(8,128)(2,1)} %all-gather.12.cloned.1.call-done.refs_4_.refs_5_, bf16[512,1536]{1,0:T(8,128)(2,1)} %collective-permute-done.7, bf16[512,1536]{1,0:T(8,128)(2,1)} %multiply_convert_fusion.2, pred[]{:T(512)S(6)} %eq.7), kind=kOutput, calls=%fused_computation.149 | convolution fusion | flops 6456606720 | bytes 17825792 | tf_op jit(solution)/shard_map/dot_general | solution.py:326
  330.9 12.6 %fusion.41.refs_2_.refs_3_ = f32[1024,2048]{1,0:T(8,128)} fusion(bf16[1536,2048]{1,0:T(8,128)(2,1)} %all-gather.12.cloned.1.call-done.refs_4_.refs_5_, bf16[512,1536]{1,0:T(8,128)(2,1)S(1)} %collective-permute-done.9, bf16[512,1536]{1,0:T(8,128)(2,1)} %tie.55, pred[]{:T(512)S(6)} %eq.7), kind=kOutput, calls=%fused_computation.147 | convolution fusion | flops 6456606720 | bytes 17825792 | tf_op jit(solution)/shard_map/dot_general | solution.py:326
  386.3 25.2 %collective-permute-done.12.refs_0_ = bf16[512,1536]{1,0:T(8,128)(2,1)S(1)} collective-permute-done((bf16[512,1536]{1,0:T(8,128)(2,1)}, bf16[512,1536]{1,0:T(8,128)(2,1)S(1)}, u32[]{:S(2)}, u32[]{:S(2)}) %collective-permute-start.12) | collective-permute-done | bytes 1572896 | tf_op jit(solution)/shard_map/ppermute | solution.py:245
  438.8 30.1 %attention_forward.3 = (bf16[1024,768]{1,0:T(8,128)(2,1)S(1)}, bf16[4,2048,96]{2,1,0:T(8,128)(2,1)}, bf16[4,1024,96]{2,1,0:T(8,128)(2,1)S(1)}, bf16[4,1024,96]{2,1,0:T(8,128)(2,1)S(1)}, f32[4,4,512]{2,1,0:T(4,128)S(1)}) custom-call(f32[1024,1536]{1,0:T(8,128)} %fusion.12.raw_ref, f32[1024,96]{1,0:T(8,128)S(1)} %copy.190.cos_ref, ...), custom_call_target="tpu_custom_call" | custom-call | flops 1000000 | bytes 1000000 | tf_op jit(solution)/shard_map/attention_forward/pallas_call | solution.py:118
  489.9 13.8 %fusion.39.refs_1_.refs_2_.refs_3_.refs_0_ = f32[1024,2048]{1,0:T(8,128)} fusion(bf16[1536,2048]{1,0:T(8,128)(2,1)} %all-gather.14.cloned.1.call-done.refs_4_.refs_5_, bf16[512,1536]{1,0:T(8,128)(2,1)} %collective-permute-done.17, bf16[512,1536]{1,0:T(8,128)(2,1)} %multiply_convert_fusion, pred[]{:T(512)S(6)} %eq.7), kind=kOutput, calls=%fused_computation.145 | convolution fusion | flops 6456606720 | bytes 17825792 | tf_op jit(solution)/shard_map/dot_general | solution.py:326
  513.0 12.4 collective-permute-done.20.refs_0_
  539.3 13.7 %fusion.36.refs_2_.refs_3_.refs_0_ = f32[1024,2048]{1,0:T(8,128)} fusion(bf16[1536,2048]{1,0:T(8,128)(2,1)} %all-gather.14.cloned.1.call-done.refs_4_.refs_5_, bf16[512,1536]{1,0:T(8,128)(2,1)} %copy-done.95, bf16[512,1536]{1,0:T(8,128)(2,1)} %tie.59, pred[]{:T(512)S(6)} %eq.7), kind=kOutput, calls=%fused_computation.142 | convolution fusion | flops 6456606720 | bytes 17825792 | tf_op jit(solution)/shard_map/dot_general | solution.py:326
  553.0 29.8 %mlp_backward.4 = (f32[1024,1536]{1,0:T(8,128)}, bf16[1536,1024]{1,0:T(8,128)(2,1)}, bf16[1536,1024]{1,0:T(8,128)(2,1)}, bf16[1024,1536]{1,0:T(8,128)(2,1)}) custom-call(bf16[1024,1536]{1,0:T(8,128)(2,1)} %maximum_select_fusion.8.refs_0_, bf16[1536,1024]{1,0:T(8,128)(2,1)} %copy.203.refs_1_, f32[1024,2048]{1,0:T(8,128)} %fusion.36.refs_2_.refs_3_.refs_0_, ...), custom_call_target="tpu_custom_call" | custom-call | flops 1000000 | bytes 1000000 | tf_op jit(solution)/shard_map/mlp_backward/pallas_call | solution.py:425
  595.3 30.4 %mlp_backward.5 = (f32[1024,1536]{1,0:T(8,128)}, bf16[1536,1024]{1,0:T(8,128)(2,1)}, bf16[1536,1024]{1,0:T(8,128)(2,1)}, bf16[1024,1536]{1,0:T(8,128)(2,1)}) custom-call(bf16[1024,1536]{1,0:T(8,128)(2,1)} %tie.60.refs_0_, bf16[1536,1024]{1,0:T(8,128)(2,1)} %copy.202.refs_2_.refs_1_, f32[1024,2048]{1,0:T(8,128)} %fusion.39.refs_1_.refs_2_.refs_3_.refs_0_, ...), custom_call_target="tpu_custom_call" | custom-call | flops 1000000 | bytes 1000000 | tf_op jit(solution)/shard_map/mlp_backward/pallas_call | solution.py:425
  659.2 25.4 %attention_backward.2 = bf16[1024,1536]{1,0:T(8,128)(2,1)} custom-call(bf16[4,2048,96]{2,1,0:T(8,128)(2,1)} %get-tuple-element.59.q_ref, bf16[4,1024,96]{2,1,0:T(8,128)(2,1)S(1)} %copy-done.10, bf16[4,1024,96]{2,1,0:T(8,128)(2,1)S(1)} %copy-done.12, f32[4,4,512]{2,1,0:T(4,128)S(1)} %get-tuple-element.62.lse_ref, ...), custom_call_target="tpu_custom_call" | custom-call | flops 1000000 | bytes 1000000 | tf_op jit(solution)/shard_map/attention_backward/pallas_call | solution.py:214
  746.1 14.9 %collective-permute-done.30.refs_0_ = bf16[512,1536]{1,0:T(8,128)(2,1)} collective-permute-done((bf16[512,1536]{1,0:T(8,128)(2,1)S(1)}, bf16[512,1536]{1,0:T(8,128)(2,1)}, u32[]{:S(2)}, u32[]{:S(2)}) %collective-permute-start.30) | collective-permute-done | bytes 1572896 | tf_op jit(solution)/shard_map/ppermute | solution.py:245
  768.2 29.7 %mlp_backward.6 = (f32[1024,1536]{1,0:T(8,128)}, bf16[1536,1024]{1,0:T(8,128)(2,1)}, bf16[1536,1024]{1,0:T(8,128)(2,1)}, bf16[1024,1536]{1,0:T(8,128)(2,1)}) custom-call(bf16[1024,1536]{1,0:T(8,128)(2,1)} %maximum_select_fusion.11.refs_0_, bf16[1536,1024]{1,0:T(8,128)(2,1)} %copy.196.refs_1_, f32[1024,2048]{1,0:T(8,128)} %fusion.41.refs_2_.refs_3_, ...), custom_call_target="tpu_custom_call" | custom-call | flops 1000000 | bytes 1000000 | tf_op jit(solution)/shard_map/mlp_backward/pallas_call | solution.py:425
  815.6 30.6 %mlp_backward.7 = (f32[1024,1536]{1,0:T(8,128)}, bf16[1536,1024]{1,0:T(8,128)(2,1)}, bf16[1536,1024]{1,0:T(8,128)(2,1)}, bf16[1024,1536]{1,0:T(8,128)(2,1)}) custom-call(bf16[1024,1536]{1,0:T(8,128)(2,1)} %tie.67.refs_0_, bf16[1536,1024]{1,0:T(8,128)(2,1)} %copy.195.refs_2_.refs_1_, f32[1024,2048]{1,0:T(8,128)} %fusion.43.refs_1_.refs_2_.refs_3_, ...), custom_call_target="tpu_custom_call" | custom-call | flops 1000000 | bytes 1000000 | tf_op jit(solution)/shard_map/mlp_backward/pallas_call | solution.py:425
  874.0 16.8 %collective-permute-done.29.refs_0_ = bf16[512,1536]{1,0:T(8,128)(2,1)S(1)} collective-permute-done((bf16[512,1536]{1,0:T(8,128)(2,1)}, bf16[512,1536]{1,0:T(8,128)(2,1)S(1)}, u32[]{:S(2)}, u32[]{:S(2)}) %collective-permute-start.29) | collective-permute-done | bytes 1572896 | tf_op jit(solution)/shard_map/ppermute | solution.py:245
  918.0 25.2 %attention_backward.3.refs_0_.refs_1_ = bf16[1024,1536]{1,0:T(8,128)(2,1)} custom-call(bf16[4,2048,96]{2,1,0:T(8,128)(2,1)} %get-tuple-element.68.q_ref, bf16[4,1024,96]{2,1,0:T(8,128)(2,1)S(1)} %copy-done.6, bf16[4,1024,96]{2,1,0:T(8,128)(2,1)S(1)} %copy-done.8, f32[4,4,512]{2,1,0:T(4,128)S(1)} %get-tuple-element.71.lse_ref, bf16[1024,768]{1,0:T(8,128)(2,1)S(1)} %copy-done, ...), custom_call_target="tpu_custom_call" | custom-call | flops 1000000 | bytes 1000000 | tf_op jit(solution)/shard_map/attention_backward/pallas_call | solution.py:214
  998.7 20.3 %collective-permute-done.41.refs_1_ = bf16[2,2,128,1536]{3,2,1,0:T(8,128)(2,1)} collective-permute-done((bf16[2,2,128,1536]{3,2,1,0:T(8,128)(2,1)}, bf16[2,2,128,1536]{3,2,1,0:T(8,128)(2,1)}, u32[]{:S(2)}, u32[]{:S(2)}) %collective-permute-start.41) | collective-permute-done | bytes 1572896 | tf_op jit(solution)/shard_map/ppermute | solution.py:273
  1035.5 22.8 %collective-permute-done.42.refs_1_ = bf16[2,192,2048]{2,1,0:T(8,128)(2,1)S(1)} collective-permute-done((bf16[2,192,2048]{2,1,0:T(8,128)(2,1)}, bf16[2,192,2048]{2,1,0:T(8,128)(2,1)S(1)}, u32[]{:S(2)}, u32[]{:S(2)}) %collective-permute-start.42) | collective-permute-done | bytes 1572896 | tf_op jit(solution)/shard_map/ppermute | solution.py:273
  1071.5 24.2 %collective-permute-done.43.refs_1_ = bf16[2,128,1536]{2,1,0:T(8,128)(2,1)S(1)} collective-permute-done((bf16[2,128,1536]{2,1,0:T(8,128)(2,1)}, bf16[2,128,1536]{2,1,0:T(8,128)(2,1)S(1)}, u32[]{:S(2)}, u32[]{:S(2)}) %collective-permute-start.43) | collective-permute-done | bytes 786464 | tf_op jit(solution)/shard_map/ppermute | solution.py:273
  1124.7 21.4 %collective-permute-done.56.refs_0_ = bf16[192,4352]{1,0:T(8,128)(2,1)S(1)} collective-permute-done((bf16[192,4352]{1,0:T(8,128)(2,1)}, bf16[192,4352]{1,0:T(8,128)(2,1)S(1)}, u32[]{:S(2)}, u32[]{:S(2)}) %collective-permute-start.56) | collective-permute-done | bytes 1671200 | tf_op jit(solution)/shard_map/ppermute | solution.py:245
  1163.5 16.3 %collective-permute-done.51.refs_0_ = bf16[192,2048]{1,0:T(8,128)(2,1)S(1)} collective-permute-done((bf16[192,2048]{1,0:T(8,128)(2,1)}, bf16[192,2048]{1,0:T(8,128)(2,1)S(1)}, u32[]{:S(2)}, u32[]{:S(2)}) %collective-permute-start.51) | collective-permute-done | bytes 786464 | tf_op jit(solution)/shard_map/ppermute | solution.py:245
  (663 shorter events, 664.2 us)
Async XLA Ops:
  7.2 83.9 %all-gather.16.cloned.1.call-start = ((), (), s32[]{:S(2)}) async-start(), calls=%async_computation.7 | async-start | bytes 4202496 | tf_op jit(solution)/shard_map/all_gather | solution.py:263
  20.6 136.9 %all-gather.10.cloned.1.call-start = ((), (), s32[]{:S(2)}) async-start(), calls=%async_computation.2 | async-start | bytes 3981312 | tf_op jit(solution)/shard_map/all_gather | solution.py:263
  23.9 40.9 %collective-permute-start = (bf16[2,256,1536]{2,1,0:T(8,128)(2,1)}, bf16[2,256,1536]{2,1,0:T(8,128)(2,1)S(1)}, u32[]{:S(2)}, u32[]{:S(2)}) collective-permute-start(bf16[2,256,1536]{2,1,0:T(8,128)(2,1)} %pad_maximum_fusion.2), channel_id=1, source_target_pairs={{0,2},{2,0},{1,3},{3,1},{4,6},{6,4},{5,7},{7,5},{8,10},{10,8},{9,1... | collective-permute-start | bytes 4718600 | tf_op jit(solution)/shard_map/ppermute | solution.py:245
  66.0 233.0 %all-gather.12.cloned.1.call-start = ((), (), s32[]{:S(2)}) async-start(), calls=%async_computation.3 | async-start | bytes 7077888 | tf_op jit(solution)/shard_map/all_gather | solution.py:263
  94.5 66.7 %collective-permute-start.1 = (bf16[768,1664]{1,0:T(8,128)(2,1)}, bf16[768,1664]{1,0:T(8,128)(2,1)S(1)}, u32[]{:S(2)}, u32[]{:S(2)}) collective-permute-start(bf16[768,1664]{1,0:T(8,128)(2,1)} %slice.146), channel_id=1, source_target_pairs={{0,2},{2,0},{1,3},{3,1},{4,6},{6,4},{5,7},{7,5},{8,10},{10,8},{9,1... | collective-permute-start | bytes 7667720 | tf_op jit(solution)/shard_map/ppermute | solution.py:245
  157.5 191.9 %all-gather.18.cloned.1.call-start = ((), (), s32[]{:S(2)}) async-start(), calls=%async_computation.8 | async-start | bytes 3538944 | tf_op jit(solution)/shard_map/all_gather | solution.py:263
  189.7 76.7 %collective-permute-start.4 = (bf16[768,2304]{1,0:T(8,128)(2,1)}, bf16[768,2304]{1,0:T(8,128)(2,1)}, u32[]{:S(2)}, u32[]{:S(2)}) collective-permute-start(bf16[768,2304]{1,0:T(8,128)(2,1)} %tie.52), channel_id=1, source_target_pairs={{0,2},{2,0},{1,3},{3,1},{4,6},{6,4},{5,7},{7,5},{8,10},{10,8},{9,1... | collective-permute-start | bytes 10616840 | tf_op jit(solution)/shard_map/ppermute | solution.py:245
  202.2 64.2 %collective-permute-start.5 = (bf16[768,768]{1,0:T(8,128)(2,1)}, bf16[768,768]{1,0:T(8,128)(2,1)}, u32[]{:S(2)}, u32[]{:S(2)}) collective-permute-start(bf16[768,768]{1,0:T(8,128)(2,1)} %get-tuple-element.134), channel_id=1, source_target_pairs={{0,1},{1,0},{2,3},{3,2},{4,5},{5,4},{6,7},{7,6},{8,9},{9,8},{10,11... | collective-permute-start | bytes 3538952 | tf_op jit(solution)/shard_map/ppermute | solution.py:241
  288.0 201.6 %all-gather.14.cloned.1.call-start = ((), (), s32[]{:S(2)}) async-start(), calls=%async_computation.4 | async-start | bytes 7077888 | tf_op jit(solution)/shard_map/all_gather | solution.py:263
  360.2 192.7 %all-gather.20.cloned.1.call-start = ((), (), s32[]{:S(2)}) async-start(), calls=%async_computation.9 | async-start | bytes 3538944 | tf_op jit(solution)/shard_map/all_gather | solution.py:263
  420.5 51.6 %collective-permute-start.14 = (bf16[512,1536]{1,0:T(8,128)(2,1)S(1)}, bf16[512,1536]{1,0:T(8,128)(2,1)S(1)}, u32[]{:S(2)}, u32[]{:S(2)}) collective-permute-start(bf16[512,1536]{1,0:T(8,128)(2,1)S(1)} %maximum_select_fusion.22), channel_id=1, source_target_pairs={{0,2},{2,0},{1,3},{3,1},{4,6},{6,4},{5,7},{7,5},{8,10},{10,8},{9,1... | collective-permute-start | bytes 4718600 | tf_op jit(solution)/shard_map/ppermute | solution.py:245
  428.8 44.5 %collective-permute-start.15 = (bf16[768,768]{1,0:T(8,128)(2,1)}, bf16[768,768]{1,0:T(8,128)(2,1)}, u32[]{:S(2)}, u32[]{:S(2)}) collective-permute-start(bf16[768,768]{1,0:T(8,128)(2,1)} %get-tuple-element.132), channel_id=1, source_target_pairs={{0,1},{1,0},{2,3},{3,2},{4,5},{5,4},{6,7},{7,6},{8,9},{9,8},{10,11... | collective-permute-start | bytes 3538952 | tf_op jit(solution)/shard_map/ppermute | solution.py:241
  488.1 580.0 %reduce-scatter.3.cloned.1.call-start = ((), (), s32[]{:S(2)}) async-start(), calls=%async_computation.5 | async-start | bytes 3538944 | tf_op jit(solution)/shard_map/reduce_scatter | solution.py:821
  641.4 465.1 %reduce-scatter.5.cloned.1.call-start = ((), (), s32[]{:S(2)}) async-start(), calls=%async_computation.6 | async-start | bytes 15040512 | tf_op jit(solution)/shard_map/reduce_scatter | solution.py:823
  652.0 51.7 %collective-permute-start.55 = (bf16[768,768]{1,0:T(8,128)(2,1)}, bf16[768,768]{1,0:T(8,128)(2,1)}, u32[]{:S(2)}, u32[]{:S(2)}) collective-permute-start(bf16[768,768]{1,0:T(8,128)(2,1)} %get-tuple-element.126), channel_id=1, source_target_pairs={{0,1},{1,0},{2,3},{3,2},{4,5},{5,4},{6,7},{7,6},{8,9},{9,8},{10,11... | collective-permute-start | bytes 3538952 | tf_op jit(solution)/shard_map/ppermute | solution.py:241
  808.2 38.0 %collective-permute-start.33 = (bf16[512,1536]{1,0:T(8,128)(2,1)}, bf16[512,1536]{1,0:T(8,128)(2,1)}, u32[]{:S(2)}, u32[]{:S(2)}) collective-permute-start(bf16[512,1536]{1,0:T(8,128)(2,1)} %add_convert_fusion.refs_1_), channel_id=1, source_target_pairs={{0,2},{2,0},{1,3},{3,1},{4,6},{6,4},{5,7},{7,5},{8,10},{10,8},{9,1... | collective-permute-start | bytes 4718600 | tf_op jit(solution)/shard_map/ppermute | solution.py:245
  812.0 38.3 %collective-permute-start.28 = (bf16[512,1536]{1,0:T(8,128)(2,1)}, bf16[512,1536]{1,0:T(8,128)(2,1)}, u32[]{:S(2)}, u32[]{:S(2)}) collective-permute-start(bf16[512,1536]{1,0:T(8,128)(2,1)} %dynamic-slice_convert_fusion.3), channel_id=1, source_target_pairs={{0,1},{1,0},{2,3},{3,2},{4,5},{5,4},{6,7},{7,6},{8,9},{9,8},{10,11... | collective-permute-start | bytes 4718600 | tf_op jit(solution)/shard_map/ppermute | solution.py:241
  866.0 88.8 %collective-permute-start.40 = (bf16[2,2,192,2048]{3,2,1,0:T(8,128)(2,1)}, bf16[2,2,192,2048]{3,2,1,0:T(8,128)(2,1)}, u32[]{:S(2)}, u32[]{:S(2)}) collective-permute-start(bf16[2,2,192,2048]{3,2,1,0:T(8,128)(2,1)} %dynamic-slice_bitcast_fusion), channel_id=1, source_target_pairs={{0,4},{4,0},{8,12},{12,8},{16,20},{20,16},{24,28},{28,24},{1,5},{5... | collective-permute-start | bytes 9437192 | tf_op jit(solution)/shard_map/ppermute | solution.py:273
  986.9 71.4 %collective-permute-start.42 = (bf16[2,192,2048]{2,1,0:T(8,128)(2,1)}, bf16[2,192,2048]{2,1,0:T(8,128)(2,1)S(1)}, u32[]{:S(2)}, u32[]{:S(2)}) collective-permute-start(bf16[2,192,2048]{2,1,0:T(8,128)(2,1)} %dynamic-slice_bitcast_fusion.1), channel_id=1, source_target_pairs={{0,16},{4,20},{8,24},{12,28},{16,0},{20,4},{24,8},{28,12},{1,17},{... | collective-permute-start | bytes 4718600 | tf_op jit(solution)/shard_map/ppermute | solution.py:273
  1027.5 74.7 %collective-permute-start.46 = (bf16[768,1664]{1,0:T(8,128)(2,1)}, bf16[768,1664]{1,0:T(8,128)(2,1)}, u32[]{:S(2)}, u32[]{:S(2)}) collective-permute-start(bf16[768,1664]{1,0:T(8,128)(2,1)} %tie.76), channel_id=1, source_target_pairs={{0,2},{2,0},{1,3},{3,1},{4,6},{6,4},{5,7},{7,5},{8,10},{10,8},{9,1... | collective-permute-start | bytes 7667720 | tf_op jit(solution)/shard_map/ppermute | solution.py:245
  1068.1 79.2 %collective-permute-start.54 = (bf16[128,1536]{1,0:T(8,128)(2,1)}, bf16[128,1536]{1,0:T(8,128)(2,1)}, u32[]{:S(2)}, u32[]{:S(2)}) collective-permute-start(bf16[128,1536]{1,0:T(8,128)(2,1)} %reduce-scatter.3.cloned.1.call-done.refs_4_), channel_id=1, source_target_pairs={{0,2},{2,0},{1,3},{3,1},{4,6},{6,4},{5,7},{7,5},{8,10},{10,8},{9,1... | collective-permute-start | bytes 1179656 | tf_op jit(solution)/shard_map/ppermute | solution.py:245
  1106.4 39.6 %collective-permute-start.56 = (bf16[192,4352]{1,0:T(8,128)(2,1)}, bf16[192,4352]{1,0:T(8,128)(2,1)S(1)}, u32[]{:S(2)}, u32[]{:S(2)}) collective-permute-start(bf16[192,4352]{1,0:T(8,128)(2,1)} %reduce-scatter.5.cloned.1.call-done.refs_0_), channel_id=1, source_target_pairs={{0,2},{2,0},{1,3},{3,1},{4,6},{6,4},{5,7},{7,5},{8,10},{10,8},{9,1... | collective-permute-start | bytes 5013512 | tf_op jit(solution)/shard_map/ppermute | solution.py:245
  1112.7 42.3 %collective-permute-start.52 = (bf16[2,2,96,1664]{3,2,1,0:T(8,128)(2,1)}, bf16[2,2,96,1664]{3,2,1,0:T(8,128)(2,1)}, u32[]{:S(2)}, u32[]{:S(2)}) collective-permute-start(bf16[2,2,96,1664]{3,2,1,0:T(8,128)(2,1)} %bitcast.266), channel_id=1, source_target_pairs={{0,4},{4,0},{8,12},{12,8},{16,20},{20,16},{24,28},{28,24},{1,5},{5... | collective-permute-start | bytes 3833864 | tf_op jit(solution)/shard_map/ppermute | solution.py:273
  1122.5 63.8 %collective-permute-start.39 = (bf16[256,1536]{1,0:T(8,128)(2,1)}, bf16[256,1536]{1,0:T(8,128)(2,1)}, u32[]{:S(2)}, u32[]{:S(2)}) collective-permute-start(bf16[256,1536]{1,0:T(8,128)(2,1)} %fusion.35), channel_id=1, source_target_pairs={{0,2},{2,0},{1,3},{3,1},{4,6},{6,4},{5,7},{7,5},{8,10},{10,8},{9,1... | collective-permute-start | bytes 2359304 | tf_op jit(solution)/shard_map/ppermute | solution.py:245
  (188 other events, 2231.7 us)
Sparse Core Ops, SparseCore 0:
  20.7 70.3 all-gather.15
  93.8 63.5 all-gather.9
  159.7 97.5 all-gather.11
  288.1 61.2 all-gather.17
  360.4 97.7 all-gather.13
  488.2 58.7 all-gather.19
  641.5 72.7 reduce-scatter.2
  718.0 224.7 reduce-scatter.4

commit v5 on v4

--- a/solution.py
+++ b/solution.py
@@ -796,9 +796,9 @@
         gate_up = finish(add(gate_up))
         qkv = send(qkv_near + take(qkv_far), 0, "x")
         down = finish(add(down))
-        earlier = [[four_taken(piece) for piece in pieces] for pieces in earlier]
         out = finish(add(out))
         qkv = send(add(qkv), 1, "z")
+        earlier = [[four_taken(piece) for piece in pieces] for pieces in earlier]
         gate_up = four_taken(gate_up)
         down = four_taken(down)
         got_grad = take(swapped(grad))

time: 1250 us -> 1260 us (level)
  waiting for transfers between devices: 374 us -> 390 us
    unnamed x281 -> x283, local copies, waits for them, and re-layouts: 74.9 us -> 74.5 us
  transfers between devices with their start and end apart: 79 -> 79, of which waited for: 32 -> 33; matrix products, arithmetic and copies ran while one was open for 37% -> 37% of each run, Pallas kernels for 17% -> 17%
where the time goes in v5:
time: 1260 us
  waiting for transfers between devices  390 us (31%)
  Pallas kernels  250 us (20%)
  local copies, waits for them, and re-layouts  206 us (16%)
  matrix products  185 us (15%)
  other arithmetic  167 us (13%)
  starting transfers between devices  43.3 us (3%)
  between operations  16.1 us (1%)
    ppermute x21, waiting for transfers between devices, other_y(): return lax.ppermute(value, 'seq', Y_SWAP)  174 us
    dot_general x12, matrix products, dot(): return jnp.dot(left, right, preferred_element_type=jnp.float32)  124 us
    pallas_call x4, Pallas kernels, mlp_back(): pl.pallas_call(mlp_back_kernel, grid=(steps,), in_specs=[whole(grad.shape...  121 us
    ppermute x12, waiting for transfers between devices, dp_swap(): return lax.ppermute(value, 'dp', [(d, d ^ 1 << bit) for d in range(size)])  94.4 us
    all_gather x6, waiting for transfers between devices, gather_dp(): return lax.all_gather(piece, 'dp', axis=0, tiled=True)  92.2 us
    unnamed x283, local copies, waits for them, and re-layouts  74.5 us
    pallas_call x2, Pallas kernels, attend_forward(): pl.pallas_call(forward_kernel, grid=(groups,), in_specs=[whole(raw.shape)...  60.2 us
    pallas_call x2, Pallas kernels, attend_backward(): pl.pallas_call(backward_kernel, grid=(groups,), in_specs=[each((2 * rows,...  50.7 us
  transfers between devices with their start and end apart: 79, of which 33 were waited for; matrix products, arithmetic and copies ran while one was open for 37% of the time, Pallas kernels for 17%

profile of v5, /device:TPU:0, one launch (start us, length us, event | category | flops | bytes accessed | tf_op | source)
XLA Modules:
  0.0 1257.4 jit_solution(8294900901293986350)
XLA Ops:
  66.0 25.0 %all-gather.16.cloned.1.call-done = bf16[1,768,2432]{2,1,0:T(8,128)(2,1)} async-done(((bf16[1,96,2432]{2,1,0:T(8,128)(2,1)}), bf16[1,768,2432]{2,1,0:T(8,128)(2,1)}) %all-gather.16.cloned.1.call-update) | async-done | bytes 3735568 | tf_op jit(solution)/shard_map/all_gather | solution.py:263
  95.9 61.5 %all-gather.10.cloned.1.call-done.refs_1_ = bf16[768,2304]{1,0:T(8,128)(2,1)} async-done(((bf16[96,2304]{1,0:T(8,128)(2,1)}), bf16[768,2304]{1,0:T(8,128)(2,1)}) %all-gather.10.cloned.1.call-update) | async-done | bytes 3538960 | tf_op jit(solution)/shard_map/all_gather | solution.py:263
  215.1 30.1 %attention_forward.2 = (bf16[1024,768]{1,0:T(8,128)(2,1)S(1)}, bf16[4,2048,96]{2,1,0:T(8,128)(2,1)}, bf16[4,1024,96]{2,1,0:T(8,128)(2,1)S(1)}, bf16[4,1024,96]{2,1,0:T(8,128)(2,1)S(1)}, f32[4,4,512]{2,1,0:T(4,128)S(1)}) custom-call(f32[1024,1536]{1,0:T(8,128)} %fusion.16.raw_ref, f32[1024,96]{1,0:T(8,128)S(1)} %copy.190.cos_ref, ...), custom_call_target="tpu_custom_call" | custom-call | flops 1000000 | bytes 1000000 | tf_op jit(solution)/shard_map/attention_forward/pallas_call | solution.py:118
  248.3 18.1 %collective-permute-done.4.refs_1_ = bf16[768,2304]{1,0:T(8,128)(2,1)} collective-permute-done((bf16[768,2304]{1,0:T(8,128)(2,1)}, bf16[768,2304]{1,0:T(8,128)(2,1)}, u32[]{:S(2)}, u32[]{:S(2)}) %collective-permute-start.4) | collective-permute-done | bytes 3538976 | tf_op jit(solution)/shard_map/ppermute | solution.py:245
  299.0 13.8 %fusion.43.refs_1_.refs_2_.refs_3_ = f32[1024,2048]{1,0:T(8,128)} fusion(bf16[1536,2048]{1,0:T(8,128)(2,1)} %all-gather.12.cloned.1.call-done.refs_4_.refs_5_, bf16[512,1536]{1,0:T(8,128)(2,1)} %collective-permute-done.7, bf16[512,1536]{1,0:T(8,128)(2,1)} %multiply_convert_fusion.2, pred[]{:T(512)S(6)} %eq.7), kind=kOutput, calls=%fused_computation.149 | convolution fusion | flops 6456606720 | bytes 17825792 | tf_op jit(solution)/shard_map/dot_general | solution.py:326
  330.9 12.9 %fusion.41.refs_2_.refs_3_ = f32[1024,2048]{1,0:T(8,128)} fusion(bf16[1536,2048]{1,0:T(8,128)(2,1)} %all-gather.12.cloned.1.call-done.refs_4_.refs_5_, bf16[512,1536]{1,0:T(8,128)(2,1)S(1)} %collective-permute-done.9, bf16[512,1536]{1,0:T(8,128)(2,1)} %tie.55, pred[]{:T(512)S(6)} %eq.7), kind=kOutput, calls=%fused_computation.147 | convolution fusion | flops 6456606720 | bytes 17825792 | tf_op jit(solution)/shard_map/dot_general | solution.py:326
  386.3 25.3 %collective-permute-done.12.refs_0_ = bf16[512,1536]{1,0:T(8,128)(2,1)S(1)} collective-permute-done((bf16[512,1536]{1,0:T(8,128)(2,1)}, bf16[512,1536]{1,0:T(8,128)(2,1)S(1)}, u32[]{:S(2)}, u32[]{:S(2)}) %collective-permute-start.12) | collective-permute-done | bytes 1572896 | tf_op jit(solution)/shard_map/ppermute | solution.py:245
  438.8 30.1 %attention_forward.3 = (bf16[1024,768]{1,0:T(8,128)(2,1)S(1)}, bf16[4,2048,96]{2,1,0:T(8,128)(2,1)}, bf16[4,1024,96]{2,1,0:T(8,128)(2,1)S(1)}, bf16[4,1024,96]{2,1,0:T(8,128)(2,1)S(1)}, f32[4,4,512]{2,1,0:T(4,128)S(1)}) custom-call(f32[1024,1536]{1,0:T(8,128)} %fusion.12.raw_ref, f32[1024,96]{1,0:T(8,128)S(1)} %copy.190.cos_ref, ...), custom_call_target="tpu_custom_call" | custom-call | flops 1000000 | bytes 1000000 | tf_op jit(solution)/shard_map/attention_forward/pallas_call | solution.py:118
  489.8 14.0 %fusion.39.refs_1_.refs_2_.refs_3_.refs_0_ = f32[1024,2048]{1,0:T(8,128)} fusion(bf16[1536,2048]{1,0:T(8,128)(2,1)} %all-gather.14.cloned.1.call-done.refs_4_.refs_5_, bf16[512,1536]{1,0:T(8,128)(2,1)} %collective-permute-done.17, bf16[512,1536]{1,0:T(8,128)(2,1)} %multiply_convert_fusion, pred[]{:T(512)S(6)} %eq.7), kind=kOutput, calls=%fused_computation.145 | convolution fusion | flops 6456606720 | bytes 17825792 | tf_op jit(solution)/shard_map/dot_general | solution.py:326
  513.0 12.2 collective-permute-done.20.refs_0_
  539.0 13.7 %fusion.36.refs_2_.refs_3_.refs_0_ = f32[1024,2048]{1,0:T(8,128)} fusion(bf16[1536,2048]{1,0:T(8,128)(2,1)} %all-gather.14.cloned.1.call-done.refs_4_.refs_5_, bf16[512,1536]{1,0:T(8,128)(2,1)} %copy-done.98, bf16[512,1536]{1,0:T(8,128)(2,1)} %tie.59, pred[]{:T(512)S(6)} %eq.7), kind=kOutput, calls=%fused_computation.142 | convolution fusion | flops 6456606720 | bytes 17825792 | tf_op jit(solution)/shard_map/dot_general | solution.py:326
  552.6 29.8 %mlp_backward.4 = (f32[1024,1536]{1,0:T(8,128)}, bf16[1536,1024]{1,0:T(8,128)(2,1)}, bf16[1536,1024]{1,0:T(8,128)(2,1)}, bf16[1024,1536]{1,0:T(8,128)(2,1)}) custom-call(bf16[1024,1536]{1,0:T(8,128)(2,1)} %maximum_select_fusion.8.refs_0_, bf16[1536,1024]{1,0:T(8,128)(2,1)} %copy.203.refs_1_, f32[1024,2048]{1,0:T(8,128)} %fusion.36.refs_2_.refs_3_.refs_0_, ...), custom_call_target="tpu_custom_call" | custom-call | flops 1000000 | bytes 1000000 | tf_op jit(solution)/shard_map/mlp_backward/pallas_call | solution.py:425
  595.1 30.4 %mlp_backward.5 = (f32[1024,1536]{1,0:T(8,128)}, bf16[1536,1024]{1,0:T(8,128)(2,1)}, bf16[1536,1024]{1,0:T(8,128)(2,1)}, bf16[1024,1536]{1,0:T(8,128)(2,1)}) custom-call(bf16[1024,1536]{1,0:T(8,128)(2,1)} %tie.60.refs_0_, bf16[1536,1024]{1,0:T(8,128)(2,1)} %copy.202.refs_2_.refs_1_, f32[1024,2048]{1,0:T(8,128)} %fusion.39.refs_1_.refs_2_.refs_3_.refs_0_, ...), custom_call_target="tpu_custom_call" | custom-call | flops 1000000 | bytes 1000000 | tf_op jit(solution)/shard_map/mlp_backward/pallas_call | solution.py:425
  658.9 25.4 %attention_backward.2 = bf16[1024,1536]{1,0:T(8,128)(2,1)} custom-call(bf16[4,2048,96]{2,1,0:T(8,128)(2,1)} %get-tuple-element.59.q_ref, bf16[4,1024,96]{2,1,0:T(8,128)(2,1)S(1)} %copy-done.10, bf16[4,1024,96]{2,1,0:T(8,128)(2,1)S(1)} %copy-done.12, f32[4,4,512]{2,1,0:T(4,128)S(1)} %get-tuple-element.62.lse_ref, ...), custom_call_target="tpu_custom_call" | custom-call | flops 1000000 | bytes 1000000 | tf_op jit(solution)/shard_map/attention_backward/pallas_call | solution.py:214
  745.7 15.2 %collective-permute-done.30.refs_0_ = bf16[512,1536]{1,0:T(8,128)(2,1)} collective-permute-done((bf16[512,1536]{1,0:T(8,128)(2,1)S(1)}, bf16[512,1536]{1,0:T(8,128)(2,1)}, u32[]{:S(2)}, u32[]{:S(2)}) %collective-permute-start.30) | collective-permute-done | bytes 1572896 | tf_op jit(solution)/shard_map/ppermute | solution.py:245
  768.1 29.7 %mlp_backward.6 = (f32[1024,1536]{1,0:T(8,128)}, bf16[1536,1024]{1,0:T(8,128)(2,1)}, bf16[1536,1024]{1,0:T(8,128)(2,1)}, bf16[1024,1536]{1,0:T(8,128)(2,1)}) custom-call(bf16[1024,1536]{1,0:T(8,128)(2,1)} %maximum_select_fusion.11.refs_0_, bf16[1536,1024]{1,0:T(8,128)(2,1)} %copy.196.refs_1_, f32[1024,2048]{1,0:T(8,128)} %fusion.41.refs_2_.refs_3_, ...), custom_call_target="tpu_custom_call" | custom-call | flops 1000000 | bytes 1000000 | tf_op jit(solution)/shard_map/mlp_backward/pallas_call | solution.py:425
  815.4 30.6 %mlp_backward.7 = (f32[1024,1536]{1,0:T(8,128)}, bf16[1536,1024]{1,0:T(8,128)(2,1)}, bf16[1536,1024]{1,0:T(8,128)(2,1)}, bf16[1024,1536]{1,0:T(8,128)(2,1)}) custom-call(bf16[1024,1536]{1,0:T(8,128)(2,1)} %tie.67.refs_0_, bf16[1536,1024]{1,0:T(8,128)(2,1)} %copy.195.refs_2_.refs_1_, f32[1024,2048]{1,0:T(8,128)} %fusion.43.refs_1_.refs_2_.refs_3_, ...), custom_call_target="tpu_custom_call" | custom-call | flops 1000000 | bytes 1000000 | tf_op jit(solution)/shard_map/mlp_backward/pallas_call | solution.py:425
  874.2 16.6 %collective-permute-done.29.refs_0_ = bf16[512,1536]{1,0:T(8,128)(2,1)S(1)} collective-permute-done((bf16[512,1536]{1,0:T(8,128)(2,1)}, bf16[512,1536]{1,0:T(8,128)(2,1)S(1)}, u32[]{:S(2)}, u32[]{:S(2)}) %collective-permute-start.29) | collective-permute-done | bytes 1572896 | tf_op jit(solution)/shard_map/ppermute | solution.py:245
  918.3 25.2 %attention_backward.3.refs_0_.refs_1_ = bf16[1024,1536]{1,0:T(8,128)(2,1)} custom-call(bf16[4,2048,96]{2,1,0:T(8,128)(2,1)} %get-tuple-element.68.q_ref, bf16[4,1024,96]{2,1,0:T(8,128)(2,1)S(1)} %copy-done.6, bf16[4,1024,96]{2,1,0:T(8,128)(2,1)S(1)} %copy-done.8, f32[4,4,512]{2,1,0:T(4,128)S(1)} %get-tuple-element.71.lse_ref, bf16[1024,768]{1,0:T(8,128)(2,1)S(1)} %copy-done, ...), custom_call_target="tpu_custom_call" | custom-call | flops 1000000 | bytes 1000000 | tf_op jit(solution)/shard_map/attention_backward/pallas_call | solution.py:214
  998.3 21.2 %collective-permute-done.41.refs_1_ = bf16[2,2,128,1536]{3,2,1,0:T(8,128)(2,1)} collective-permute-done((bf16[2,2,128,1536]{3,2,1,0:T(8,128)(2,1)}, bf16[2,2,128,1536]{3,2,1,0:T(8,128)(2,1)}, u32[]{:S(2)}, u32[]{:S(2)}) %collective-permute-start.41) | collective-permute-done | bytes 1572896 | tf_op jit(solution)/shard_map/ppermute | solution.py:273
  1035.1 23.5 %collective-permute-done.42.refs_1_ = bf16[2,192,2048]{2,1,0:T(8,128)(2,1)S(1)} collective-permute-done((bf16[2,192,2048]{2,1,0:T(8,128)(2,1)}, bf16[2,192,2048]{2,1,0:T(8,128)(2,1)S(1)}, u32[]{:S(2)}, u32[]{:S(2)}) %collective-permute-start.42) | collective-permute-done | bytes 1572896 | tf_op jit(solution)/shard_map/ppermute | solution.py:273
  1071.1 24.2 %collective-permute-done.43.refs_1_ = bf16[2,128,1536]{2,1,0:T(8,128)(2,1)S(1)} collective-permute-done((bf16[2,128,1536]{2,1,0:T(8,128)(2,1)}, bf16[2,128,1536]{2,1,0:T(8,128)(2,1)S(1)}, u32[]{:S(2)}, u32[]{:S(2)}) %collective-permute-start.43) | collective-permute-done | bytes 786464 | tf_op jit(solution)/shard_map/ppermute | solution.py:273
  1148.8 27.8 %collective-permute-done.54.refs_0_ = bf16[192,4352]{1,0:T(8,128)(2,1)S(1)} collective-permute-done((bf16[192,4352]{1,0:T(8,128)(2,1)}, bf16[192,4352]{1,0:T(8,128)(2,1)S(1)}, u32[]{:S(2)}, u32[]{:S(2)}) %collective-permute-start.54) | collective-permute-done | bytes 1671200 | tf_op jit(solution)/shard_map/ppermute | solution.py:245
  1178.5 15.0 %collective-permute-done.51.refs_0_ = bf16[192,2048]{1,0:T(8,128)(2,1)} collective-permute-done((bf16[192,2048]{1,0:T(8,128)(2,1)}, bf16[192,2048]{1,0:T(8,128)(2,1)}, u32[]{:S(2)}, u32[]{:S(2)}) %collective-permute-start.51) | collective-permute-done | bytes 786464 | tf_op jit(solution)/shard_map/ppermute | solution.py:245
  (665 shorter events, 669.9 us)
Async XLA Ops:
  7.2 83.9 %all-gather.16.cloned.1.call-start = ((), (), s32[]{:S(2)}) async-start(), calls=%async_computation.7 | async-start | bytes 4202496 | tf_op jit(solution)/shard_map/all_gather | solution.py:263
  20.6 136.9 %all-gather.10.cloned.1.call-start = ((), (), s32[]{:S(2)}) async-start(), calls=%async_computation.2 | async-start | bytes 3981312 | tf_op jit(solution)/shard_map/all_gather | solution.py:263
  23.9 40.9 %collective-permute-start = (bf16[2,256,1536]{2,1,0:T(8,128)(2,1)}, bf16[2,256,1536]{2,1,0:T(8,128)(2,1)S(1)}, u32[]{:S(2)}, u32[]{:S(2)}) collective-permute-start(bf16[2,256,1536]{2,1,0:T(8,128)(2,1)} %pad_maximum_fusion.2), channel_id=1, source_target_pairs={{0,2},{2,0},{1,3},{3,1},{4,6},{6,4},{5,7},{7,5},{8,10},{10,8},{9,1... | collective-permute-start | bytes 4718600 | tf_op jit(solution)/shard_map/ppermute | solution.py:245
  66.0 233.0 %all-gather.12.cloned.1.call-start = ((), (), s32[]{:S(2)}) async-start(), calls=%async_computation.3 | async-start | bytes 7077888 | tf_op jit(solution)/shard_map/all_gather | solution.py:263
  94.4 66.7 %collective-permute-start.1 = (bf16[768,1664]{1,0:T(8,128)(2,1)}, bf16[768,1664]{1,0:T(8,128)(2,1)S(1)}, u32[]{:S(2)}, u32[]{:S(2)}) collective-permute-start(bf16[768,1664]{1,0:T(8,128)(2,1)} %slice.146), channel_id=1, source_target_pairs={{0,2},{2,0},{1,3},{3,1},{4,6},{6,4},{5,7},{7,5},{8,10},{10,8},{9,1... | collective-permute-start | bytes 7667720 | tf_op jit(solution)/shard_map/ppermute | solution.py:245
  157.5 191.9 %all-gather.18.cloned.1.call-start = ((), (), s32[]{:S(2)}) async-start(), calls=%async_computation.8 | async-start | bytes 3538944 | tf_op jit(solution)/shard_map/all_gather | solution.py:263
  189.7 76.7 %collective-permute-start.4 = (bf16[768,2304]{1,0:T(8,128)(2,1)}, bf16[768,2304]{1,0:T(8,128)(2,1)}, u32[]{:S(2)}, u32[]{:S(2)}) collective-permute-start(bf16[768,2304]{1,0:T(8,128)(2,1)} %tie.52), channel_id=1, source_target_pairs={{0,2},{2,0},{1,3},{3,1},{4,6},{6,4},{5,7},{7,5},{8,10},{10,8},{9,1... | collective-permute-start | bytes 10616840 | tf_op jit(solution)/shard_map/ppermute | solution.py:245
  202.2 64.2 %collective-permute-start.5 = (bf16[768,768]{1,0:T(8,128)(2,1)}, bf16[768,768]{1,0:T(8,128)(2,1)}, u32[]{:S(2)}, u32[]{:S(2)}) collective-permute-start(bf16[768,768]{1,0:T(8,128)(2,1)} %get-tuple-element.134), channel_id=1, source_target_pairs={{0,1},{1,0},{2,3},{3,2},{4,5},{5,4},{6,7},{7,6},{8,9},{9,8},{10,11... | collective-permute-start | bytes 3538952 | tf_op jit(solution)/shard_map/ppermute | solution.py:241
  287.9 201.5 %all-gather.14.cloned.1.call-start = ((), (), s32[]{:S(2)}) async-start(), calls=%async_computation.4 | async-start | bytes 7077888 | tf_op jit(solution)/shard_map/all_gather | solution.py:263
  360.2 192.4 %all-gather.20.cloned.1.call-start = ((), (), s32[]{:S(2)}) async-start(), calls=%async_computation.9 | async-start | bytes 3538944 | tf_op jit(solution)/shard_map/all_gather | solution.py:263
  420.5 51.5 %collective-permute-start.14 = (bf16[512,1536]{1,0:T(8,128)(2,1)S(1)}, bf16[512,1536]{1,0:T(8,128)(2,1)S(1)}, u32[]{:S(2)}, u32[]{:S(2)}) collective-permute-start(bf16[512,1536]{1,0:T(8,128)(2,1)S(1)} %maximum_select_fusion.22), channel_id=1, source_target_pairs={{0,2},{2,0},{1,3},{3,1},{4,6},{6,4},{5,7},{7,5},{8,10},{10,8},{9,1... | collective-permute-start | bytes 4718600 | tf_op jit(solution)/shard_map/ppermute | solution.py:245
  428.7 44.5 %collective-permute-start.15 = (bf16[768,768]{1,0:T(8,128)(2,1)}, bf16[768,768]{1,0:T(8,128)(2,1)}, u32[]{:S(2)}, u32[]{:S(2)}) collective-permute-start(bf16[768,768]{1,0:T(8,128)(2,1)} %get-tuple-element.132), channel_id=1, source_target_pairs={{0,1},{1,0},{2,3},{3,2},{4,5},{5,4},{6,7},{7,6},{8,9},{9,8},{10,11... | collective-permute-start | bytes 3538952 | tf_op jit(solution)/shard_map/ppermute | solution.py:241
  488.0 579.7 %reduce-scatter.3.cloned.1.call-start = ((), (), s32[]{:S(2)}) async-start(), calls=%async_computation.5 | async-start | bytes 3538944 | tf_op jit(solution)/shard_map/reduce_scatter | solution.py:821
  641.0 484.9 %reduce-scatter.5.cloned.1.call-start = ((), (), s32[]{:S(2)}) async-start(), calls=%async_computation.6 | async-start | bytes 15040512 | tf_op jit(solution)/shard_map/reduce_scatter | solution.py:823
  651.7 51.7 %collective-permute-start.53 = (bf16[768,768]{1,0:T(8,128)(2,1)}, bf16[768,768]{1,0:T(8,128)(2,1)}, u32[]{:S(2)}, u32[]{:S(2)}) collective-permute-start(bf16[768,768]{1,0:T(8,128)(2,1)} %get-tuple-element.126), channel_id=1, source_target_pairs={{0,1},{1,0},{2,3},{3,2},{4,5},{5,4},{6,7},{7,6},{8,9},{9,8},{10,11... | collective-permute-start | bytes 3538952 | tf_op jit(solution)/shard_map/ppermute | solution.py:241
  811.8 38.2 %collective-permute-start.28 = (bf16[512,1536]{1,0:T(8,128)(2,1)}, bf16[512,1536]{1,0:T(8,128)(2,1)}, u32[]{:S(2)}, u32[]{:S(2)}) collective-permute-start(bf16[512,1536]{1,0:T(8,128)(2,1)} %dynamic-slice_convert_fusion.3), channel_id=1, source_target_pairs={{0,1},{1,0},{2,3},{3,2},{4,5},{5,4},{6,7},{7,6},{8,9},{9,8},{10,11... | collective-permute-start | bytes 4718600 | tf_op jit(solution)/shard_map/ppermute | solution.py:241
  866.4 88.9 %collective-permute-start.40 = (bf16[2,2,192,2048]{3,2,1,0:T(8,128)(2,1)}, bf16[2,2,192,2048]{3,2,1,0:T(8,128)(2,1)}, u32[]{:S(2)}, u32[]{:S(2)}) collective-permute-start(bf16[2,2,192,2048]{3,2,1,0:T(8,128)(2,1)} %dynamic-slice_bitcast_fusion), channel_id=1, source_target_pairs={{0,4},{4,0},{8,12},{12,8},{16,20},{20,16},{24,28},{28,24},{1,5},{5... | collective-permute-start | bytes 9437192 | tf_op jit(solution)/shard_map/ppermute | solution.py:273
  987.3 71.3 %collective-permute-start.42 = (bf16[2,192,2048]{2,1,0:T(8,128)(2,1)}, bf16[2,192,2048]{2,1,0:T(8,128)(2,1)S(1)}, u32[]{:S(2)}, u32[]{:S(2)}) collective-permute-start(bf16[2,192,2048]{2,1,0:T(8,128)(2,1)} %dynamic-slice_bitcast_fusion.1), channel_id=1, source_target_pairs={{0,16},{4,20},{8,24},{12,28},{16,0},{20,4},{24,8},{28,12},{1,17},{... | collective-permute-start | bytes 4718600 | tf_op jit(solution)/shard_map/ppermute | solution.py:273
  1027.9 74.4 %collective-permute-start.46 = (bf16[768,1664]{1,0:T(8,128)(2,1)}, bf16[768,1664]{1,0:T(8,128)(2,1)}, u32[]{:S(2)}, u32[]{:S(2)}) collective-permute-start(bf16[768,1664]{1,0:T(8,128)(2,1)} %tie.76), channel_id=1, source_target_pairs={{0,2},{2,0},{1,3},{3,1},{4,6},{6,4},{5,7},{7,5},{8,10},{10,8},{9,1... | collective-permute-start | bytes 7667720 | tf_op jit(solution)/shard_map/ppermute | solution.py:245
  1067.8 110.0 %collective-permute-start.52 = (bf16[128,1536]{1,0:T(8,128)(2,1)}, bf16[128,1536]{1,0:T(8,128)(2,1)S(1)}, u32[]{:S(2)}, u32[]{:S(2)}) collective-permute-start(bf16[128,1536]{1,0:T(8,128)(2,1)} %reduce-scatter.3.cloned.1.call-done.refs_4_), channel_id=1, source_target_pairs={{0,2},{2,0},{1,3},{3,1},{4,6},{6,4},{5,7},{7,5},{8,10},{10,8},{9,1... | collective-permute-start | bytes 1179656 | tf_op jit(solution)/shard_map/ppermute | solution.py:245
  1120.1 80.0 %collective-permute-start.39 = (bf16[256,1536]{1,0:T(8,128)(2,1)}, bf16[256,1536]{1,0:T(8,128)(2,1)}, u32[]{:S(2)}, u32[]{:S(2)}) collective-permute-start(bf16[256,1536]{1,0:T(8,128)(2,1)} %fusion.35), channel_id=1, source_target_pairs={{0,2},{2,0},{1,3},{3,1},{4,6},{6,4},{5,7},{7,5},{8,10},{10,8},{9,1... | collective-permute-start | bytes 2359304 | tf_op jit(solution)/shard_map/ppermute | solution.py:245
  1125.9 50.6 %collective-permute-start.54 = (bf16[192,4352]{1,0:T(8,128)(2,1)}, bf16[192,4352]{1,0:T(8,128)(2,1)S(1)}, u32[]{:S(2)}, u32[]{:S(2)}) collective-permute-start(bf16[192,4352]{1,0:T(8,128)(2,1)} %reduce-scatter.5.cloned.1.call-done.refs_0_), channel_id=1, source_target_pairs={{0,2},{2,0},{1,3},{3,1},{4,6},{6,4},{5,7},{7,5},{8,10},{10,8},{9,1... | collective-permute-start | bytes 5013512 | tf_op jit(solution)/shard_map/ppermute | solution.py:245
  1129.8 63.7 %collective-permute-start.51 = (bf16[192,2048]{1,0:T(8,128)(2,1)}, bf16[192,2048]{1,0:T(8,128)(2,1)}, u32[]{:S(2)}, u32[]{:S(2)}) collective-permute-start(bf16[192,2048]{1,0:T(8,128)(2,1)} %bitcast_add_fusion.6.refs_0_), channel_id=1, source_target_pairs={{0,2},{2,0},{1,3},{3,1},{4,6},{6,4},{5,7},{7,5},{8,10},{10,8},{9,1... | collective-permute-start | bytes 2359304 | tf_op jit(solution)/shard_map/ppermute | solution.py:245
  1144.5 55.6 %collective-permute-start.60 = (bf16[2,96,1664]{2,1,0:T(8,128)(2,1)}, bf16[2,96,1664]{2,1,0:T(8,128)(2,1)S(1)}, u32[]{:S(2)}, u32[]{:S(2)}) collective-permute-start(bf16[2,96,1664]{2,1,0:T(8,128)(2,1)} %bitcast.281), channel_id=1, source_target_pairs={{0,16},{4,20},{8,24},{12,28},{16,0},{20,4},{24,8},{28,12},{1,17},{... | collective-permute-start | bytes 1916936 | tf_op jit(solution)/shard_map/ppermute | solution.py:273
  (189 other events, 2205.4 us)
Sparse Core Ops, SparseCore 0:
  20.7 70.3 all-gather.15
  93.8 63.5 all-gather.9
  159.6 97.5 all-gather.11
  288.1 61.2 all-gather.17
  360.3 97.8 all-gather.13
  488.1 58.7 all-gather.19
  641.2 72.5 reduce-scatter.2
  717.5 224.6 reduce-scatter.4
